TPU v7x, 32 devices: a whole 2x2x4 slice. The times are simulated.
32 devices in a mesh: cell: 8 (over z, x), spot: 4 (over y, core).
Axes of the slice: x: 2, y: 2, z: 4, core: 2. Of those that a mesh axis runs over, the one named last changes fastest.
Arguments:
- logits: float32 [32768, 2048], P('cell', 'spot'), may hold values from -8 to 8
- expression: bfloat16 [32768, 2048], P('cell'), may hold values from 0.099609375 to 10
- target: float32 [2048, 2048], P('cell', 'spot'), may hold values from 0.1 to 10
- keep_mask: int32 [32768], P('cell'), may hold values from 0 to 1, as said below
- slide_ids: int32 [2048], P('spot'), may hold values from 0 to 7, as said below
- slide_counts: int32 [8], replicated, may hold values from 64 to 768, as said below
Outputs:
- mapping_loss: float32 [], replicated
- predicted: float32 [2048, 2048], P('cell', 'spot')
- grad_logits: float32 [32768, 2048], P('cell', 'spot')
- grad_expression: float32 [32768, 2048], P('cell', 'spot')
Inputs may be any that keep to these rules, and one draw needn't show every extreme that they name: `keep_mask`: the first cell of every aligned block of 4096 cells is kept. `slide_ids`: every slide has at least 64 spots and at most 768. slide_counts[k] is the number of spots whose slide id is k.
All inputs are finite; a program needn't handle non-finite values.
Results may differ from a plain program's by a relative error of at most 0.0043.
Values may be sent and summed in bfloat16 or wider, within the bound.
No kernel may reach another device: no remote copies, remote signals or barrier semaphores. Data moves between devices by JAX's collectives and lax.ppermute only.
A program may use at most 192 MiB of HBM per device.

v0:
```python
import jax
import jax.numpy as jnp
from jax import lax
from jax.sharding import PartitionSpec as P

density_weight = 32.0
expression_scale = 64.0
norm_eps = 1e-06


def per_device(logits, expression, target, keep_mask, slide_ids, slide_counts):
    highest = lax.Precision.HIGHEST
    slide_total = slide_counts.shape[0]
    keep_flag = keep_mask > 0
    keep_weight = keep_flag.astype(jnp.float32)
    masked = jnp.where(keep_flag[:, None], logits, -1e30)
    local_top = jnp.max(masked, axis=0)
    row_top = lax.pmax(local_top, "cell")
    exponent = jnp.where(keep_flag[:, None], jnp.exp(masked - row_top[None, :]), 0.0)
    row_total, kept_total = lax.psum((jnp.sum(exponent, axis=0), jnp.sum(keep_weight)), "cell")
    mapping = exponent / row_total[None, :]
    mapping_low = mapping.astype(jnp.bfloat16)
    predicted = lax.psum_scatter(
        lax.dot_general(
            expression, mapping_low, (((0,), (0,)), ((), ())), preferred_element_type=jnp.float32
        ),
        "cell",
        scatter_dimension=0,
        tiled=True,
    )
    onehot = (slide_ids[:, None] == jnp.arange(slide_total, dtype=jnp.int32)[None, :]).astype(
        jnp.float32
    )
    counts = slide_counts.astype(jnp.float32)
    inner_part = jnp.dot(predicted * target, onehot, precision=highest)
    predict_part = jnp.dot(predicted * predicted, onehot, precision=highest)
    target_part = jnp.dot(target * target, onehot, precision=highest)
    density_part = jnp.dot(mapping, onehot, precision=highest)
    inner_prod, predict_sq, target_sq, density_sum = lax.psum(
        (inner_part, predict_part, target_part, density_part), "spot"
    )
    inv_predict = lax.rsqrt(predict_sq + norm_eps)
    inv_target = lax.rsqrt(target_sq + norm_eps)
    cosine = inner_prod * inv_predict * inv_target
    density = density_sum / counts[None, :]
    safe_density = jnp.where(keep_flag[:, None], density, 1.0)
    diverge_part = (
        jnp.sum(keep_weight[:, None] * (-jnp.log(kept_total) - jnp.log(safe_density)), axis=0)
        / kept_total
    )
    cosine_total, diverge = lax.psum((jnp.sum(cosine), diverge_part), "cell")
    mapping_loss = (-cosine_total + density_weight * jnp.sum(diverge)) / (
        slide_total * expression.shape[1]
    )
    pair_coef = jnp.dot(inv_predict * inv_target, onehot.T, precision=highest)
    curve_coef = jnp.dot(cosine * inv_predict * inv_predict, onehot.T, precision=highest)
    pred_grad = (predicted * curve_coef - target * pair_coef).astype(jnp.bfloat16)
    whole_grad = lax.all_gather(pred_grad, "cell", axis=0, tiled=True)
    density_grad = -density_weight * keep_weight[:, None] / (kept_total * safe_density)
    mapping_grad = jnp.dot(expression, whole_grad, preferred_element_type=jnp.float32)
    mapping_grad = mapping_grad + jnp.dot(
        density_grad / counts[None, :], onehot.T, precision=highest
    )
    spot_sum = lax.psum(jnp.sum(mapping * mapping_grad, axis=0), "cell")
    grad_logits = kept_total * mapping * (mapping_grad - spot_sum[None, :])
    regrouped = lax.all_to_all(whole_grad, "spot", split_axis=0, concat_axis=1, tiled=True)
    expr_sum = lax.dot_general(
        lax.all_gather(mapping_low, "spot", axis=1, tiled=True),
        regrouped,
        (((1,), (1,)), ((), ())),
        preferred_element_type=jnp.float32,
    )
    grad_expression = expression_scale * kept_total * expr_sum
    return (mapping_loss, predicted, grad_logits, grad_expression)


def solution(mesh):
    in_specs = (P("cell", "spot"), P("cell", None), P("cell", "spot"), P("cell"), P("spot"), P())
    out_specs = (P(), P("cell", "spot"), P("cell", "spot"), P("cell", "spot"))
    return jax.shard_map(
        per_device, mesh=mesh, in_specs=in_specs, out_specs=out_specs, check_vma=False
    )
```

profile of v0, /device:TPU:0, one launch (start us, length us, event | category | flops | bytes accessed | tf_op | source)
XLA Modules:
  0.0 392.1 jit_solution(7509671063362095456)
XLA Ops:
  8.1 8.9 %copy.18 = f32[4096,512]{0,1:T(8,128)} copy(f32[4096,512]{1,0:T(8,128)} %param.6) | data formatting | bytes 16777216 | tf_op args[0]
  17.0 0.6 convert_reduce_fusion
  17.6 4.2 %select_reduce_fusion = f32[512]{0:T(512)S(1)} fusion(f32[4096,512]{0,1:T(8,128)} %copy.18, pred[4096]{0:T(1024)(128)(4,1)S(1)} %get-tuple-element.21), kind=kLoop, calls=%fused_computation.4 | loop fusion | flops 4193792 | bytes 8394752 | tf_op jit(solution)/shard_map/reduce_max | solution.py:17
  21.8 23.1 %pmax.7 = f32[512]{0:T(512)S(1)} all-reduce(f32[512]{0:T(512)S(1)} %select_reduce_fusion), channel_id=1, replica_groups=mesh['cell'=8,'spot'=4] {'cell'}, use_global_device_ids=true, to_apply=%region_1.2 | all-reduce | flops 512 | bytes 4096 | tf_op jit(solution)/shard_map/pmax | solution.py:18
  44.9 4.6 %fusion.1 = f32[512]{0:T(512)S(1)} fusion(f32[4096,512]{0,1:T(8,128)} %copy.18, f32[512]{0:T(512)S(1)} %pmax.7, pred[4096]{0:T(1024)(128)(4,1)S(1)} %get-tuple-element.21), kind=kLoop, calls=%fused_computation.7 | loop fusion | flops 8388096 | bytes 8396800 | tf_op jit(solution)/shard_map/reduce_sum | solution.py:20
  49.4 17.8 %all-reduce.1 = (f32[512]{0:T(512)S(1)}, f32[]{:T(128)}) all-reduce(f32[512]{0:T(512)S(1)} %fusion.1, f32[]{:T(128)} %convert_reduce_fusion), channel_id=1, replica_groups=mesh['cell'=8,'spot'=4] {'cell'}, use_global_device_ids=true, to_apply=%region_3.4 | all-reduce | flops 513 | bytes 4104 | tf_op jit(solution)/shard_map/psum | solution.py:20
  67.2 8.0 %fusion.31 = (bf16[4096,512]{0,1:T(8,128)(2,1)}, f32[4096,512]{0,1:T(8,128)}) fusion(f32[512]{0:T(512)S(1)} %get-tuple-element.15, f32[512]{0:T(512)S(1)} %pmax.7, f32[4096,512]{0,1:T(8,128)} %copy.18, pred[4096]{0:T(1024)(128)(4,1)S(1)} %get-tuple-element.21), kind=kLoop, calls=%fused_computation.52 | loop fusion | flops 10485760 | bytes 20979712 | tf_op jit(solution)/shard_map/convert_element_type | solution.py:22
  75.2 14.9 %convolution_bitcast_fusion = f32[2048,512]{0,1:T(8,128)} fusion(bf16[4096,512]{0,1:T(8,128)(2,1)} %get-tuple-element.22, bf16[4096,2048]{1,0:T(8,128)(2,1)} %param.7), kind=kOutput, calls=%fused_computation.8 | convolution fusion | flops 8589934592 | bytes 25165824 | tf_op jit(solution)/shard_map/dot_general | solution.py:24
  90.2 6.9 %fusion.10 = f32[4096,8]{0,1:T(8,128)} fusion(f32[4096,512]{0,1:T(8,128)} %get-tuple-element.23, s32[512]{0:T(512)S(1)} %copy-done.3), kind=kOutput, calls=%fused_computation.21 | convolution fusion | flops 201330688 | bytes 8521728 | tf_op jit(solution)/shard_map/dot_general | solution.py:38
  97.1 0.4 fusion.4
  97.8 79.6 %reduce-scatter.2.cloned.1.call-done = f32[256,512]{0,1:T(8,128)} async-done(((f32[2048,512]{0,1:T(8,128)}), f32[256,512]{0,1:T(8,128)}) %reduce-scatter.2.cloned.1.call-update) | async-done | bytes 524304 | tf_op jit(solution)/shard_map/reduce_scatter | solution.py:23
  177.4 1.6 fusion.6
  179.0 1.5 fusion.8
  180.5 11.3 %all-reduce.2 = (f32[256,8]{0,1:T(8,128)S(1)}, f32[256,8]{0,1:T(8,128)S(1)}, f32[256,8]{0,1:T(8,128)S(1)}) all-reduce(f32[256,8]{0,1:T(8,128)S(1)} %fusion.4, f32[256,8]{0,1:T(8,128)S(1)} %fusion.8, f32[256,8]{0,1:T(8,128)S(1)} %fusion.6), channel_id=1, replica_groups=mesh['cell'=8,'spot'=4] {'spot'}, use_global_device_ids=true, to_apply=%region_7.8 | all-reduce | flops 6144 | bytes 49152 | tf_op jit(solution)/shard_map/psum | solution.py:39
  191.9 0.4 convolution_multiply_fusion.1
  192.3 2.2 fusion.3
  194.6 0.7 all-gather.5.cloned.1.call-update
  196.7 1.1 multiply_reduce_fusion.1
  197.8 0.7 broadcast_divide_fusion
  198.5 1.0 copy.25
  199.5 0.7 fusion.27
  200.1 44.6 %all-gather.3.cloned.1.call-done = bf16[2048,512]{0,1:T(8,128)(2,1)} async-done(((bf16[256,512]{0,1:T(8,128)(2,1)}), bf16[2048,512]{0,1:T(8,128)(2,1)}) %all-gather.3.cloned.1.call-update) | async-done | bytes 2097168 | tf_op jit(solution)/shard_map/all_gather | solution.py:58
  244.7 3.1 copy.32
  247.8 3.7 all-to-all-start
  251.5 14.8 %fusion.33 = f32[512,4096]{1,0:T(8,128)S(1)} fusion(bf16[2048,512]{0,1:T(8,128)(2,1)} %all-gather.3.cloned.1.call-done, bf16[4096,2048]{1,0:T(8,128)(2,1)} %param.7), kind=kOutput, calls=%fused_computation.53 | convolution fusion | flops 8589934592 | bytes 27262976 | tf_op jit(solution)/shard_map/dot_general | solution.py:60
  266.3 9.6 %multiply_reduce_fusion = (f32[512]{0:T(512)S(1)}, f32[4096,512]{0,1:T(8,128)}) fusion(f32[4096,512]{0,1:T(8,128)} %get-tuple-element.23, s32[512]{0:T(512)S(1)} %copy-done.3, f32[]{:T(128)} %get-tuple-element.16, f32[4096]{0:T(1024)S(1)} %get-tuple-element.20, f32[8]{0:T(128)S(1)} %convert_element_type.15, f32[4096,8]{0,1:T(8,128)S(1)} %copy-done.2, ...), kind=kOutput, calls=%fused_computation.2 | convolution fusion | flops 207785472 | bytes 25321508 | tf_op jit(solution)/shard_map/dot_general | solution.py:61
  275.9 19.3 %all-reduce = (f32[]{:T(128)}, f32[8]{0:T(128)S(1)}, f32[512]{0:T(512)S(1)}) all-reduce(f32[]{:T(128)} %fusion.27, f32[8]{0:T(128)S(1)} %broadcast_divide_fusion, f32[512]{0:T(512)S(1)} %get-tuple-element.24), channel_id=1, replica_groups=mesh['cell'=8,'spot'=4] {'cell'}, use_global_device_ids=true, to_apply=%region_9.10 | all-reduce | flops 521 | bytes 4168 | tf_op jit(solution)/shard_map/psum | solution.py:51
  295.9 12.7 %subtract_multiply_fusion = f32[4096,512]{0,1:T(8,128)} fusion(f32[4096,512]{0,1:T(8,128)} %get-tuple-element.25, f32[4096,512]{0,1:T(8,128)} %get-tuple-element.23, f32[512]{0:T(512)S(1)} %get-tuple-element.14, f32[]{:T(128)} %get-tuple-element.16), kind=kLoop, calls=%fused_computation.1 | loop fusion | flops 6291456 | bytes 25167876 | tf_op jit(solution)/shard_map/mul | solution.py:65
  308.6 9.0 %copy.26 = f32[4096,512]{1,0:T(8,128)} copy(f32[4096,512]{0,1:T(8,128)} %subtract_multiply_fusion) | data formatting | bytes 16777216
  317.5 0.6 reduce_sum.58
  318.8 50.4 %all-gather.5.cloned.1.call-done = bf16[4096,2048]{0,1:T(8,128)(2,1)} async-done(((bf16[4096,512]{0,1:T(8,128)(2,1)}), bf16[4096,2048]{0,1:T(8,128)(2,1)}) %all-gather.5.cloned.1.call-update) | async-done | bytes 16777232 | tf_op jit(solution)/shard_map/all_gather | solution.py:68
  369.2 14.6 %convolution_multiply_fusion = f32[4096,512]{1,0:T(8,128)} fusion(bf16[4096,2048]{0,1:T(8,128)(2,1)} %all-gather.5.cloned.1.call-done, bf16[512,2048]{0,1:T(8,128)(2,1)S(1)} %bitcast.18, f32[]{:T(128)S(6)} %mul_shard_map.7), kind=kOutput, calls=%fused_computation.5 | convolution fusion | flops 8592031744 | bytes 27262980 | tf_op jit(solution)/shard_map/dot_general | solution.py:67
  (25 shorter events, 0.5 us)
Async XLA Ops:
  8.0 9.0 %copy-start.4 = (s32[4096]{0:T(1024)S(1)}, s32[4096]{0:T(1024)}, u32[]{:S(2)}) copy-start(s32[4096]{0:T(1024)} %param.9) | copy-start | bytes 49156
  8.0 169.4 %reduce-scatter.2.cloned.1.call-start = ((), (), s32[]{:S(2)}) async-start(), calls=%async_computation.2 | async-start | bytes 4718592 | tf_op jit(solution)/shard_map/reduce_scatter | solution.py:23
  75.2 15.0 %copy-start.3 = (s32[512]{0:T(512)S(1)}, s32[512]{0:T(512)}, u32[]{:S(2)}) copy-start(s32[512]{0:T(512)} %param.10) | copy-start | bytes 6148
  90.1 7.1 %copy-start.1 = (f32[256,512]{1,0:T(8,128)S(1)}, f32[256,512]{1,0:T(8,128)}, u32[]{:S(2)}) copy-start(f32[256,512]{1,0:T(8,128)} %param.8) | copy-start | bytes 1572868
  90.1 106.6 %all-reduce.5.cloned.1.call-start = ((), (), s32[]{:S(2)}) async-start(), calls=%async_computation.3 | async-start | bytes 262144 | tf_op jit(solution)/shard_map/psum | solution.py:39
  90.1 105.8 %copy-start.5 = (s32[8]{0:T(128)S(1)}, s32[8]{0:T(128)}, u32[]{:S(2)}) copy-start(s32[8]{0:T(128)} %param.11) | copy-start | bytes 100
  97.1 147.6 %all-gather.3.cloned.1.call-start = ((), (), s32[]{:S(2)}) async-start(), calls=%async_computation.4 | async-start | bytes 2359296 | tf_op jit(solution)/shard_map/all_gather | solution.py:58
  177.4 21.0 %copy-start = (f32[256,512]{0,1:T(8,128)S(1)}, f32[256,512]{0,1:T(8,128)}, u32[]{:S(2)}) copy-start(f32[256,512]{0,1:T(8,128)} %reduce-scatter.2.cloned.1.call-done) | copy-start | bytes 1572868
  194.5 174.7 %all-gather.5.cloned.1.call-start = ((), (), s32[]{:S(2)}) async-start(), calls=%async_computation.5 | async-start | bytes 20971520 | tf_op jit(solution)/shard_map/all_gather | solution.py:68
  247.8 71.0 %all-to-all-start = ((bf16[4,512,512]{1,2,0:T(8,128)(2,1)}), bf16[4,512,512]{1,2,0:T(8,128)(2,1)S(1)}, u32[]{:S(2)}, u32[]{:S(2)}) async-start(bf16[4,512,512]{1,2,0:T(8,128)(2,1)} %bitcast.17), calls=%async_computation.1 | async-start | bytes 4194304 | tf_op jit(solution)/shard_map/all_to_all | solution.py:66
  251.5 14.8 %copy-start.2 = (f32[4096,8]{0,1:T(8,128)S(1)}, f32[4096,8]{0,1:T(8,128)}, u32[]{:S(2)}) copy-start(f32[4096,8]{0,1:T(8,128)} %all-reduce.5.cloned.1.call-done) | copy-start | bytes 393220
Sparse Core Ops, SparseCore 0:
  90.2 87.1 reduce-scatter.1
  194.6 49.9 all-gather.2
  246.2 122.9 all-gather.4
Sparse Core Ops, SparseCore 1:
  97.2 30.1 all-reduce.4
where the time goes:
time: 393 us; the launch traced here: 392 us
  waiting for transfers between devices  175 us (45%)
  blocking collectives  71.5 us (18%)
  matrix products  67 us (17%)
  other arithmetic  33.1 us (8%)
  local copies, waits for them, and re-layouts  22.2 us (6%)
  between operations  19.1 us (5%)
    reduce_scatter x1, waiting for transfers between devices, per_device(): lax.psum_scatter(lax.dot_general(expression, mapping_low, (((0,), (0,)),...  79.6 us
    all_gather x1, waiting for transfers between devices, per_device(): lax.all_gather(mapping_low, 'spot', axis=1, tiled=True)  50.4 us
    all_gather x1, waiting for transfers between devices, per_device(): whole_grad = lax.all_gather(pred_grad, 'cell', axis=0, tiled=True)  44.6 us
    pmax x1, blocking collectives, per_device(): row_top = lax.pmax(local_top, 'cell')  23.1 us
    psum x1, blocking collectives, per_device(): cosine_total, diverge = lax.psum((jnp.sum(cosine), diverge_part), 'cell')  19.3 us
    unnamed x16, local copies, waits for them, and re-layouts  19.1 us
    psum x1, blocking collectives, per_device(): lax.psum((jnp.sum(exponent, axis=0), jnp.sum(keep_weight)), 'cell')  17.8 us
    dot_general x1, matrix products, per_device(): lax.dot_general(expression, mapping_low, (((0,), (0,)), ((), ())), prefer...  14.9 us
  transfers between devices with their start and end apart: 5, of which 3 were waited for; matrix products, arithmetic and copies ran while one was open for 17% of the time, Pallas kernels for 0%

commit v1 on v0

v1 whole, which is shorter than its diff:
```python
import functools

import jax
import jax.numpy as jnp
from jax import lax
from jax.experimental import pallas as pl
from jax.experimental.pallas import tpu as pltpu
from jax.sharding import PartitionSpec as P

density_weight = 32.0
expression_scale = 64.0
norm_eps = 1e-06
f32 = jnp.float32
bf16 = jnp.bfloat16
VMEM_LIMIT = 56 << 20
COST_SHARE = 0.2
NT = (((1,), (1,)), ((), ()))
TN = (((0,), (0,)), ((), ()))


def cost(flops, bytes_accessed):
    return pl.CostEstimate(
        flops=int(flops * COST_SHARE),
        bytes_accessed=int(bytes_accessed * COST_SHARE),
        transcendentals=0,
    )


def params():
    return pltpu.CompilerParams(vmem_limit_bytes=VMEM_LIMIT)


def shape(dims, dtype):
    return jax.ShapeDtypeStruct(dims, dtype)


def dot(a, b, dims=(((1,), (0,)), ((), ()))):
    return lax.dot_general(a, b, dims, preferred_element_type=f32)


def halves(value):
    high = value.astype(bf16)
    return high, (value - high.astype(f32)).astype(bf16)


def thirds(value):
    high = value.astype(bf16)
    rest = value - high.astype(f32)
    middle = rest.astype(bf16)
    return high, middle, (rest - middle.astype(f32)).astype(bf16)


def split_rows(cells):
    unit = cells // 8
    return [unit, 2 * unit, 2 * unit, 2 * unit, unit]


def exp_call(logits, keep_rows, sums, whole, start, pieces_rows, final):
    cells, spots = logits.shape
    tile = 512
    first = start // tile
    counts = [size // tile for size in pieces_rows]
    begins = [sum(counts[:c]) for c in range(len(counts))]

    def body(x_ref, k_ref, *refs):
        if start:
            before_ref, refs = refs[0], refs[2:]
        piece_refs, (whole_ref, sum_ref) = refs[:-2], refs[-2:]
        step = pl.program_id(0)

        @pl.when(step == 0)
        def _():
            if start:
                sum_ref[...] = before_ref[...]
            else:
                sum_ref[...] = jnp.zeros_like(sum_ref)
            if final:
                kept = jnp.sum(k_ref[...].astype(f32)) * 0.125
                sum_ref[8:16, :] = jnp.full((8, spots), kept, f32)

        total = sum_ref[0:8, :]
        for g in range(tile // 128):
            row = (step + first) * (tile // 128) + g
            mask = jnp.broadcast_to(k_ref[pl.ds(row, 1), :].astype(f32), (128, 128)).T
            mask = jnp.concatenate([mask] * (spots // 128), axis=1)
            rise = jnp.exp(x_ref[g * 128 : (g + 1) * 128, :]) * mask
            whole_ref[g * 128 : (g + 1) * 128, :] = rise.astype(bf16)
            total = total + jnp.sum(rise.reshape(16, 8, spots), axis=0)
        sum_ref[0:8, :] = total
        for ref, begin, count in zip(piece_refs, begins, counts):

            @pl.when((step >= begin) & (step < begin + count))
            def _():
                ref[...] = whole_ref[...]

    def rows(c):
        return lambda i: (jnp.clip(i - begins[c], 0, counts[c] - 1), 0)

    in_specs = [
        pl.BlockSpec((tile, spots), lambda i: (i + first, 0)),
        pl.BlockSpec(keep_rows.shape, lambda i: (0, 0)),
    ]
    operands = [logits, keep_rows]
    aliases = {}
    if start:
        in_specs += [
            pl.BlockSpec((16, spots), lambda i: (0, 0)),
            pl.BlockSpec(memory_space=pl.ANY),
        ]
        operands += [sums, whole]
        aliases = {3: len(counts)}
    return pl.pallas_call(
        body,
        grid=(sum(counts),),
        in_specs=in_specs,
        out_specs=[pl.BlockSpec((tile, spots), rows(c)) for c in range(len(counts))]
        + [
            pl.BlockSpec((tile, spots), lambda i: (i + first, 0)),
            pl.BlockSpec((16, spots), lambda i: (0, 0)),
        ],
        out_shape=[shape((size, spots), bf16) for size in pieces_rows]
        + [shape((cells, spots), bf16), shape((16, spots), f32)],
        input_output_aliases=aliases,
        compiler_params=params(),
        cost_estimate=cost(0, 8 * sum(pieces_rows) * spots),
        name="exp_rows",
    )(*operands)


def part_call(expression, mapping, ids, picks, adds, dtypes):
    cells, spots = mapping.shape
    count = len(picks)
    block = expression.shape[1] // ids.shape[0]

    def body(ids_ref, *refs):
        e_refs, u_ref = refs[:count], refs[count]
        a_refs = refs[count + 1 : count + 1 + len(adds)]
        o_refs = refs[count + 1 + len(adds) :]
        both = jnp.concatenate([ref[...] for ref in e_refs], axis=1)
        terms = dot(both, u_ref[...], TN)
        for q in range(count):
            total = terms[q * block : (q + 1) * block, :]
            if q < len(adds):
                total = total + a_refs[q][...].astype(f32)
            o_refs[q][...] = total.astype(dtypes[q])

    def column(q):
        return lambda k, ids_ref: (0, ids_ref[q])

    flat = pl.BlockSpec((block, spots), lambda k, ids_ref: (0, 0))
    return pl.pallas_call(
        body,
        grid_spec=pltpu.PrefetchScalarGridSpec(
            num_scalar_prefetch=1,
            grid=(1,),
            in_specs=[pl.BlockSpec((cells, block), column(q)) for q in picks]
            + [pl.BlockSpec((cells, spots), lambda k, ids_ref: (0, 0))]
            + [flat] * len(adds),
            out_specs=[flat] * count,
        ),
        out_shape=[shape((block, spots), dtype) for dtype in dtypes],
        compiler_params=params(),
        cost_estimate=cost(
            2 * count * block * cells * spots, 2 * cells * (count * block + spots)
        ),
        name="part",
    )(ids, *[expression] * count, mapping, *adds)


def add_call(values):
    def body(*refs):
        total = refs[0][...].astype(f32)
        for ref in refs[1:-1]:
            total = total + ref[...].astype(f32)
        refs[-1][...] = total.astype(bf16)

    return pl.pallas_call(
        body,
        out_shape=shape(values[0].shape, bf16),
        compiler_params=params(),
        cost_estimate=cost(0, 8 * values[0].size),
        name="add_blocks",
    )(*values)


def total_of(tops_ref):
    return jnp.sum(tops_ref[0:8, :], axis=0, keepdims=True)


def kept_of(tops_ref):
    return jnp.sum(tops_ref[8:16, 0:1], axis=0, keepdims=True)


def predicted_call(values, tops, target, member):
    block, spots = target.shape
    slides = member.shape[0]

    def body(*refs):
        v_refs, (tops_ref, t_ref, m_ref, p_ref, s_ref) = refs[:-5], refs[-5:]
        total = v_refs[0][...].astype(f32)
        for ref in v_refs[1:]:
            total = total + ref[...].astype(f32)
        pred = total / total_of(tops_ref)
        p_ref[...] = pred
        target_now = t_ref[...]
        member_low = m_ref[...].astype(bf16)
        for q, value in enumerate((pred * target_now, pred * pred, target_now * target_now)):
            high, low = halves(value)
            s_ref[q * slides : (q + 1) * slides, :] = dot(member_low, high, NT) + dot(
                member_low, low, NT
            )

    return pl.pallas_call(
        body,
        out_shape=[shape((block, spots), f32), shape((3 * slides, block), f32)],
        compiler_params=params(),
        cost_estimate=cost(0, 16 * block * spots),
        name="predicted",
    )(*values, tops, target, member)


def grad_call(sums, far, pred, target, tops, member):
    block, spots = target.shape
    slides = member.shape[0]

    def body(s_ref, f_ref, p_ref, t_ref, tops_ref, m_ref, g_ref, e_ref):
        total = s_ref[...] + f_ref[...]
        inner = total[0:slides, :]
        inv_predict = lax.rsqrt(total[slides : 2 * slides, :] + norm_eps)
        inv_target = lax.rsqrt(total[2 * slides : 3 * slides, :] + norm_eps)
        pair = inv_predict * inv_target
        cosine = inner * pair
        member_low = m_ref[...].astype(bf16)
        pair_at = sum(dot(v, member_low, TN) for v in thirds(pair))
        curve_at = sum(dot(v, member_low, TN) for v in thirds(cosine * inv_predict * inv_predict))
        pred = p_ref[...]
        grad = (pred * curve_at - t_ref[...] * pair_at) / total_of(tops_ref)
        grad = grad.astype(bf16)
        g_ref[...] = grad
        column = jnp.sum(pred * grad.astype(f32), axis=0, keepdims=True)
        total = jnp.sum(jnp.sum(cosine, axis=1, keepdims=True), axis=0, keepdims=True)
        e_ref[...] = jnp.concatenate(
            [column, jnp.broadcast_to(total, (1, spots)), jnp.zeros((6, spots), f32)], axis=0
        )

    return pl.pallas_call(
        body,
        out_shape=[shape((block, spots), bf16), shape((8, spots), f32)],
        compiler_params=params(),
        cost_estimate=cost(0, 12 * block * spots),
        name="grad",
    )(sums, far, pred, target, tops, member)


def density_call(mapping, tops, member):
    cells, spots = mapping.shape
    slides = member.shape[0]
    tile = min(cells, 2048)

    def body(u_ref, tops_ref, m_ref, o_ref):
        high, low = halves(m_ref[...] / total_of(tops_ref))
        both = jnp.concatenate([high, low], axis=0)
        pad = jnp.zeros((128 - 2 * slides, spots), bf16)
        got = dot(u_ref[...], jnp.concatenate([both, pad], axis=0), NT).T
        o_ref[...] = got[0:slides, :] + got[slides : 2 * slides, :]

    return pl.pallas_call(
        body,
        grid=(cells // tile,),
        in_specs=[
            pl.BlockSpec((tile, spots), lambda i: (i, 0)),
            pl.BlockSpec((16, spots), lambda i: (0, 0)),
            pl.BlockSpec((slides, spots), lambda i: (0, 0)),
        ],
        out_specs=pl.BlockSpec((slides, tile), lambda i: (0, i)),
        out_shape=shape((slides, cells), f32),
        compiler_params=params(),
        cost_estimate=cost(0, 2 * cells * spots),
        name="density",
    )(mapping, tops, member)


def diverge_call(density, far, keep_line, counts, mapping, tops, member, ends):
    cells, spots = mapping.shape
    slides = member.shape[0]
    tile = min(cells, 2048)
    steps = cells // tile

    def body(d_ref, f_ref, k_ref, c_ref, u_ref, tops_ref, m_ref, ends_ref, o_ref, w_ref, e_ref, acc):
        step = pl.program_id(0)
        keep = k_ref[...].astype(f32)
        kept = kept_of(tops_ref)
        total = total_of(tops_ref)
        weight = m_ref[...] / total
        safe = jnp.where(keep > 0, d_ref[...] + f_ref[...], 1.0)
        slope = -density_weight * keep / (kept * safe)
        high, low = halves(slope)
        parts = jnp.concatenate([high, high, low, jnp.zeros_like(low)], axis=0)
        o_ref[...] = parts
        w_high, w_low = halves(weight)
        weights = jnp.concatenate([w_high, w_low, w_high, jnp.zeros_like(w_low)], axis=0)
        w_ref[...] = weights
        column = jnp.zeros((8, spots), f32)
        chunk = 256
        for r in range(tile // chunk):
            at = slice(r * chunk, (r + 1) * chunk)
            pulled = dot(parts[:, at], weights, TN) * u_ref[at, :].astype(f32)
            column += jnp.sum(pulled.reshape(chunk // 8, 8, spots), axis=0)
        logs = jnp.log(c_ref[...].astype(f32)) - jnp.log(kept) - jnp.log(safe)
        logs = jnp.sum(jnp.where(keep > 0, logs, 0.0), axis=1, keepdims=True)
        logs = jnp.sum(logs, axis=0, keepdims=True) / kept
        column = jnp.sum(column, axis=0, keepdims=True) / total

        @pl.when(step == 0)
        def _():
            acc[...] = ends_ref[...]

        acc[...] += jnp.concatenate(
            [
                column,
                jnp.zeros_like(column),
                jnp.broadcast_to(logs, (1, spots)),
                jnp.zeros((5, spots), f32),
            ],
            axis=0,
        )
        e_ref[...] = acc[...]

    return pl.pallas_call(
        body,
        grid=(steps,),
        in_specs=[
            pl.BlockSpec((slides, tile), lambda i: (0, i)),
            pl.BlockSpec((slides, tile), lambda i: (0, i)),
            pl.BlockSpec((1, tile), lambda i: (0, i)),
            pl.BlockSpec((slides, 1), lambda i: (0, 0)),
            pl.BlockSpec((tile, spots), lambda i: (i, 0)),
            pl.BlockSpec((16, spots), lambda i: (0, 0)),
            pl.BlockSpec((slides, spots), lambda i: (0, 0)),
            pl.BlockSpec((8, spots), lambda i: (0, 0)),
        ],
        out_specs=[
            pl.BlockSpec((4 * slides, tile), lambda i: (0, i)),
            pl.BlockSpec((4 * slides, spots), lambda i: (0, 0)),
            pl.BlockSpec((8, spots), lambda i: (0, 0)),
        ],
        out_shape=[
            shape((4 * slides, cells), bf16),
            shape((4 * slides, spots), bf16),
            shape((8, spots), f32),
        ],
        scratch_shapes=[pltpu.VMEM((8, spots), f32)],
        compiler_params=params(),
        cost_estimate=cost(0, 2 * cells * spots),
        name="diverge",
    )(density, far, keep_line, counts, mapping, tops, member, ends)


def regroup_call(blocks, ids, place, spread):
    count = len(blocks)
    block, spots = blocks[0].shape
    share = count * block // spread
    fars = spread // 2 - 1

    def body(ids_ref, place_ref, *refs):
        b_refs, o_refs = refs[:count], refs[count : count + 2 + fars]
        held, in_sem, out_sem = refs[count + 2 + fars :]
        here = place_ref[0]

        def rows(start, size):
            return held.at[pl.ds(pl.multiple_of(start, size), size)]

        copies = [
            pltpu.make_async_copy(b_refs[q], rows(ids_ref[q] * block, block), in_sem.at[q])
            for q in range(count)
        ]
        for copy in copies:
            copy.start()
        for copy in copies:
            copy.wait()
        copies = [
            pltpu.make_async_copy(
                rows(((here >> 1) ^ (w + 1)) * (2 * share), 2 * share),
                o_refs[2 + w],
                out_sem.at[2 + w],
            )
            for w in range(fars)
        ]
        copies += [
            pltpu.make_async_copy(rows((here ^ w) * share, share), o_refs[w], out_sem.at[w])
            for w in range(2)
        ]
        for copy in copies:
            copy.start()
        for copy in copies:
            copy.wait()

    smem = pl.BlockSpec(memory_space=pltpu.SMEM)
    anywhere = pl.BlockSpec(memory_space=pl.ANY)
    return pl.pallas_call(
        body,
        in_specs=[smem, smem] + [anywhere] * count,
        out_specs=[anywhere] * (2 + fars),
        out_shape=[shape((share, spots), bf16)] * 2 + [shape((2 * share, spots), bf16)] * fars,
        scratch_shapes=[
            pltpu.VMEM((count * block, spots), bf16),
            pltpu.SemaphoreType.DMA((count,)),
            pltpu.SemaphoreType.DMA((2 + fars,)),
        ],
        compiler_params=params(),
        cost_estimate=cost(0, 4 * count * block * spots),
        name="regroup",
    )(ids, place, *blocks)


def logit_call(expression, blocks, ids, mapping, slope, weight, ends, tops):
    cells, genes = expression.shape
    block, spots = blocks[0].shape
    count = len(blocks)
    tile = min(cells, 1024)

    def body(ids_ref, e_ref, u_ref, d_ref, w_ref, ends_ref, tops_ref, *refs):
        b_refs, (o_ref, held, sem) = refs[:count], refs[count:]

        @pl.when(pl.program_id(0) == 0)
        def _():
            copies = []
            for q in range(count):
                at = pl.ds(pl.multiple_of(ids_ref[q] * block, block), block)
                copies.append(pltpu.make_async_copy(b_refs[q], held.at[at], sem.at[q]))
            for copy in copies:
                copy.start()
            for copy in copies:
                copy.wait()

        acc = dot(e_ref[...], held[...])
        acc += dot(d_ref[...], w_ref[...], TN) - ends_ref[0:1, :]
        o_ref[...] = u_ref[...].astype(f32) * (acc * kept_of(tops_ref))

    return pl.pallas_call(
        body,
        grid=(cells // tile,),
        in_specs=[
            pl.BlockSpec(memory_space=pltpu.SMEM),
            pl.BlockSpec((tile, genes), lambda i: (i, 0)),
            pl.BlockSpec((tile, spots), lambda i: (i, 0)),
            pl.BlockSpec((slope.shape[0], tile), lambda i: (0, i)),
            pl.BlockSpec(weight.shape, lambda i: (0, 0)),
            pl.BlockSpec((8, spots), lambda i: (0, 0)),
            pl.BlockSpec((16, spots), lambda i: (0, 0)),
        ]
        + [pl.BlockSpec(memory_space=pl.ANY)] * count,
        out_specs=pl.BlockSpec((tile, spots), lambda i: (i, 0)),
        out_shape=shape((cells, spots), f32),
        scratch_shapes=[pltpu.VMEM((genes, spots), bf16), pltpu.SemaphoreType.DMA((count,))],
        compiler_params=params(),
        cost_estimate=cost(2 * cells * genes * spots, 2 * cells * genes + 6 * cells * spots),
        name="grad_logits",
    )(ids, expression, mapping, slope, weight, ends, tops, *blocks)


def expr_call(base, chunks, grads, tops, cells, start):
    spots = chunks[0][0].shape[1]
    genes = grads[0].shape[0]
    count = len(grads)
    tile = 512
    steps = [c[0].shape[0] // tile for c in chunks]
    begins = [sum(steps[:c]) for c in range(len(chunks))]
    first = start // tile

    def body(*refs):
        o_ref = refs[-1]
        g_refs = refs[len(chunks) * count : len(chunks) * count + count]
        tops_ref = refs[len(chunks) * count + count]
        step = pl.program_id(0)
        for c in range(len(chunks)):

            @pl.when((step >= begins[c]) & (step < begins[c] + steps[c]))
            def _():
                total = None
                for q in range(count):
                    term = dot(refs[c * count + q][...], g_refs[q][...], NT)
                    total = term if total is None else total + term
                o_ref[...] = total * (expression_scale * kept_of(tops_ref))

    def rows(c):
        return lambda i: (jnp.clip(i - begins[c], 0, steps[c] - 1), 0)

    in_specs = [pl.BlockSpec((tile, spots), rows(c)) for c in range(len(chunks)) for _ in range(count)]
    in_specs += [pl.BlockSpec((genes, spots), lambda i: (0, 0))] * count
    in_specs += [pl.BlockSpec((16, spots), lambda i: (0, 0))]
    operands = [v for c in chunks for v in c] + [*grads, tops]
    aliases = {}
    if base is not None:
        in_specs.append(pl.BlockSpec(memory_space=pl.ANY))
        operands.append(base)
        aliases = {len(operands) - 1: 0}
    rows_all = sum(steps) * tile
    return pl.pallas_call(
        body,
        grid=(sum(steps),),
        in_specs=in_specs,
        out_specs=pl.BlockSpec((tile, genes), lambda i: (i + first, 0)),
        out_shape=shape((cells, genes), f32),
        input_output_aliases=aliases,
        compiler_params=params(),
        cost_estimate=cost(
            2 * rows_all * spots * count * genes, 2 * rows_all * spots * count + 4 * rows_all * genes
        ),
        name="grad_expression",
    )(*operands)


def per_device(n, m, logits, expression, target, keep_mask, slide_ids, slide_counts):
    cells, spots = logits.shape
    genes = expression.shape[1]
    block = genes // n
    slide_total = slide_counts.shape[0]
    levels = n.bit_length() - 1
    lead = levels - 3
    orders = [[1 << k for k in range(levels)] for _ in range(2)]
    orders[1][0], orders[1][1] = 2, 1
    me = lax.axis_index("cell")
    place = lax.axis_index("spot")
    core = place & 1

    def across(value, k):
        pairs = [
            (i * m + j, (i ^ orders[j & 1][k]) * m + j) for i in range(n) for j in range(m)
        ]
        return lax.ppermute(value, ("cell", "spot"), pairs)

    def over_spot(value, mask):
        return lax.ppermute(value, "spot", [(j, j ^ mask) for j in range(m)])

    def over_cell(value, cell_mask, spot_mask):
        pairs = [
            (i * m + j, (i ^ cell_mask) * m + (j ^ spot_mask)) for i in range(n) for j in range(m)
        ]
        return lax.ppermute(value, ("cell", "spot"), pairs)

    def sum_cell(value):
        for k in range(levels):
            value = value + across(value, k)
        return value

    def sum_spot(value, aside):
        other = over_spot(value, 1)
        mask = 2
        while mask < m:
            value = value + other
            if aside:
                other = over_cell(over_cell(value, 1, 0), 1, mask)
            else:
                other = over_spot(value, mask)
            mask *= 2
        return value, other

    def tie(value, others):
        return lax.optimization_barrier((value, *others))[0]

    keep_rows = keep_mask.reshape(cells // 128, 128)
    sizes = split_rows(cells)
    starts = [sum(sizes[:c]) for c in range(len(sizes))]
    first, mapping, sums = exp_call(logits, keep_rows, None, None, 0, sizes[:1], False)
    *rest, mapping, sums = exp_call(logits, keep_rows, sums, mapping, sizes[0], sizes[1:], True)
    pieces = [first, *rest]
    gathered = []
    for piece in pieces:
        quarters = [None] * m
        for mask in range(0, m, 2):
            quarters[mask] = over_spot(piece, mask) if mask else piece
            quarters[mask + 1] = over_spot(quarters[mask], 1)
        gathered.append(quarters)

    def arrived(c):
        return [gathered[c][mask] for mask in range(2, m, 2)]

    tops = sum_cell(sums)

    def place_of(code):
        value = me
        for k in range(levels):
            if code[k]:
                value = value ^ jnp.where(core == 1, orders[1][k], orders[0][k])
        return value

    def codes(prefix):
        out = [prefix]
        while len(out[0]) < levels:
            out = [c + (b,) for c in out for b in (1, 0)]
        return out

    ids = jnp.stack([place_of(c) for c in codes(())])
    order = {c[lead:]: q for q, c in enumerate(codes((0,) * lead))}

    def products(first, second, adds, dtypes):
        return part_call(expression, mapping, ids, [order[first], order[second]], adds, dtypes)

    part, got, step = {}, {}, {}
    if lead or block % 128:
        have = dot(expression, mapping, TN).reshape(n, block, spots)
        have = jnp.take(have, ids, axis=0)
        for k in range(lead):
            half = have.shape[0] // 2
            have = have[half:] + across(have[:half].astype(bf16), k).astype(f32)
        for code, q in order.items():
            part[code] = have[q]
        for a in (1, 0):
            for b in (1, 0):
                got[1, a, b] = across(part[1, a, b].astype(bf16), lead)
        for b in (1, 0):
            part[0, 1, b] = add_call([part[0, 1, b], got[1, 1, b]])
            step[0, 1, b] = across(part[0, 1, b], lead + 1)
        adds = [part[0, 0, 0], got[1, 0, 0]]
    else:
        part[1, 1, 1], part[1, 0, 1] = products((1, 1, 1), (1, 0, 1), [], [bf16] * 2)
        got[1, 1, 1], got[1, 0, 1] = across(part[1, 1, 1], 0), across(part[1, 0, 1], 0)
        got[1, 1, 1] = tie(got[1, 1, 1], arrived(0))
        part[0, 1, 1], part[0, 0, 1] = products(
            (0, 1, 1), (0, 0, 1), [got[1, 1, 1]], [bf16, f32]
        )
        step[0, 1, 1] = across(part[0, 1, 1], 1)
        part[1, 1, 0], part[1, 0, 0] = products((1, 1, 0), (1, 0, 0), [], [bf16] * 2)
        got[1, 1, 0], got[1, 0, 0] = across(part[1, 1, 0], 0), across(part[1, 0, 0], 0)
        part[0, 1, 0], part[0, 0, 0] = products(
            (0, 1, 0), (0, 0, 0), [got[1, 1, 0], got[1, 0, 0]], [bf16, f32]
        )
        step[0, 1, 0] = across(part[0, 1, 0], 1)
        adds = [part[0, 0, 0]]
    last = add_call([part[0, 0, 1], got[1, 0, 1], step[0, 1, 1]])
    last = across(last, lead + 2)

    slides = jnp.arange(slide_total, dtype=jnp.int32)
    member = (slide_ids[None, :] == slides[:, None]).astype(f32)
    last = tie(last, arrived(1))
    predicted, gene_sums = predicted_call(
        [*adds, step[0, 1, 0], last], tops, target, member
    )
    gene_sums, far_sums = sum_spot(gene_sums, True)
    far_sums = tie(far_sums, arrived(2))
    grad, ends = grad_call(gene_sums, far_sums, predicted, target, tops, member)

    have = {(0, 0, 0): grad}
    for k in (2, 1, 0):
        for code in list(have):
            other = tuple(1 if q == k else b for q, b in enumerate(code))
            have[other] = across(have[code], lead + k)
    tail = codes((0,) * lead)
    blocks = [have[c[lead:]] for c in tail]
    if lead:
        blocks = jnp.stack(blocks)
        for k in reversed(range(lead)):
            blocks = jnp.concatenate([across(blocks, k), blocks])
        blocks = [blocks[q] for q in range(n)]

    density, far_density = sum_spot(density_call(mapping, tops, member), False)
    slope, weight, ends = diverge_call(
        density,
        far_density,
        keep_mask[None, :],
        slide_counts[:, None],
        mapping,
        tops,
        member,
        ends,
    )
    ends = sum_cell(ends)
    mapping_loss = (-ends[1, 0] + density_weight * ends[2, 0]) / (slide_total * genes)

    mine, beside, *far = regroup_call(blocks, ids, place[None], m)
    grad_logits = logit_call(
        expression, blocks, ids, mapping, slope, weight, tie(ends, arrived(3)), tops
    )
    share = genes // m
    regrouped = [None] * m
    regrouped[0], regrouped[1] = mine, over_spot(beside, 1)
    for q, pair in enumerate(far):
        mask = 2 * (q + 1)
        pair = over_spot(pair, mask).reshape(2, share, spots)
        regrouped[mask] = lax.dynamic_index_in_dim(pair, core, 0, keepdims=False)
        regrouped[mask + 1] = over_spot(
            lax.dynamic_index_in_dim(pair, 1 - core, 0, keepdims=False), 1
        )
    grad_expression = expr_call(None, gathered[:-1], regrouped, tops, cells, 0)
    grad_expression = expr_call(
        grad_expression, gathered[-1:], regrouped, tops, cells, starts[-1]
    )
    return (mapping_loss, predicted, grad_logits, grad_expression)


def solution(mesh):
    in_specs = (P("cell", "spot"), P("cell", None), P("cell", "spot"), P("cell"), P("spot"), P())
    out_specs = (P(), P("cell", "spot"), P("cell", "spot"), P("cell", "spot"))
    body = functools.partial(per_device, mesh.shape["cell"], mesh.shape["spot"])
    return jax.shard_map(
        body, mesh=mesh, in_specs=in_specs, out_specs=out_specs, check_vma=False
    )
```

time: 393 us -> 218 us (0.55)
  waiting for transfers between devices: 175 us -> 70.9 us
  Pallas kernels: 0 us -> 97.7 us
  blocking collectives: 71.5 us -> 0 us
  matrix products: 67 us -> 0 us
  other arithmetic: 33.1 us -> 3.61 us
  starting transfers between devices: 3.85 us -> 31.7 us
  between operations: 19.1 us -> 3.42 us
  local copies, waits for them, and re-layouts: 22.2 us -> 10.1 us
    pallas_call x0 -> x15, Pallas kernels: none -> 97.7 us  [the longest x4 29.2 us: part_call(): pl.pallas_call(body, grid_spec=pltpu.PrefetchScalarGridSpec(num_scalar_pr...]
    all_gather x2 -> x0, waiting for transfers between devices: 95 us -> none  [the longest x1 50.4 us: per_device(): lax.all_gather(mapping_low, 'spot', axis=1, tiled=True)]
    reduce_scatter x1 -> x0, waiting for transfers between devices: 79.6 us -> none  [per_device(): lax.psum_scatter(lax.dot_general(expression, mapping_low, (((0,), (0,)),...]
    ppermute x0 -> x43, waiting for transfers between devices: none -> 70.9 us  [the longest x20 32.3 us: across(): return lax.ppermute(value, ('cell', 'spot'), pairs)]
    dot_general x10 -> x0, matrix products: 67 us -> none  [the longest x1 14.9 us: per_device(): lax.dot_general(expression, mapping_low, (((0,), (0,)), ((), ())), prefer...]
    psum x3 -> x0, blocking collectives: 48.4 us -> none  [the longest x1 19.3 us: per_device(): cosine_total, diverge = lax.psum((jnp.sum(cosine), diverge_part), 'cell')]
    ppermute x0 -> x43, starting transfers between devices: none -> 31.7 us  [the longest x20 20.6 us: across(): return lax.ppermute(value, ('cell', 'spot'), pairs)]
    pmax x1 -> x0, blocking collectives: 23.1 us -> none  [per_device(): row_top = lax.pmax(local_top, 'cell')]
  transfers between devices with their start and end apart: 5 -> 43, of which waited for: 3 -> 16; matrix products, arithmetic and copies ran while one was open for 17% -> 3% of each run, Pallas kernels for 0% -> 42%
where the time goes in v1:
time: 218 us; the launch traced here: 217 us
  Pallas kernels  97.7 us (45%)
  waiting for transfers between devices  70.9 us (33%)
  starting transfers between devices  31.7 us (15%)
  local copies, waits for them, and re-layouts  10.1 us (5%)
  other arithmetic  3.61 us (2%)
  between operations  3.42 us (2%)
    ppermute x20, waiting for transfers between devices, across(): return lax.ppermute(value, ('cell', 'spot'), pairs)  32.3 us
    ppermute x21, waiting for transfers between devices, over_spot(): return lax.ppermute(value, 'spot', [(j, j ^ mask) for j in range(m)])  31.2 us
    pallas_call x4, Pallas kernels, part_call(): pl.pallas_call(body, grid_spec=pltpu.PrefetchScalarGridSpec(num_scalar_pr...  29.2 us
    ppermute x20, starting transfers between devices, across(): return lax.ppermute(value, ('cell', 'spot'), pairs)  20.6 us
    pallas_call x2, Pallas kernels, expr_call(): pl.pallas_call(body, grid=(sum(steps),), in_specs=in_specs, out_specs=pl....  20.3 us
    pallas_call x1, Pallas kernels, logit_call(): pl.pallas_call(body, grid=(cells // tile,), in_specs=[pl.BlockSpec(memory...  17.9 us
    pallas_call x2, Pallas kernels, exp_call(): pl.pallas_call(body, grid=(sum(counts),), in_specs=in_specs, out_specs=[p...  11.7 us
    ppermute x21, starting transfers between devices, over_spot(): return lax.ppermute(value, 'spot', [(j, j ^ mask) for j in range(m)])  9.94 us
  transfers between devices with their start and end apart: 43, of which 16 were waited for; matrix products, arithmetic and copies ran while one was open for 3% of the time, Pallas kernels for 42%

profile of v1, /device:TPU:0, one launch (start us, length us, event | category | flops | bytes accessed | tf_op | source)
XLA Modules:
  0.0 217.4 jit_solution(14996561761160923551)
XLA Ops:
  0.6 2.4 %exp_rows.2 = (bf16[512,512]{1,0:T(8,128)(2,1)}, bf16[4096,512]{1,0:T(8,128)(2,1)}, f32[16,512]{1,0:T(8,128)}) custom-call(f32[4096,512]{1,0:T(8,128)} %x_ref.3, s32[32,128]{1,0:T(8,128)} %bitcast.18), custom_call_target="tpu_custom_call" | custom-call | bytes 419430 | tf_op jit(solution)/shard_map/exp_rows/pallas_call | solution.py:112
  3.0 3.0 %collective-permute-start.9 = (bf16[512,512]{1,0:T(8,128)(2,1)}, bf16[512,512]{1,0:T(8,128)(2,1)S(1)}, u32[]{:S(2)}, u32[]{:S(2)}) collective-permute-start(bf16[512,512]{1,0:T(8,128)(2,1)} %get-tuple-element.44.refs_0_), channel_id=1, source_target_pairs={{0,2},{1,3},{2,0},{3,1},{4,6},{5,7},{6,4},{7,5},{8,10},{9,11},{10,... | collective-permute-start | bytes 1572872 | tf_op jit(solution)/shard_map/ppermute | solution.py:534
  6.0 9.3 %exp_rows.3 = (bf16[1024,512]{1,0:T(8,128)(2,1)}, bf16[1024,512]{1,0:T(8,128)(2,1)}, bf16[1024,512]{1,0:T(8,128)(2,1)}, bf16[512,512]{1,0:T(8,128)(2,1)}, bf16[4096,512]{1,0:T(8,128)(2,1)}, /*index=5*/f32[16,512]{1,0:T(8,128)}) custom-call(f32[4096,512]{1,0:T(8,128)} %x_ref.3, s32[32,128]{1,0:T(8,128)} %bitcast.19, ...), custom_call_target="tpu_custom_call", output_to_operand_aliasing={{4}: (3, {})} | custom-call | bytes 2936012 | tf_op jit(solution)/shard_map/exp_rows/pallas_call | solution.py:112
  15.4 2.0 collective-permute-start.17
  18.0 7.2 %part.6 = (bf16[256,512]{1,0:T(8,128)(2,1)}, bf16[256,512]{1,0:T(8,128)(2,1)}) custom-call(s32[8]{0:T(128)} %stack.35.ids_ref, bf16[4096,2048]{1,0:T(8,128)(2,1)} %e_ref.1, bf16[4096,2048]{1,0:T(8,128)(2,1)} %e_ref.1, bf16[4096,512]{1,0:T(8,128)(2,1)} %get-tuple-element.37.u_ref.refs_2_), custom_call_target="tpu_custom_call" | custom-call | flops 429496736 | bytes 1677721 | tf_op jit(solution)/shard_map/part/pallas_call | solution.py:151
  27.3 7.2 %part.4 = (bf16[256,512]{1,0:T(8,128)(2,1)}, bf16[256,512]{1,0:T(8,128)(2,1)}) custom-call(s32[8]{0:T(128)} %stack.35.ids_ref, bf16[4096,2048]{1,0:T(8,128)(2,1)} %e_ref.1, bf16[4096,2048]{1,0:T(8,128)(2,1)} %e_ref.1, bf16[4096,512]{1,0:T(8,128)(2,1)} %get-tuple-element.37.u_ref.refs_2_), custom_call_target="tpu_custom_call" | custom-call | flops 429496736 | bytes 1677721 | tf_op jit(solution)/shard_map/part/pallas_call | solution.py:151
  36.1 7.3 %part.7 = (bf16[256,512]{1,0:T(8,128)(2,1)}, f32[256,512]{1,0:T(8,128)}) custom-call(s32[8]{0:T(128)} %stack.35.ids_ref, bf16[4096,2048]{1,0:T(8,128)(2,1)} %e_ref.1, bf16[4096,2048]{1,0:T(8,128)(2,1)} %e_ref.1, bf16[4096,512]{1,0:T(8,128)(2,1)} %get-tuple-element.37.u_ref.refs_2_, bf16[256,512]{1,0:T(8,128)(2,1)} %copy-done.23), custom_call_target="tpu_custom_call" | custom-call | flops 429496736 | bytes 1677721 | tf_op jit(solution)/shard_map/part/pallas_call | solution.py:151
  47.1 5.8 %collective-permute-done.11.refs_2_ = bf16[256,512]{1,0:T(8,128)(2,1)S(1)} collective-permute-done((bf16[256,512]{1,0:T(8,128)(2,1)}, bf16[256,512]{1,0:T(8,128)(2,1)S(1)}, u32[]{:S(2)}, u32[]{:S(2)}) %collective-permute-start.11) | collective-permute-done | bytes 262176 | tf_op jit(solution)/shard_map/ppermute | solution.py:531
  54.5 2.0 add_blocks.1
  56.5 2.7 %collective-permute-start.12 = (bf16[256,512]{1,0:T(8,128)(2,1)}, bf16[256,512]{1,0:T(8,128)(2,1)S(1)}, u32[]{:S(2)}, u32[]{:S(2)}) collective-permute-start(bf16[256,512]{1,0:T(8,128)(2,1)} %add_blocks.1), channel_id=1, source_target_pairs={{0,16},{1,17},{2,18},{3,19},{4,20},{5,21},{6,22},{7,23},{8,24},{9,... | collective-permute-start | bytes 786440 | tf_op jit(solution)/shard_map/ppermute | solution.py:531
  59.9 7.4 %part.5 = (bf16[256,512]{1,0:T(8,128)(2,1)}, f32[256,512]{1,0:T(8,128)}) custom-call(s32[8]{0:T(128)} %stack.35.ids_ref, bf16[4096,2048]{1,0:T(8,128)(2,1)} %e_ref.1, bf16[4096,2048]{1,0:T(8,128)(2,1)} %e_ref.1, bf16[4096,512]{1,0:T(8,128)(2,1)} %get-tuple-element.37.u_ref.refs_2_, bf16[256,512]{1,0:T(8,128)(2,1)} %copy-done.21, bf16[256,512]{1,0:T(8,128)(2,1)} %copy-done.22), custom_call_target="tpu_custom_call" | custom-call | flops 429496736 | bytes 1677721 | tf_op jit(solution)/shard_map/part/pallas_call | solution.py:151
  68.7 4.3 %collective-permute-done.2 = f32[16,512]{1,0:T(8,128)S(1)} collective-permute-done((f32[16,512]{1,0:T(8,128)S(1)}, f32[16,512]{1,0:T(8,128)S(1)}, u32[]{:S(2)}, u32[]{:S(2)}) %collective-permute-start.2) | collective-permute-done | bytes 32800 | tf_op jit(solution)/shard_map/ppermute | solution.py:531
  75.0 2.5 %predicted.1 = (f32[256,512]{1,0:T(8,128)}, f32[24,256]{1,0:T(8,128)}) custom-call(f32[256,512]{1,0:T(8,128)} %get-tuple-element.41.refs_0_, bf16[256,512]{1,0:T(8,128)(2,1)} %copy-done.26, bf16[256,512]{1,0:T(8,128)(2,1)} %copy-done.25, f32[16,512]{1,0:T(8,128)} %add.38.tops_ref.refs_3_.refs_20_.refs_8_, f32[256,512]{1,0:T(8,128)} %t_ref.1, ...), custom_call_target="tpu_custom_call" | custom-call | bytes 419430 | tf_op jit(solution)/shard_map/predicted/pallas_call | solution.py:213
  80.5 3.2 %collective-permute-done.15 = f32[24,256]{1,0:T(8,128)S(1)} collective-permute-done((f32[24,256]{1,0:T(8,128)S(1)}, f32[24,256]{1,0:T(8,128)S(1)}, u32[]{:S(2)}, u32[]{:S(2)}) %collective-permute-start.15) | collective-permute-done | bytes 24608 | tf_op jit(solution)/shard_map/ppermute | solution.py:540
  84.2 4.2 %collective-permute-done.16.f_ref = f32[24,256]{1,0:T(8,128)S(1)} collective-permute-done((f32[24,256]{1,0:T(8,128)S(1)}, f32[24,256]{1,0:T(8,128)S(1)}, u32[]{:S(2)}, u32[]{:S(2)}) %collective-permute-start.16) | collective-permute-done | bytes 24608 | tf_op jit(solution)/shard_map/ppermute | solution.py:540
  89.0 2.6 %grad.1 = (bf16[256,512]{1,0:T(8,128)(2,1)}, f32[8,512]{1,0:T(8,128)}) custom-call(f32[24,256]{1,0:T(8,128)} %copy-done.29, f32[24,256]{1,0:T(8,128)} %copy-done.32, f32[256,512]{1,0:T(8,128)} %get-tuple-element.32.p_ref, f32[256,512]{1,0:T(8,128)} %t_ref.1, f32[16,512]{1,0:T(8,128)} %add.38.tops_ref.refs_3_.refs_20_.refs_8_, f32[8,512]{1,0:T(8,128)} %fusion.m_ref.refs_5_), custom_call_target="tpu_custom_call" | custom-call | bytes 314572 | tf_op jit(solution)/shard_map/grad/pallas_call | solution.py:246
  91.6 2.8 %collective-permute-start.22 = (bf16[256,512]{1,0:T(8,128)(2,1)}, bf16[256,512]{1,0:T(8,128)(2,1)S(1)}, u32[]{:S(2)}, u32[]{:S(2)}) collective-permute-start(bf16[256,512]{1,0:T(8,128)(2,1)} %get-tuple-element.61.refs_7_), channel_id=1, source_target_pairs={{0,16},{1,17},{2,18},{3,19},{4,20},{5,21},{6,22},{7,23},{8,24},{9,... | collective-permute-start | bytes 786440 | tf_op jit(solution)/shard_map/ppermute | solution.py:531
  94.5 3.7 %density.1 = f32[8,4096]{1,0:T(8,128)} custom-call(bf16[4096,512]{1,0:T(8,128)(2,1)} %get-tuple-element.37.u_ref.refs_2_, f32[16,512]{1,0:T(8,128)} %add.38.tops_ref.refs_3_.refs_20_.refs_8_, f32[8,512]{1,0:T(8,128)} %fusion.m_ref.refs_5_), custom_call_target="tpu_custom_call" | custom-call | bytes 838860 | tf_op jit(solution)/shard_map/density/pallas_call | solution.py:267
  101.2 3.7 %collective-permute-done.22.refs_6_ = bf16[256,512]{1,0:T(8,128)(2,1)S(1)} collective-permute-done((bf16[256,512]{1,0:T(8,128)(2,1)}, bf16[256,512]{1,0:T(8,128)(2,1)S(1)}, u32[]{:S(2)}, u32[]{:S(2)}) %collective-permute-start.22) | collective-permute-done | bytes 262176 | tf_op jit(solution)/shard_map/ppermute | solution.py:531
  108.6 5.5 %collective-permute-done.23.refs_4_ = bf16[256,512]{1,0:T(8,128)(2,1)S(1)} collective-permute-done((bf16[256,512]{1,0:T(8,128)(2,1)S(1)}, bf16[256,512]{1,0:T(8,128)(2,1)S(1)}, u32[]{:S(2)}, u32[]{:S(2)}) %collective-permute-start.23) | collective-permute-done | bytes 262176 | tf_op jit(solution)/shard_map/ppermute | solution.py:531
  116.9 3.6 %collective-permute-done.24.refs_0_ = bf16[256,512]{1,0:T(8,128)(2,1)S(1)} collective-permute-done((bf16[256,512]{1,0:T(8,128)(2,1)S(1)}, bf16[256,512]{1,0:T(8,128)(2,1)S(1)}, u32[]{:S(2)}, u32[]{:S(2)}) %collective-permute-start.24) | collective-permute-done | bytes 262176 | tf_op jit(solution)/shard_map/ppermute | solution.py:531
  121.2 3.6 %regroup.1 = (bf16[512,512]{1,0:T(8,128)(2,1)}, bf16[512,512]{1,0:T(8,128)(2,1)}, bf16[1024,512]{1,0:T(8,128)(2,1)}) custom-call(s32[8]{0:T(128)} %stack.35.ids_ref, s32[1]{0:T(128)} %bitcast.12.place_ref, bf16[256,512]{1,0:T(8,128)(2,1)} %copy-done.8, bf16[256,512]{1,0:T(8,128)(2,1)} %copy-done.6, bf16[256,512]{1,0:T(8,128)(2,1)} %copy-done.7, ...), custom_call_target="tpu_custom_call" | custom-call | bytes 838860 | tf_op jit(solution)/shard_map/regroup/pallas_call | solution.py:400
  124.8 18.3 %collective-permute-done.30.refs_2_ = bf16[512,512]{1,0:T(8,128)(2,1)S(1)} collective-permute-done((bf16[512,512]{1,0:T(8,128)(2,1)S(1)}, bf16[512,512]{1,0:T(8,128)(2,1)S(1)}, u32[]{:S(2)}, u32[]{:S(2)}) %collective-permute-start.30) | collective-permute-done | bytes 524320 | tf_op jit(solution)/shard_map/ppermute | solution.py:534
  145.2 4.2 %diverge.1 = (bf16[32,4096]{1,0:T(8,128)(2,1)}, bf16[32,512]{1,0:T(8,128)(2,1)}, f32[8,512]{1,0:T(8,128)}) custom-call(f32[8,4096]{1,0:T(8,128)} %copy-done.20, f32[8,4096]{1,0:T(8,128)} %copy-done.28, s32[1,4096]{1,0:T(1,128)} %bitcast.20, s32[8,1]{1,0:T(8,128)} %copy.12.c_ref, bf16[4096,512]{1,0:T(8,128)(2,1)} %get-tuple-element.37.u_ref.refs_2_, ...), custom_call_target="tpu_custom_call" | custom-call | bytes 838860 | tf_op jit(solution)/shard_map/diverge/pallas_call | solution.py:329
  150.0 3.3 %collective-permute-done.18 = f32[8,512]{1,0:T(8,128)S(1)} collective-permute-done((f32[8,512]{1,0:T(8,128)}, f32[8,512]{1,0:T(8,128)S(1)}, u32[]{:S(2)}, u32[]{:S(2)}) %collective-permute-start.18) | collective-permute-done | bytes 16416 | tf_op jit(solution)/shard_map/ppermute | solution.py:531
  155.1 2.8 %collective-permute-done.19 = f32[8,512]{1,0:T(8,128)S(1)} collective-permute-done((f32[8,512]{1,0:T(8,128)S(1)}, f32[8,512]{1,0:T(8,128)S(1)}, u32[]{:S(2)}, u32[]{:S(2)}) %collective-permute-start.19) | collective-permute-done | bytes 16416 | tf_op jit(solution)/shard_map/ppermute | solution.py:531
  157.8 10.5 %collective-permute-done.33 = bf16[1024,512]{1,0:T(8,128)(2,1)} collective-permute-done((bf16[1024,512]{1,0:T(8,128)(2,1)}, bf16[1024,512]{1,0:T(8,128)(2,1)}, u32[]{:S(2)}, u32[]{:S(2)}) %collective-permute-start.33) | collective-permute-done | bytes 1048608 | tf_op jit(solution)/shard_map/ppermute | solution.py:534
  168.7 2.1 dynamic-slice_bitcast_fusion
  170.7 2.2 %collective-permute-done.20 = f32[8,512]{1,0:T(8,128)S(1)} collective-permute-done((f32[8,512]{1,0:T(8,128)S(1)}, f32[8,512]{1,0:T(8,128)S(1)}, u32[]{:S(2)}, u32[]{:S(2)}) %collective-permute-start.20) | collective-permute-done | bytes 16416 | tf_op jit(solution)/shard_map/ppermute | solution.py:531
  175.4 17.9 %grad_logits.1 = f32[4096,512]{1,0:T(8,128)} custom-call(s32[8]{0:T(128)} %stack.35.ids_ref, bf16[4096,2048]{1,0:T(8,128)(2,1)} %e_ref.1, bf16[4096,512]{1,0:T(8,128)(2,1)} %get-tuple-element.37.u_ref.refs_2_, bf16[32,4096]{1,0:T(8,128)(2,1)} %get-tuple-element.57.d_ref, bf16[32,512]{1,0:T(8,128)(2,1)} %get-tuple-element.58.w_ref, f32[8,512]{1,0:T(8,128)} %copy-done.30, ...), custom_call_target="tpu_custom_call" | custom-call | flops 1717986944 | bytes 5872025 | tf_op jit(solution)/shard_map/grad_logits/pallas_call | solution.py:440
  194.4 15.9 %grad_expression.2.refs_9_ = f32[4096,512]{1,0:T(8,128)} custom-call(bf16[512,512]{1,0:T(8,128)(2,1)} %get-tuple-element.44.refs_0_, bf16[512,512]{1,0:T(8,128)(2,1)} %copy-done.16, bf16[512,512]{1,0:T(8,128)(2,1)} %copy-done.15, bf16[512,512]{1,0:T(8,128)(2,1)} %collective-permute-done.36.refs_3_, bf16[1024,512]{1,0:T(8,128)(2,1)} %get-tuple-element.49.refs_4_, ...), custom_call_target="tpu_custom_call" | custom-call | flops 1503238528 | bytes 4404019 | tf_op jit(solution)/shard_map/grad_expression/pallas_call | solution.py:499
  211.9 4.4 %grad_expression.3 = f32[4096,512]{1,0:T(8,128)} custom-call(bf16[512,512]{1,0:T(8,128)(2,1)} %get-tuple-element.62.refs_0_, bf16[512,512]{1,0:T(8,128)(2,1)} %copy-done.18, bf16[512,512]{1,0:T(8,128)(2,1)} %copy-done.17, bf16[512,512]{1,0:T(8,128)(2,1)} %copy-done.19, ...), custom_call_target="tpu_custom_call", output_to_operand_aliasing={{}: (9, {})} | custom-call | flops 214748368 | bytes 629145 | tf_op jit(solution)/shard_map/grad_expression/pallas_call | solution.py:499
  (156 shorter events, 36.2 us)
Async XLA Ops:
  3.0 33.1 %collective-permute-start.9 = (bf16[512,512]{1,0:T(8,128)(2,1)}, bf16[512,512]{1,0:T(8,128)(2,1)S(1)}, u32[]{:S(2)}, u32[]{:S(2)}) collective-permute-start(bf16[512,512]{1,0:T(8,128)(2,1)} %get-tuple-element.44.refs_0_), channel_id=1, source_target_pairs={{0,2},{1,3},{2,0},{3,1},{4,6},{5,7},{6,4},{7,5},{8,10},{9,11},{10,... | collective-permute-start | bytes 1572872 | tf_op jit(solution)/shard_map/ppermute | solution.py:534
  15.3 58.8 %collective-permute-start.13 = (bf16[1024,512]{1,0:T(8,128)(2,1)}, bf16[1024,512]{1,0:T(8,128)(2,1)S(1)}, u32[]{:S(2)}, u32[]{:S(2)}) collective-permute-start(bf16[1024,512]{1,0:T(8,128)(2,1)} %get-tuple-element.49.refs_4_), channel_id=1, source_target_pairs={{0,2},{1,3},{2,0},{3,1},{4,6},{5,7},{6,4},{7,5},{8,10},{9,11},{10,... | collective-permute-start | bytes 3145736 | tf_op jit(solution)/shard_map/ppermute | solution.py:534
  15.4 68.8 %collective-permute-start.17 = (bf16[1024,512]{1,0:T(8,128)(2,1)}, bf16[1024,512]{1,0:T(8,128)(2,1)S(1)}, u32[]{:S(2)}, u32[]{:S(2)}) collective-permute-start(bf16[1024,512]{1,0:T(8,128)(2,1)} %get-tuple-element.52.refs_8_), channel_id=1, source_target_pairs={{0,2},{1,3},{2,0},{3,1},{4,6},{5,7},{6,4},{7,5},{8,10},{9,11},{10,... | collective-permute-start | bytes 3145736 | tf_op jit(solution)/shard_map/ppermute | solution.py:534
  25.3 9.3 %collective-permute-start.8 = (bf16[256,512]{1,0:T(8,128)(2,1)}, bf16[256,512]{1,0:T(8,128)(2,1)S(1)}, u32[]{:S(2)}, u32[]{:S(2)}) collective-permute-start(bf16[256,512]{1,0:T(8,128)(2,1)} %get-tuple-element.43), channel_id=1, source_target_pairs={{0,4},{1,9},{2,6},{3,11},{4,0},{5,13},{6,2},{7,15},{8,12},{9,1},{1... | collective-permute-start | bytes 786440 | tf_op jit(solution)/shard_map/ppermute | solution.py:531
  26.8 18.9 %collective-permute-start.10 = (bf16[256,512]{1,0:T(8,128)(2,1)}, bf16[256,512]{1,0:T(8,128)(2,1)S(1)}, u32[]{:S(2)}, u32[]{:S(2)}) collective-permute-start(bf16[256,512]{1,0:T(8,128)(2,1)} %get-tuple-element.47), channel_id=1, source_target_pairs={{0,4},{1,9},{2,6},{3,11},{4,0},{5,13},{6,2},{7,15},{8,12},{9,1},{1... | collective-permute-start | bytes 786440 | tf_op jit(solution)/shard_map/ppermute | solution.py:531
  34.6 10.5 %collective-permute-start = (f32[16,512]{1,0:T(8,128)S(1)}, f32[16,512]{1,0:T(8,128)S(1)}, u32[]{:S(2)}, u32[]{:S(2)}) collective-permute-start(f32[16,512]{1,0:T(8,128)S(1)} %copy-done.31), channel_id=1, source_target_pairs={{0,4},{1,9},{2,6},{3,11},{4,0},{5,13},{6,2},{7,15},{8,12},{9,1},{1... | collective-permute-start | bytes 98312 | tf_op jit(solution)/shard_map/ppermute | solution.py:531
  43.5 9.5 %collective-permute-start.11 = (bf16[256,512]{1,0:T(8,128)(2,1)}, bf16[256,512]{1,0:T(8,128)(2,1)S(1)}, u32[]{:S(2)}, u32[]{:S(2)}) collective-permute-start(bf16[256,512]{1,0:T(8,128)(2,1)} %get-tuple-element.48), channel_id=1, source_target_pairs={{0,8},{1,5},{2,10},{3,7},{4,12},{5,1},{6,14},{7,3},{8,0},{9,13},{1... | collective-permute-start | bytes 786440 | tf_op jit(solution)/shard_map/ppermute | solution.py:531
  45.0 11.4 %collective-permute-start.5 = (bf16[256,512]{1,0:T(8,128)(2,1)S(1)}, bf16[256,512]{1,0:T(8,128)(2,1)S(1)}, u32[]{:S(2)}, u32[]{:S(2)}) collective-permute-start(bf16[256,512]{1,0:T(8,128)(2,1)S(1)} %copy-done.36), channel_id=1, source_target_pairs={{0,4},{1,9},{2,6},{3,11},{4,0},{5,13},{6,2},{7,15},{8,12},{9,1},{1... | collective-permute-start | bytes 786440 | tf_op jit(solution)/shard_map/ppermute | solution.py:531
  45.6 13.5 %collective-permute-start.6 = (bf16[256,512]{1,0:T(8,128)(2,1)S(1)}, bf16[256,512]{1,0:T(8,128)(2,1)S(1)}, u32[]{:S(2)}, u32[]{:S(2)}) collective-permute-start(bf16[256,512]{1,0:T(8,128)(2,1)S(1)} %copy-done.35), channel_id=1, source_target_pairs={{0,4},{1,9},{2,6},{3,11},{4,0},{5,13},{6,2},{7,15},{8,12},{9,1},{1... | collective-permute-start | bytes 786440 | tf_op jit(solution)/shard_map/ppermute | solution.py:531
  52.9 15.1 %collective-permute-start.1 = (f32[16,512]{1,0:T(8,128)S(1)}, f32[16,512]{1,0:T(8,128)S(1)}, u32[]{:S(2)}, u32[]{:S(2)}) collective-permute-start(f32[16,512]{1,0:T(8,128)S(1)} %add.36), channel_id=1, source_target_pairs={{0,8},{1,5},{2,10},{3,7},{4,12},{5,1},{6,14},{7,3},{8,0},{9,13},{1... | collective-permute-start | bytes 98312 | tf_op jit(solution)/shard_map/ppermute | solution.py:531
  56.5 17.7 %collective-permute-start.12 = (bf16[256,512]{1,0:T(8,128)(2,1)}, bf16[256,512]{1,0:T(8,128)(2,1)S(1)}, u32[]{:S(2)}, u32[]{:S(2)}) collective-permute-start(bf16[256,512]{1,0:T(8,128)(2,1)} %add_blocks.1), channel_id=1, source_target_pairs={{0,16},{1,17},{2,18},{3,19},{4,20},{5,21},{6,22},{7,23},{8,24},{9,... | collective-permute-start | bytes 786440 | tf_op jit(solution)/shard_map/ppermute | solution.py:531
  73.0 34.4 %collective-permute-start.35 = (bf16[512,512]{1,0:T(8,128)(2,1)S(1)}, bf16[512,512]{1,0:T(8,128)(2,1)S(1)}, u32[]{:S(2)}, u32[]{:S(2)}) collective-permute-start(bf16[512,512]{1,0:T(8,128)(2,1)S(1)} %copy-done.14), channel_id=1, source_target_pairs={{0,1},{1,0},{2,3},{3,2},{4,5},{5,4},{6,7},{7,6},{8,9},{9,8},{10,11... | collective-permute-start | bytes 1572872 | tf_op jit(solution)/shard_map/ppermute | solution.py:534
  91.6 13.3 %collective-permute-start.22 = (bf16[256,512]{1,0:T(8,128)(2,1)}, bf16[256,512]{1,0:T(8,128)(2,1)S(1)}, u32[]{:S(2)}, u32[]{:S(2)}) collective-permute-start(bf16[256,512]{1,0:T(8,128)(2,1)} %get-tuple-element.61.refs_7_), channel_id=1, source_target_pairs={{0,16},{1,17},{2,18},{3,19},{4,20},{5,21},{6,22},{7,23},{8,24},{9,... | collective-permute-start | bytes 786440 | tf_op jit(solution)/shard_map/ppermute | solution.py:531
  94.5 11.5 %collective-permute-start.25 = (bf16[256,512]{1,0:T(8,128)(2,1)}, bf16[256,512]{1,0:T(8,128)(2,1)S(1)}, u32[]{:S(2)}, u32[]{:S(2)}) collective-permute-start(bf16[256,512]{1,0:T(8,128)(2,1)} %get-tuple-element.61.refs_7_), channel_id=1, source_target_pairs={{0,8},{1,5},{2,10},{3,7},{4,12},{5,1},{6,14},{7,3},{8,0},{9,13},{1... | collective-permute-start | bytes 786440 | tf_op jit(solution)/shard_map/ppermute | solution.py:531
  98.2 9.3 %collective-permute-start.28 = (bf16[256,512]{1,0:T(8,128)(2,1)}, bf16[256,512]{1,0:T(8,128)(2,1)S(1)}, u32[]{:S(2)}, u32[]{:S(2)}) collective-permute-start(bf16[256,512]{1,0:T(8,128)(2,1)} %get-tuple-element.61.refs_7_), channel_id=1, source_target_pairs={{0,4},{1,9},{2,6},{3,11},{4,0},{5,13},{6,2},{7,15},{8,12},{9,1},{1... | collective-permute-start | bytes 786440 | tf_op jit(solution)/shard_map/ppermute | solution.py:531
  104.9 9.2 %collective-permute-start.23 = (bf16[256,512]{1,0:T(8,128)(2,1)S(1)}, bf16[256,512]{1,0:T(8,128)(2,1)S(1)}, u32[]{:S(2)}, u32[]{:S(2)}) collective-permute-start(bf16[256,512]{1,0:T(8,128)(2,1)S(1)} %collective-permute-done.22.refs_6_), channel_id=1, source_target_pairs={{0,8},{1,5},{2,10},{3,7},{4,12},{5,1},{6,14},{7,3},{8,0},{9,13},{1... | collective-permute-start | bytes 786440 | tf_op jit(solution)/shard_map/ppermute | solution.py:531
  105.9 8.8 %collective-permute-start.26 = (bf16[256,512]{1,0:T(8,128)(2,1)S(1)}, bf16[256,512]{1,0:T(8,128)(2,1)S(1)}, u32[]{:S(2)}, u32[]{:S(2)}) collective-permute-start(bf16[256,512]{1,0:T(8,128)(2,1)S(1)} %collective-permute-done.25.refs_5_), channel_id=1, source_target_pairs={{0,4},{1,9},{2,6},{3,11},{4,0},{5,13},{6,2},{7,15},{8,12},{9,1},{1... | collective-permute-start | bytes 786440 | tf_op jit(solution)/shard_map/ppermute | solution.py:531
  106.8 42.5 %collective-permute-start.21 = (bf16[1024,512]{1,0:T(8,128)(2,1)}, bf16[1024,512]{1,0:T(8,128)(2,1)}, u32[]{:S(2)}, u32[]{:S(2)}) collective-permute-start(bf16[1024,512]{1,0:T(8,128)(2,1)} %get-tuple-element.59.refs_12_), channel_id=1, source_target_pairs={{0,2},{1,3},{2,0},{3,1},{4,6},{5,7},{6,4},{7,5},{8,10},{9,11},{10,... | collective-permute-start | bytes 3145736 | tf_op jit(solution)/shard_map/ppermute | solution.py:534
  107.3 42.7 %collective-permute-start.37 = (bf16[1024,512]{1,0:T(8,128)(2,1)S(1)}, bf16[1024,512]{1,0:T(8,128)(2,1)}, u32[]{:S(2)}, u32[]{:S(2)}) collective-permute-start(bf16[1024,512]{1,0:T(8,128)(2,1)S(1)} %copy-done.9), channel_id=1, source_target_pairs={{0,1},{1,0},{2,3},{3,2},{4,5},{5,4},{6,7},{7,6},{8,9},{9,8},{10,11... | collective-permute-start | bytes 3145736 | tf_op jit(solution)/shard_map/ppermute | solution.py:534
  107.4 7.9 %collective-permute-start.27 = (bf16[256,512]{1,0:T(8,128)(2,1)S(1)}, bf16[256,512]{1,0:T(8,128)(2,1)S(1)}, u32[]{:S(2)}, u32[]{:S(2)}) collective-permute-start(bf16[256,512]{1,0:T(8,128)(2,1)S(1)} %collective-permute-done.22.refs_6_), channel_id=1, source_target_pairs={{0,4},{1,9},{2,6},{3,11},{4,0},{5,13},{6,2},{7,15},{8,12},{9,1},{1... | collective-permute-start | bytes 786440 | tf_op jit(solution)/shard_map/ppermute | solution.py:531
  114.8 28.4 %collective-permute-start.30 = (bf16[512,512]{1,0:T(8,128)(2,1)S(1)}, bf16[512,512]{1,0:T(8,128)(2,1)S(1)}, u32[]{:S(2)}, u32[]{:S(2)}) collective-permute-start(bf16[512,512]{1,0:T(8,128)(2,1)S(1)} %copy-done.13), channel_id=1, source_target_pairs={{0,2},{1,3},{2,0},{3,1},{4,6},{5,7},{6,4},{7,5},{8,10},{9,11},{10,... | collective-permute-start | bytes 1572872 | tf_op jit(solution)/shard_map/ppermute | solution.py:534
  115.3 38.7 %collective-permute-start.39 = (bf16[1024,512]{1,0:T(8,128)(2,1)}, bf16[1024,512]{1,0:T(8,128)(2,1)}, u32[]{:S(2)}, u32[]{:S(2)}) collective-permute-start(bf16[1024,512]{1,0:T(8,128)(2,1)} %get-tuple-element.52.refs_8_), channel_id=1, source_target_pairs={{0,1},{1,0},{2,3},{3,2},{4,5},{5,4},{6,7},{7,6},{8,9},{9,8},{10,11... | collective-permute-start | bytes 3145736 | tf_op jit(solution)/shard_map/ppermute | solution.py:534
  120.5 34.5 %collective-permute-start.41 = (bf16[1024,512]{1,0:T(8,128)(2,1)}, bf16[1024,512]{1,0:T(8,128)(2,1)}, u32[]{:S(2)}, u32[]{:S(2)}) collective-permute-start(bf16[1024,512]{1,0:T(8,128)(2,1)} %get-tuple-element.59.refs_12_), channel_id=1, source_target_pairs={{0,1},{1,0},{2,3},{3,2},{4,5},{5,4},{6,7},{7,6},{8,9},{9,8},{10,11... | collective-permute-start | bytes 3145736 | tf_op jit(solution)/shard_map/ppermute | solution.py:534
  144.0 24.3 %collective-permute-start.33 = (bf16[1024,512]{1,0:T(8,128)(2,1)}, bf16[1024,512]{1,0:T(8,128)(2,1)}, u32[]{:S(2)}, u32[]{:S(2)}) collective-permute-start(bf16[1024,512]{1,0:T(8,128)(2,1)} %get-tuple-element.65), channel_id=1, source_target_pairs={{0,2},{1,3},{2,0},{3,1},{4,6},{5,7},{6,4},{7,5},{8,10},{9,11},{10,... | collective-permute-start | bytes 3145736 | tf_op jit(solution)/shard_map/ppermute | solution.py:534
  150.0 23.0 %collective-permute-start.38 = (bf16[1024,512]{1,0:T(8,128)(2,1)S(1)}, bf16[1024,512]{1,0:T(8,128)(2,1)S(1)}, u32[]{:S(2)}, u32[]{:S(2)}) collective-permute-start(bf16[1024,512]{1,0:T(8,128)(2,1)S(1)} %collective-permute-done.13.refs_6_), channel_id=1, source_target_pairs={{0,1},{1,0},{2,3},{3,2},{4,5},{5,4},{6,7},{7,6},{8,9},{9,8},{10,11... | collective-permute-start | bytes 3145736 | tf_op jit(solution)/shard_map/ppermute | solution.py:534
  153.4 20.1 %collective-permute-start.40 = (bf16[1024,512]{1,0:T(8,128)(2,1)S(1)}, bf16[1024,512]{1,0:T(8,128)(2,1)}, u32[]{:S(2)}, u32[]{:S(2)}) collective-permute-start(bf16[1024,512]{1,0:T(8,128)(2,1)S(1)} %collective-permute-done.17.refs_10_), channel_id=1, source_target_pairs={{0,1},{1,0},{2,3},{3,2},{4,5},{5,4},{6,7},{7,6},{8,9},{9,8},{10,11... | collective-permute-start | bytes 3145736 | tf_op jit(solution)/shard_map/ppermute | solution.py:534
  155.0 15.7 %collective-permute-start.36 = (bf16[512,512]{1,0:T(8,128)(2,1)}, bf16[512,512]{1,0:T(8,128)(2,1)}, u32[]{:S(2)}, u32[]{:S(2)}) collective-permute-start(bf16[512,512]{1,0:T(8,128)(2,1)} %copy-done.15), channel_id=1, source_target_pairs={{0,1},{1,0},{2,3},{3,2},{4,5},{5,4},{6,7},{7,6},{8,9},{9,8},{10,11... | collective-permute-start | bytes 1572872 | tf_op jit(solution)/shard_map/ppermute | solution.py:534
  157.8 35.5 %collective-permute-start.42 = (bf16[1024,512]{1,0:T(8,128)(2,1)}, bf16[1024,512]{1,0:T(8,128)(2,1)}, u32[]{:S(2)}, u32[]{:S(2)}) collective-permute-start(bf16[1024,512]{1,0:T(8,128)(2,1)} %collective-permute-done.21.refs_14_), channel_id=1, source_target_pairs={{0,1},{1,0},{2,3},{3,2},{4,5},{5,4},{6,7},{7,6},{8,9},{9,8},{10,11... | collective-permute-start | bytes 3145736 | tf_op jit(solution)/shard_map/ppermute | solution.py:534
  170.7 22.7 %collective-permute-start.32 = (bf16[512,512]{1,0:T(8,128)(2,1)}, bf16[512,512]{1,0:T(8,128)(2,1)S(1)}, u32[]{:S(2)}, u32[]{:S(2)}) collective-permute-start(bf16[512,512]{1,0:T(8,128)(2,1)} %get-tuple-element.64), channel_id=1, source_target_pairs={{0,1},{1,0},{2,3},{3,2},{4,5},{5,4},{6,7},{7,6},{8,9},{9,8},{10,11... | collective-permute-start | bytes 1572872 | tf_op jit(solution)/shard_map/ppermute | solution.py:534
  173.0 20.4 %collective-permute-start.34 = (bf16[512,512]{1,0:T(8,128)(2,1)S(1)}, bf16[512,512]{1,0:T(8,128)(2,1)S(1)}, u32[]{:S(2)}, u32[]{:S(2)}) collective-permute-start(bf16[512,512]{1,0:T(8,128)(2,1)S(1)} %get-tuple-element.66), channel_id=1, source_target_pairs={{0,1},{1,0},{2,3},{3,2},{4,5},{5,4},{6,7},{7,6},{8,9},{9,8},{10,11... | collective-permute-start | bytes 1572872 | tf_op jit(solution)/shard_map/ppermute | solution.py:534
  173.0 37.3 %collective-permute-start.29 = (bf16[512,512]{1,0:T(8,128)(2,1)}, bf16[512,512]{1,0:T(8,128)(2,1)S(1)}, u32[]{:S(2)}, u32[]{:S(2)}) collective-permute-start(bf16[512,512]{1,0:T(8,128)(2,1)} %get-tuple-element.62.refs_0_), channel_id=1, source_target_pairs={{0,1},{1,0},{2,3},{3,2},{4,5},{5,4},{6,7},{7,6},{8,9},{9,8},{10,11... | collective-permute-start | bytes 1572872 | tf_op jit(solution)/shard_map/ppermute | solution.py:534
  173.5 36.8 %collective-permute-start.31 = (bf16[512,512]{1,0:T(8,128)(2,1)}, bf16[512,512]{1,0:T(8,128)(2,1)S(1)}, u32[]{:S(2)}, u32[]{:S(2)}) collective-permute-start(bf16[512,512]{1,0:T(8,128)(2,1)} %copy-done.17), channel_id=1, source_target_pairs={{0,1},{1,0},{2,3},{3,2},{4,5},{5,4},{6,7},{7,6},{8,9},{9,8},{10,11... | collective-permute-start | bytes 1572872 | tf_op jit(solution)/shard_map/ppermute | solution.py:534
  (48 other events, 765.7 us)

commit v2 on v1

v2 whole, which is shorter than its diff:
```python
import functools

import jax
import jax.numpy as jnp
from jax import lax
from jax.experimental import pallas as pl
from jax.experimental.pallas import tpu as pltpu
from jax.sharding import PartitionSpec as P

density_weight = 32.0
expression_scale = 64.0
norm_eps = 1e-06
f32 = jnp.float32
bf16 = jnp.bfloat16
VMEM_LIMIT = 16 << 20
COST_SHARE = 1.0
NT = (((1,), (1,)), ((), ()))
TN = (((0,), (0,)), ((), ()))


def cost(flops, bytes_accessed):
    return pl.CostEstimate(
        flops=int(flops * COST_SHARE),
        bytes_accessed=int(bytes_accessed * COST_SHARE),
        transcendentals=0,
    )


ANY = pl.BlockSpec(memory_space=pl.ANY)
HBM = pl.BlockSpec(memory_space=pltpu.HBM)
VMEM = pl.BlockSpec(memory_space=pltpu.VMEM)
SMEM = pl.BlockSpec(memory_space=pltpu.SMEM)


def params():
    return pltpu.CompilerParams(vmem_limit_bytes=VMEM_LIMIT)


def shape(dims, dtype):
    return jax.ShapeDtypeStruct(dims, dtype)


def dot(a, b, dims=(((1,), (0,)), ((), ()))):
    return lax.dot_general(a, b, dims, preferred_element_type=f32)


def halves(value):
    high = value.astype(bf16)
    return high, (value - high.astype(f32)).astype(bf16)


def thirds(value):
    high = value.astype(bf16)
    rest = value - high.astype(f32)
    middle = rest.astype(bf16)
    return high, middle, (rest - middle.astype(f32)).astype(bf16)


def split_rows(cells):
    unit = cells // 8
    return [unit, 2 * unit, 2 * unit, 2 * unit, unit]


def column_mask(k_ref, group, spots):
    line = jnp.broadcast_to(k_ref[group : group + 1, :].astype(f32), (128, 128)).T
    return jnp.concatenate([line] * (spots // 128), axis=1)


def in_hbm(value):
    return pltpu.with_memory_space_constraint(value, pltpu.HBM)


def first_call(logits, keep_rows, size):
    spots = logits.shape[1]

    def body(x_ref, k_ref, o_ref, x_buf, sem):
        copy = pltpu.make_async_copy(x_ref.at[pl.ds(0, size)], x_buf, sem)
        copy.start()
        copy.wait()
        for g in range(size // 128):
            at = slice(g * 128, (g + 1) * 128)
            o_ref[at, :] = (jnp.exp(x_buf[at, :]) * column_mask(k_ref, g, spots)).astype(bf16)

    return pl.pallas_call(
        body,
        in_specs=[HBM, VMEM],
        out_specs=VMEM,
        out_shape=shape((size, spots), bf16),
        scratch_shapes=[pltpu.VMEM((size, spots), f32), pltpu.SemaphoreType.DMA],
        compiler_params=params(),
        cost_estimate=cost(0, 6 * size * spots),
        name="exp_first",
    )(in_hbm(logits), keep_rows)


def exp_call(logits, keep_rows, sizes):
    cells, spots = logits.shape
    tile = 512
    steps = cells // tile
    starts = [sum(sizes[:c]) for c in range(len(sizes))]

    def body(x_ref, k_ref, *refs):
        piece_refs = (None, *refs[: len(sizes) - 1])
        u_ref, s_ref, x_buf, sem, p_sem = refs[len(sizes) - 1 :]
        fetch = [
            pltpu.make_async_copy(
                x_ref.at[pl.ds(t * tile, tile)], x_buf.at[pl.ds(t * tile, tile)], sem.at[t]
            )
            for t in range(steps)
        ]
        for copy in fetch:
            copy.start()
        total = jnp.zeros((8, spots), f32)
        sent = []
        for t in range(steps):
            fetch[t].wait()
            for g in range(tile // 128):
                at = slice(t * tile + g * 128, t * tile + (g + 1) * 128)
                rise = jnp.exp(x_buf[at, :])
                rise = rise * column_mask(k_ref, t * (tile // 128) + g, spots)
                u_ref[at, :] = rise.astype(bf16)
                total = total + jnp.sum(rise.reshape(16, 8, spots), axis=0)
            for c in range(1, len(sizes)):
                if starts[c] + sizes[c] == (t + 1) * tile:
                    copy = pltpu.make_async_copy(
                        u_ref.at[pl.ds(starts[c], sizes[c])], piece_refs[c], p_sem.at[c]
                    )
                    copy.start()
                    sent.append(copy)
        s_ref[0:8, :] = total
        kept = jnp.sum(k_ref[...].astype(f32)) * 0.125
        s_ref[8:16, :] = jnp.full((8, spots), kept, f32)
        for copy in sent:
            copy.wait()

    return pl.pallas_call(
        body,
        in_specs=[HBM, VMEM],
        out_specs=[HBM] * (len(sizes) - 1) + [VMEM] * 2,
        out_shape=[pltpu.HBM((size, spots), bf16) for size in sizes[1:]]
        + [shape((cells, spots), bf16), shape((16, spots), f32)],
        scratch_shapes=[
            pltpu.VMEM((cells, spots), f32),
            pltpu.SemaphoreType.DMA((steps,)),
            pltpu.SemaphoreType.DMA((len(sizes),)),
        ],
        compiler_params=params(),
        cost_estimate=cost(0, 8 * cells * spots),
        name="exp_rows",
    )(in_hbm(logits), keep_rows)


def part_call(expression, mapping, ids, picks, adds, dtypes):
    cells, spots = mapping.shape
    count = len(picks)
    block = expression.shape[1] // ids.shape[0]

    def body(ids_ref, e_ref, u_ref, *refs):
        a_refs, o_refs = refs[: len(adds)], refs[len(adds) : len(adds) + count]
        held, sem = refs[len(adds) + count :]
        copies = []
        for q, pick in enumerate(picks):
            at = pl.ds(pl.multiple_of(ids_ref[pick] * block, block), block)
            copies.append(pltpu.make_async_copy(e_ref.at[:, at], held.at[q], sem.at[q]))
            copies[q].start()
        for q in range(count):
            copies[q].wait()
            total = dot(held[q], u_ref[...], TN)
            if q < len(adds):
                total = total + a_refs[q][...].astype(f32)
            o_refs[q][...] = total.astype(dtypes[q])

    return pl.pallas_call(
        body,
        in_specs=[SMEM, HBM, VMEM] + [VMEM] * len(adds),
        out_specs=[VMEM] * count,
        out_shape=[shape((block, spots), dtype) for dtype in dtypes],
        scratch_shapes=[
            pltpu.VMEM((count, cells, block), bf16),
            pltpu.SemaphoreType.DMA((count,)),
        ],
        compiler_params=params(),
        cost_estimate=cost(
            2 * count * block * cells * spots, 2 * cells * (count * block + spots)
        ),
        name="part",
    )(ids, in_hbm(expression), mapping, *adds)


def add_call(values):
    def body(*refs):
        total = refs[0][...].astype(f32)
        for ref in refs[1:-1]:
            total = total + ref[...].astype(f32)
        refs[-1][...] = total.astype(bf16)

    return pl.pallas_call(
        body,
        out_shape=shape(values[0].shape, bf16),
        compiler_params=params(),
        cost_estimate=cost(0, 8 * values[0].size),
        name="add_blocks",
    )(*values)


def total_of(tops_ref):
    return jnp.sum(tops_ref[0:8, :], axis=0, keepdims=True)


def kept_of(tops_ref):
    return jnp.sum(tops_ref[8:16, 0:1], axis=0, keepdims=True)


def predicted_call(values, tops, target, member):
    block, spots = target.shape
    slides = member.shape[0]

    def body(*refs):
        v_refs, (tops_ref, t_ref, m_ref, p_ref, s_ref) = refs[:-5], refs[-5:]
        total = v_refs[0][...].astype(f32)
        for ref in v_refs[1:]:
            total = total + ref[...].astype(f32)
        pred = total / total_of(tops_ref)
        p_ref[...] = pred
        target_now = t_ref[...]
        member_low = m_ref[...].astype(bf16)
        for q, value in enumerate((pred * target_now, pred * pred, target_now * target_now)):
            high, low = halves(value)
            s_ref[q * slides : (q + 1) * slides, :] = dot(member_low, high, NT) + dot(
                member_low, low, NT
            )

    return pl.pallas_call(
        body,
        out_shape=[shape((block, spots), f32), shape((3 * slides, block), f32)],
        compiler_params=params(),
        cost_estimate=cost(0, 16 * block * spots),
        name="predicted",
    )(*values, tops, target, member)


def grad_call(sums, far, pred, target, tops, member):
    block, spots = target.shape
    slides = member.shape[0]

    def body(s_ref, f_ref, p_ref, t_ref, tops_ref, m_ref, g_ref, e_ref):
        total = s_ref[...] + f_ref[...]
        inner = total[0:slides, :]
        inv_predict = lax.rsqrt(total[slides : 2 * slides, :] + norm_eps)
        inv_target = lax.rsqrt(total[2 * slides : 3 * slides, :] + norm_eps)
        pair = inv_predict * inv_target
        cosine = inner * pair
        member_low = m_ref[...].astype(bf16)
        pair_at = sum(dot(v, member_low, TN) for v in thirds(pair))
        curve_at = sum(dot(v, member_low, TN) for v in thirds(cosine * inv_predict * inv_predict))
        pred = p_ref[...]
        grad = (pred * curve_at - t_ref[...] * pair_at) / total_of(tops_ref)
        grad = grad.astype(bf16)
        g_ref[...] = grad
        column = jnp.sum(pred * grad.astype(f32), axis=0, keepdims=True)
        total = jnp.sum(jnp.sum(cosine, axis=1, keepdims=True), axis=0, keepdims=True)
        e_ref[...] = jnp.concatenate(
            [column, jnp.broadcast_to(total, (1, spots)), jnp.zeros((6, spots), f32)], axis=0
        )

    return pl.pallas_call(
        body,
        out_shape=[shape((block, spots), bf16), shape((8, spots), f32)],
        compiler_params=params(),
        cost_estimate=cost(0, 12 * block * spots),
        name="grad",
    )(sums, far, pred, target, tops, member)


def density_call(mapping, tops, member):
    cells, spots = mapping.shape
    slides = member.shape[0]
    tile = min(cells, 1024)

    def body(u_ref, tops_ref, m_ref, o_ref):
        high, low = halves(m_ref[...] / total_of(tops_ref))
        pad = jnp.zeros((128 - 2 * slides, spots), bf16)
        both = jnp.concatenate([high, low, pad], axis=0)
        for t in range(cells // tile):
            at = slice(t * tile, (t + 1) * tile)
            got = dot(u_ref[at, :], both, NT).T
            o_ref[:, at] = got[0:slides, :] + got[slides : 2 * slides, :]

    return pl.pallas_call(
        body,
        in_specs=[VMEM] * 3,
        out_specs=VMEM,
        out_shape=shape((slides, cells), f32),
        compiler_params=params(),
        cost_estimate=cost(0, 2 * cells * spots),
        name="density",
    )(mapping, tops, member)


def diverge_call(density, far, keep_line, counts, mapping, tops, member):
    cells, spots = mapping.shape
    slides = member.shape[0]

    def body(d_ref, f_ref, k_ref, c_ref, u_ref, tops_ref, m_ref, o_ref, w_ref, e_ref):
        keep = k_ref[...].astype(f32)
        kept = kept_of(tops_ref)
        total = total_of(tops_ref)
        safe = jnp.where(keep > 0, d_ref[...] + f_ref[...], 1.0)
        high, low = halves(-density_weight * keep / (kept * safe))
        o_ref[...] = jnp.concatenate([high, high, low, jnp.zeros_like(low)], axis=0)
        w_high, w_low = halves(m_ref[...] / total)
        w_ref[...] = jnp.concatenate([w_high, w_low, w_high, jnp.zeros_like(w_low)], axis=0)
        column = jnp.zeros((8, spots), f32)
        chunk = 256
        for r in range(cells // chunk):
            at = slice(r * chunk, (r + 1) * chunk)
            pulled = dot(o_ref[:, at], w_ref[...], TN) * u_ref[at, :].astype(f32)
            column += jnp.sum(pulled.reshape(chunk // 8, 8, spots), axis=0)
        column = jnp.sum(column, axis=0, keepdims=True) / total
        logs = jnp.sum(jnp.log(safe), axis=0, keepdims=True)
        logs = -jnp.sum(logs, axis=1, keepdims=True)
        scale = jnp.sum(jnp.log(c_ref[...].astype(f32)), axis=1, keepdims=True)
        scale = scale - slides * jnp.log(kept)
        diverge = (logs + scale * jnp.sum(keep, axis=1, keepdims=True)) / kept
        e_ref[...] = jnp.concatenate(
            [
                column,
                jnp.zeros_like(column),
                jnp.broadcast_to(diverge, (1, spots)),
                jnp.zeros((5, spots), f32),
            ],
            axis=0,
        )

    return pl.pallas_call(
        body,
        in_specs=[VMEM] * 7,
        out_specs=[VMEM] * 3,
        out_shape=[
            shape((4 * slides, cells), bf16),
            shape((4 * slides, spots), bf16),
            shape((8, spots), f32),
        ],
        compiler_params=params(),
        cost_estimate=cost(0, 2 * cells * spots),
        name="diverge",
    )(density, far, keep_line, counts, mapping, tops, member)


def regroup_call(blocks, ids, place, spread):
    count = len(blocks)
    block, spots = blocks[0].shape
    share = count * block // spread

    def body(ids_ref, place_ref, *refs):
        b_refs, o_refs = refs[:count], refs[count : count + spread]
        held, in_sem, out_sem = refs[count + spread :]

        def rows(start, size):
            return held.at[pl.ds(pl.multiple_of(start, size), size)]

        copies = [
            pltpu.make_async_copy(b_refs[q], rows(ids_ref[q] * block, block), in_sem.at[q])
            for q in range(count)
        ]
        for copy in copies:
            copy.start()
        for copy in copies:
            copy.wait()
        copies = [
            pltpu.make_async_copy(rows((place_ref[0] ^ w) * share, share), o_refs[w], out_sem.at[w])
            for w in range(spread)
        ]
        for copy in copies:
            copy.start()
        for copy in copies:
            copy.wait()

    return pl.pallas_call(
        body,
        in_specs=[SMEM, SMEM] + [ANY] * count,
        out_specs=[HBM] * spread,
        out_shape=[shape((share, spots), bf16)] * spread,
        scratch_shapes=[
            pltpu.VMEM((count * block, spots), bf16),
            pltpu.SemaphoreType.DMA((count,)),
            pltpu.SemaphoreType.DMA((spread,)),
        ],
        compiler_params=params(),
        cost_estimate=cost(0, 4 * count * block * spots),
        name="regroup",
    )(ids, place, *blocks)


def logit_call(expression, blocks, ids, mapping, slope, weight, ends, tops):
    cells, genes = expression.shape
    block, spots = blocks[0].shape
    count = len(blocks)
    tile = min(cells, 1024)

    def body(ids_ref, e_ref, u_ref, d_ref, w_ref, ends_ref, tops_ref, *refs):
        b_refs, (o_ref, held, sem) = refs[:count], refs[count:]

        @pl.when(pl.program_id(0) == 0)
        def _():
            copies = []
            for q in range(count):
                at = pl.ds(pl.multiple_of(ids_ref[q] * block, block), block)
                copies.append(pltpu.make_async_copy(b_refs[q], held.at[at], sem.at[q]))
            for copy in copies:
                copy.start()
            for copy in copies:
                copy.wait()

        at = pl.ds(pl.multiple_of(pl.program_id(0) * tile, tile), tile)
        acc = dot(e_ref[at, :], held[...])
        acc += dot(d_ref[...], w_ref[...], TN) - ends_ref[0:1, :]
        o_ref[...] = u_ref[at, :].astype(f32) * (acc * kept_of(tops_ref))

    return pl.pallas_call(
        body,
        grid=(cells // tile,),
        in_specs=[SMEM, VMEM, VMEM, pl.BlockSpec((slope.shape[0], tile), lambda i: (0, i))]
        + [VMEM] * 3
        + [ANY] * count,
        out_specs=pl.BlockSpec((tile, spots), lambda i: (i, 0)),
        out_shape=shape((cells, spots), f32),
        scratch_shapes=[pltpu.VMEM((genes, spots), bf16), pltpu.SemaphoreType.DMA((count,))],
        compiler_params=params(),
        cost_estimate=cost(2 * cells * genes * spots, 2 * cells * genes + 6 * cells * spots),
        name="grad_logits",
    )(ids, expression, mapping, slope, weight, ends, tops, *blocks)


def expr_call(base, mapping, chunks, grads, tops, start):
    cells, spots = mapping.shape
    genes = grads[0].shape[0]
    count = len(grads)
    tile = 512
    tiles = [(c, t) for c in range(len(chunks)) for t in range(chunks[c][0].shape[0] // tile)]
    slots = min(3, len(tiles))
    flat = [v for chunk in chunks for v in chunk]

    def body(*refs):
        q_refs = refs[: len(flat)]
        u_ref = refs[len(flat)]
        g_refs = refs[len(flat) + 1 : len(flat) + 1 + count]
        tops_ref = refs[len(flat) + 1 + count]
        o_ref, held, out, in_sem, out_sem = refs[-5:]
        scale = expression_scale * kept_of(tops_ref)

        def fetch(k):
            c, t = tiles[k]
            return [
                pltpu.make_async_copy(
                    q_refs[c * (count - 1) + q].at[pl.ds(t * tile, tile)],
                    held.at[k % slots, q],
                    in_sem.at[k % slots, q],
                )
                for q in range(count - 1)
            ]

        def store(k):
            return pltpu.make_async_copy(
                out.at[k % 2], o_ref.at[pl.ds(start + k * tile, tile)], out_sem.at[k % 2]
            )

        for k in range(slots):
            for copy in fetch(k):
                copy.start()
        for k in range(len(tiles)):
            at = slice(start + k * tile, start + (k + 1) * tile)
            total = dot(u_ref[at, :], g_refs[0][...], NT)
            for copy in fetch(k):
                copy.wait()
            for q in range(1, count):
                total = total + dot(held[k % slots, q - 1], g_refs[q][...], NT)
            if k >= 2:
                store(k - 2).wait()
            out[k % 2] = total * scale
            store(k).start()
            if k + slots < len(tiles):
                for copy in fetch(k + slots):
                    copy.start()
        for k in range(max(len(tiles) - 2, 0), len(tiles)):
            store(k).wait()

    operands = [*flat, mapping, *grads, tops]
    in_specs = [ANY] * len(flat) + [VMEM] * (count + 2)
    aliases = {}
    if base is not None:
        in_specs.append(HBM)
        operands.append(base)
        aliases = {len(operands) - 1: 0}
    rows = len(tiles) * tile
    return pl.pallas_call(
        body,
        in_specs=in_specs,
        out_specs=HBM,
        out_shape=shape((cells, genes), f32),
        input_output_aliases=aliases,
        scratch_shapes=[
            pltpu.VMEM((slots, count - 1, tile, spots), bf16),
            pltpu.VMEM((2, tile, genes), f32),
            pltpu.SemaphoreType.DMA((slots, count - 1)),
            pltpu.SemaphoreType.DMA((2,)),
        ],
        compiler_params=params(),
        cost_estimate=cost(
            2 * rows * spots * count * genes, 2 * rows * spots * count + 4 * rows * genes
        ),
        name="grad_expression",
    )(*operands)


def per_device(n, m, logits, expression, target, keep_mask, slide_ids, slide_counts):
    cells, spots = logits.shape
    genes = expression.shape[1]
    block = genes // n
    slide_total = slide_counts.shape[0]
    levels = n.bit_length() - 1
    lead = levels - 3
    orders = [[1 << k for k in range(levels)] for _ in range(2)]
    orders[1][0], orders[1][1] = 2, 1
    me = lax.axis_index("cell")
    place = lax.axis_index("spot")
    core = place & 1

    def across(value, k):
        pairs = [
            (i * m + j, (i ^ orders[j & 1][k]) * m + j) for i in range(n) for j in range(m)
        ]
        return lax.ppermute(value, ("cell", "spot"), pairs)

    def over_spot(value, mask):
        return lax.ppermute(value, "spot", [(j, j ^ mask) for j in range(m)])

    def over_cell(value, cell_mask, spot_mask):
        pairs = [
            (i * m + j, (i ^ cell_mask) * m + (j ^ spot_mask)) for i in range(n) for j in range(m)
        ]
        return lax.ppermute(value, ("cell", "spot"), pairs)

    def sum_cell(value):
        for k in range(levels):
            value = value + across(value, k)
        return value

    def sum_spot(value, aside):
        other = over_spot(value, 1)
        mask = 2
        while mask < m:
            value = value + other
            if aside:
                other = over_cell(over_cell(value, 1, 0), 1, mask)
            else:
                other = over_spot(value, mask)
            mask *= 2
        return value, other

    def tie(value, others):
        return lax.optimization_barrier((value, *others))[0]

    keep_rows = keep_mask.reshape(cells // 128, 128)
    sizes = split_rows(cells)
    starts = [sum(sizes[:c]) for c in range(len(sizes))]
    pieces = [first_call(logits, keep_rows, sizes[0])]
    *rest, mapping, sums = exp_call(logits, keep_rows, sizes)
    pieces += rest
    gathered = []
    for piece in pieces:
        quarters = [None] * m
        for mask in range(0, m, 2):
            quarters[mask] = over_spot(piece, mask) if mask else piece
            quarters[mask + 1] = over_spot(quarters[mask], 1)
        gathered.append(quarters)

    def arrived(c):
        return [gathered[c][mask] for mask in range(2, m, 2)]

    tops = sum_cell(sums)

    def place_of(code):
        value = me
        for k in range(levels):
            if code[k]:
                value = value ^ jnp.where(core == 1, orders[1][k], orders[0][k])
        return value

    def codes(prefix):
        out = [prefix]
        while len(out[0]) < levels:
            out = [c + (b,) for c in out for b in (1, 0)]
        return out

    ids = jnp.stack([place_of(c) for c in codes(())])
    order = {c[lead:]: q for q, c in enumerate(codes((0,) * lead))}

    def products(first, second, adds, dtypes):
        return part_call(expression, mapping, ids, [order[first], order[second]], adds, dtypes)

    part, got, step = {}, {}, {}
    if lead or block % 128:
        have = dot(expression, mapping, TN).reshape(n, block, spots)
        have = jnp.take(have, ids, axis=0)
        for k in range(lead):
            half = have.shape[0] // 2
            have = have[half:] + across(have[:half].astype(bf16), k).astype(f32)
        for code, q in order.items():
            part[code] = have[q]
        for a in (1, 0):
            for b in (1, 0):
                got[1, a, b] = across(part[1, a, b].astype(bf16), lead)
        for b in (1, 0):
            part[0, 1, b] = add_call([part[0, 1, b], got[1, 1, b]])
            step[0, 1, b] = across(part[0, 1, b], lead + 1)
        adds = [part[0, 0, 0], got[1, 0, 0]]
    else:
        part[1, 1, 1], part[1, 0, 1] = products((1, 1, 1), (1, 0, 1), [], [bf16] * 2)
        got[1, 1, 1], got[1, 0, 1] = across(part[1, 1, 1], 0), across(part[1, 0, 1], 0)
        got[1, 1, 1] = tie(got[1, 1, 1], arrived(0))
        part[0, 1, 1], part[0, 0, 1] = products(
            (0, 1, 1), (0, 0, 1), [got[1, 1, 1]], [bf16, f32]
        )
        step[0, 1, 1] = across(part[0, 1, 1], 1)
        part[1, 1, 0], part[1, 0, 0] = products((1, 1, 0), (1, 0, 0), [], [bf16] * 2)
        got[1, 1, 0], got[1, 0, 0] = across(part[1, 1, 0], 0), across(part[1, 0, 0], 0)
        part[0, 1, 0], part[0, 0, 0] = products(
            (0, 1, 0), (0, 0, 0), [got[1, 1, 0], got[1, 0, 0]], [bf16, f32]
        )
        step[0, 1, 0] = across(part[0, 1, 0], 1)
        adds = [part[0, 0, 0]]
    last = add_call([part[0, 0, 1], got[1, 0, 1], step[0, 1, 1]])
    last = across(last, lead + 2)

    slides = jnp.arange(slide_total, dtype=jnp.int32)
    member = (slide_ids[None, :] == slides[:, None]).astype(f32)
    density, far_density = sum_spot(density_call(mapping, tops, member), True)
    last = tie(last, [*arrived(1), density])
    predicted, gene_sums = predicted_call(
        [*adds, step[0, 1, 0], last], tops, target, member
    )
    gene_sums, far_sums = sum_spot(gene_sums, True)
    far_sums = tie(far_sums, arrived(2))
    grad, ends = grad_call(gene_sums, far_sums, predicted, target, tops, member)

    slope, weight, more = diverge_call(
        density,
        far_density,
        keep_mask[None, :],
        slide_counts[None, :],
        mapping,
        tops,
        member,
    )
    ends = sum_cell(ends + more)
    mapping_loss = (-ends[1, 0] + density_weight * ends[2, 0]) / (slide_total * genes)

    have = {(0, 0, 0): grad}
    for k in (2, 1, 0):
        for code in list(have):
            other = tuple(1 if q == k else b for q, b in enumerate(code))
            source = tie(have[code], [slope]) if (k, code) == (0, (0, 1, 1)) else have[code]
            have[other] = across(source, lead + k)
    tail = codes((0,) * lead)
    blocks = [have[c[lead:]] for c in tail]
    if lead:
        blocks = jnp.stack(blocks)
        for k in reversed(range(lead)):
            blocks = jnp.concatenate([across(blocks, k), blocks])
        blocks = [blocks[q] for q in range(n)]

    grad_logits = logit_call(
        expression, blocks, ids, mapping, slope, weight, tie(ends, arrived(3)), tops
    )

    parts = regroup_call(blocks, ids, place[None], m)
    regrouped = [None] * m
    for mask in range(0, m, 2):
        regrouped[mask] = over_spot(parts[mask], mask) if mask else parts[0]
        beside = over_spot(parts[mask + 1], mask) if mask else parts[1]
        regrouped[mask + 1] = over_spot(beside, 1)
    chunks = [quarters[1:] for quarters in gathered]
    grad_expression = expr_call(None, mapping, chunks[:-1], regrouped, tops, 0)
    grad_expression = expr_call(
        grad_expression, mapping, chunks[-1:], regrouped, tops, starts[-1]
    )
    return (mapping_loss, predicted, grad_logits, grad_expression)


def solution(mesh):
    in_specs = (P("cell", "spot"), P("cell", None), P("cell", "spot"), P("cell"), P("spot"), P())
    out_specs = (P(), P("cell", "spot"), P("cell", "spot"), P("cell", "spot"))
    body = functools.partial(per_device, mesh.shape["cell"], mesh.shape["spot"])
    return jax.shard_map(
        body, mesh=mesh, in_specs=in_specs, out_specs=out_specs, check_vma=False
    )
```

time: 218 us -> 183 us (0.84)
  Pallas kernels: 97.7 us -> 59 us
  waiting for transfers between devices: 70.9 us -> 77.5 us
  starting transfers between devices: 31.7 us -> 36.4 us
  other arithmetic: 3.61 us -> 0.06 us
  local copies, waits for them, and re-layouts: 10.1 us -> 6.61 us
    pallas_call x12, Pallas kernels: 90.6 us -> 56.9 us  [the longest x4 19.1 us: part_call(): pl.pallas_call(body, in_specs=[SMEM, HBM, VMEM] + [VMEM] * len(adds), out...]
    ppermute x20, waiting for transfers between devices: 32.3 us -> 38.8 us  [across(): return lax.ppermute(value, ('cell', 'spot'), pairs)]
    ppermute x2 -> x4, waiting for transfers between devices: 7.4 us -> 11.6 us  [over_cell(): return lax.ppermute(value, ('cell', 'spot'), pairs)]
    ppermute x21, waiting for transfers between devices: 31.2 us -> 27.1 us  [over_spot(): return lax.ppermute(value, 'spot', [(j, j ^ mask) for j in range(m)])]
    ppermute x20, starting transfers between devices: 20.6 us -> 22.8 us  [across(): return lax.ppermute(value, ('cell', 'spot'), pairs)]
    unnamed x74 -> x34, local copies, waits for them, and re-layouts: 6.21 us -> 6.01 us
  transfers between devices with their start and end apart: 43 -> 45, of which waited for: 16 -> 19; matrix products, arithmetic and copies ran while one was open for 3% -> 0% of each run, Pallas kernels for 42% -> 30%
where the time goes in v2:
time: 183 us
  waiting for transfers between devices  77.5 us (42%)
  Pallas kernels  59 us (32%)
  starting transfers between devices  36.4 us (20%)
  local copies, waits for them, and re-layouts  6.61 us (4%)
  between operations  3.41 us (2%)
    ppermute x20, waiting for transfers between devices, across(): return lax.ppermute(value, ('cell', 'spot'), pairs)  38.8 us
    ppermute x21, waiting for transfers between devices, over_spot(): return lax.ppermute(value, 'spot', [(j, j ^ mask) for j in range(m)])  27.1 us
    ppermute x20, starting transfers between devices, across(): return lax.ppermute(value, ('cell', 'spot'), pairs)  22.8 us
    pallas_call x4, Pallas kernels, part_call(): pl.pallas_call(body, in_specs=[SMEM, HBM, VMEM] + [VMEM] * len(adds), out...  19.1 us
    pallas_call x2, Pallas kernels, expr_call(): pl.pallas_call(body, in_specs=in_specs, out_specs=HBM, out_shape=shape((c...  14.1 us
    pallas_call x1, Pallas kernels, logit_call(): pl.pallas_call(body, grid=(cells // tile,), in_specs=[SMEM, VMEM, VMEM, p...  13.4 us
    ppermute x4, waiting for transfers between devices, over_cell(): return lax.ppermute(value, ('cell', 'spot'), pairs)  11.6 us
    ppermute x21, starting transfers between devices, over_spot(): return lax.ppermute(value, 'spot', [(j, j ^ mask) for j in range(m)])  10.2 us
  transfers between devices with their start and end apart: 45, of which 19 were waited for; matrix products, arithmetic and copies ran while one was open for 0% of the time, Pallas kernels for 30%

profile of v2, /device:TPU:0, one launch (start us, length us, event | category | flops | bytes accessed | tf_op | source)
XLA Modules:
  0.0 182.9 jit_solution(14732800328128402920)
XLA Ops:
  2.8 3.0 %collective-permute-start.4 = (bf16[512,512]{1,0:T(8,128)(2,1)S(1)}, bf16[512,512]{1,0:T(8,128)(2,1)S(1)}, u32[]{:S(2)}, u32[]{:S(2)}) collective-permute-start(bf16[512,512]{1,0:T(8,128)(2,1)S(1)} %exp_first.1), channel_id=1, source_target_pairs={{0,2},{1,3},{2,0},{3,1},{4,6},{5,7},{6,4},{7,5},{8,10},{9,11},{10,... | collective-permute-start | bytes 1572872 | tf_op jit(solution)/shard_map/ppermute | solution.py:536
  5.8 5.3 %exp_rows.1 = (bf16[1024,512]{1,0:T(8,128)(2,1)}, bf16[1024,512]{1,0:T(8,128)(2,1)}, bf16[1024,512]{1,0:T(8,128)(2,1)}, bf16[512,512]{1,0:T(8,128)(2,1)}, bf16[4...) custom-call(f32[4096,512]{1,0:T(8,128)} %x_ref.3, s32[32,128]{1,0:T(8,128)S(1)} %bitcast.16), custom_call_target="tpu_custom_call" | custom-call | bytes 16777216 | tf_op jit(solution)/shard_map/exp_rows/pallas_call | solution.py:136
  11.1 2.0 %copy-done = bf16[4096,512]{1,0:T(8,128)(2,1)} copy-done((bf16[4096,512]{1,0:T(8,128)(2,1)}, bf16[4096,512]{1,0:T(8,128)(2,1)S(1)}, u32[]{:S(2)}) %copy-start) | copy-done | bytes 4194328
  13.2 2.2 %copy-done.1 = bf16[4096,512]{1,0:T(8,128)(2,1)S(1)} copy-done((bf16[4096,512]{1,0:T(8,128)(2,1)S(1)}, bf16[4096,512]{1,0:T(8,128)(2,1)}, u32[]{:S(2)}) %copy-start.1) | copy-done | bytes 4194328
  15.4 4.7 %part.6 = (bf16[256,512]{1,0:T(8,128)(2,1)S(1)}, bf16[256,512]{1,0:T(8,128)(2,1)S(1)}) custom-call(s32[8]{0:T(128)S(1)} %stack.35.ids_ref, bf16[4096,2048]{1,0:T(8,128)(2,1)} %e_ref.9, bf16[4096,512]{1,0:T(8,128)(2,1)S(1)} %copy-done.1), custom_call_target="tpu_custom_call" | custom-call | flops 2147483648 | bytes 8388608 | tf_op jit(solution)/shard_map/part/pallas_call | solution.py:173
  22.2 4.7 %collective-permute-done.9 = f32[16,512]{1,0:T(8,128)S(1)} collective-permute-done((f32[16,512]{1,0:T(8,128)S(1)}, f32[16,512]{1,0:T(8,128)S(1)}, u32[]{:S(2)}, u32[]{:S(2)}) %collective-permute-start.9) | collective-permute-done | bytes 32800 | tf_op jit(solution)/shard_map/ppermute | solution.py:533
  31.2 2.6 %collective-permute-start.11 = (f32[16,512]{1,0:T(8,128)S(1)}, f32[16,512]{1,0:T(8,128)S(1)}, u32[]{:S(2)}, u32[]{:S(2)}) collective-permute-start(f32[16,512]{1,0:T(8,128)S(1)} %add.32), channel_id=1, source_target_pairs={{0,16},{1,17},{2,18},{3,19},{4,20},{5,21},{6,22},{7,23},{8,24},{9,... | collective-permute-start | bytes 98312 | tf_op jit(solution)/shard_map/ppermute | solution.py:533
  33.8 4.7 %part.7 = (bf16[256,512]{1,0:T(8,128)(2,1)S(1)}, f32[256,512]{1,0:T(8,128)S(1)}) custom-call(s32[8]{0:T(128)S(1)} %stack.35.ids_ref, bf16[4096,2048]{1,0:T(8,128)(2,1)} %e_ref.9, bf16[4096,512]{1,0:T(8,128)(2,1)S(1)} %copy-done.1, bf16[256,512]{1,0:T(8,128)(2,1)S(1)} %collective-permute-done.3.refs_0_), custom_call_target="tpu_custom_call" | custom-call | flops 2147483648 | bytes 8388608 | tf_op jit(solution)/shard_map/part/pallas_call | solution.py:173
  38.5 1.6 collective-permute-start.6
  40.2 4.7 %part.4 = (bf16[256,512]{1,0:T(8,128)(2,1)S(1)}, bf16[256,512]{1,0:T(8,128)(2,1)S(1)}) custom-call(s32[8]{0:T(128)S(1)} %stack.35.ids_ref, bf16[4096,2048]{1,0:T(8,128)(2,1)} %e_ref.9, bf16[4096,512]{1,0:T(8,128)(2,1)S(1)} %copy-done.1), custom_call_target="tpu_custom_call" | custom-call | flops 2147483648 | bytes 8388608 | tf_op jit(solution)/shard_map/part/pallas_call | solution.py:173
  44.9 1.6 collective-permute-start
  52.2 2.0 %collective-permute-done.1.refs_1_ = bf16[256,512]{1,0:T(8,128)(2,1)S(1)} collective-permute-done((bf16[256,512]{1,0:T(8,128)(2,1)S(1)}, bf16[256,512]{1,0:T(8,128)(2,1)S(1)}, u32[]{:S(2)}, u32[]{:S(2)}) %collective-permute-start.1) | collective-permute-done | bytes 262176 | tf_op jit(solution)/shard_map/ppermute | solution.py:533
  54.2 5.0 %part.5 = (bf16[256,512]{1,0:T(8,128)(2,1)S(1)}, f32[256,512]{1,0:T(8,128)S(1)}) custom-call(s32[8]{0:T(128)S(1)} %stack.35.ids_ref, bf16[4096,2048]{1,0:T(8,128)(2,1)} %e_ref.9, bf16[4096,512]{1,0:T(8,128)(2,1)S(1)} %copy-done.2, bf16[256,512]{1,0:T(8,128)(2,1)S(1)} %collective-permute-done.refs_0_, bf16[256,512]{1,0:T(8,128)(2,1)S(1)} %collective-permute-done.1.refs_1_), custom_call_target="tpu_custom_call" | custom-call | flops 2147483648 | bytes 8388608 | tf_op jit(solution)/shard_map/part/pallas_call | solution.py:173
  59.1 6.0 %collective-permute-done.7.refs_2_ = bf16[256,512]{1,0:T(8,128)(2,1)S(1)} collective-permute-done((bf16[256,512]{1,0:T(8,128)(2,1)S(1)}, bf16[256,512]{1,0:T(8,128)(2,1)S(1)}, u32[]{:S(2)}, u32[]{:S(2)}) %collective-permute-start.7) | collective-permute-done | bytes 262176 | tf_op jit(solution)/shard_map/ppermute | solution.py:533
  66.7 4.8 %collective-permute-done.2.refs_1_ = bf16[256,512]{1,0:T(8,128)(2,1)S(1)} collective-permute-done((bf16[256,512]{1,0:T(8,128)(2,1)S(1)}, bf16[256,512]{1,0:T(8,128)(2,1)S(1)}, u32[]{:S(2)}, u32[]{:S(2)}) %collective-permute-start.2) | collective-permute-done | bytes 262176 | tf_op jit(solution)/shard_map/ppermute | solution.py:533
  75.3 3.3 %collective-permute-done.16.refs_7_ = bf16[1024,512]{1,0:T(8,128)(2,1)S(1)} collective-permute-done((bf16[1024,512]{1,0:T(8,128)(2,1)S(1)}, bf16[1024,512]{1,0:T(8,128)(2,1)S(1)}, u32[]{:S(2)}, u32[]{:S(2)}) %collective-permute-start.16) | collective-permute-done | bytes 1048608 | tf_op jit(solution)/shard_map/ppermute | solution.py:536
  79.1 3.3 %collective-permute-done.14 = f32[24,256]{1,0:T(8,128)S(1)} collective-permute-done((f32[24,256]{1,0:T(8,128)S(1)}, f32[24,256]{1,0:T(8,128)S(1)}, u32[]{:S(2)}, u32[]{:S(2)}) %collective-permute-start.14) | collective-permute-done | bytes 24608 | tf_op jit(solution)/shard_map/ppermute | solution.py:542
  82.8 4.3 %collective-permute-done.15.f_ref = f32[24,256]{1,0:T(8,128)S(1)} collective-permute-done((f32[24,256]{1,0:T(8,128)S(1)}, f32[24,256]{1,0:T(8,128)S(1)}, u32[]{:S(2)}, u32[]{:S(2)}) %collective-permute-start.15) | collective-permute-done | bytes 24608 | tf_op jit(solution)/shard_map/ppermute | solution.py:542
  89.7 4.0 %collective-permute-done.18.f_ref = f32[8,4096]{1,0:T(8,128)S(1)} collective-permute-done((f32[8,4096]{1,0:T(8,128)S(1)}, f32[8,4096]{1,0:T(8,128)S(1)}, u32[]{:S(2)}, u32[]{:S(2)}) %collective-permute-start.18) | collective-permute-done | bytes 131104 | tf_op jit(solution)/shard_map/ppermute | solution.py:542
  93.7 2.6 %collective-permute-start.23 = (bf16[256,512]{1,0:T(8,128)(2,1)S(1)}, bf16[256,512]{1,0:T(8,128)(2,1)S(1)}, u32[]{:S(2)}, u32[]{:S(2)}) collective-permute-start(bf16[256,512]{1,0:T(8,128)(2,1)S(1)} %get-tuple-element.57.refs_7_), channel_id=1, source_target_pairs={{0,16},{1,17},{2,18},{3,19},{4,20},{5,21},{6,22},{7,23},{8,24},{9,... | collective-permute-start | bytes 786440 | tf_op jit(solution)/shard_map/ppermute | solution.py:533
  96.3 16.4 %collective-permute-done.31.refs_1_ = bf16[512,512]{1,0:T(8,128)(2,1)S(1)} collective-permute-done((bf16[512,512]{1,0:T(8,128)(2,1)S(1)}, bf16[512,512]{1,0:T(8,128)(2,1)S(1)}, u32[]{:S(2)}, u32[]{:S(2)}) %collective-permute-start.31) | collective-permute-done | bytes 524320 | tf_op jit(solution)/shard_map/ppermute | solution.py:536
  116.3 3.0 %collective-permute-done.19 = f32[8,512]{1,0:T(8,128)S(1)} collective-permute-done((f32[8,512]{1,0:T(8,128)S(1)}, f32[8,512]{1,0:T(8,128)S(1)}, u32[]{:S(2)}, u32[]{:S(2)}) %collective-permute-start.19) | collective-permute-done | bytes 16416 | tf_op jit(solution)/shard_map/ppermute | solution.py:533
  120.5 7.9 %collective-permute-done.24.refs_4_ = bf16[256,512]{1,0:T(8,128)(2,1)S(1)} collective-permute-done((bf16[256,512]{1,0:T(8,128)(2,1)S(1)}, bf16[256,512]{1,0:T(8,128)(2,1)S(1)}, u32[]{:S(2)}, u32[]{:S(2)}) %collective-permute-start.24) | collective-permute-done | bytes 262176 | tf_op jit(solution)/shard_map/ppermute | solution.py:533
  128.7 1.7 collective-permute-start.25
  130.4 4.3 %collective-permute-done.28.refs_2_ = bf16[256,512]{1,0:T(8,128)(2,1)S(1)} collective-permute-done((bf16[256,512]{1,0:T(8,128)(2,1)S(1)}, bf16[256,512]{1,0:T(8,128)(2,1)S(1)}, u32[]{:S(2)}, u32[]{:S(2)}) %collective-permute-start.28) | collective-permute-done | bytes 262176 | tf_op jit(solution)/shard_map/ppermute | solution.py:533
  135.2 2.5 %collective-permute-done.25.refs_0_ = bf16[256,512]{1,0:T(8,128)(2,1)S(1)} collective-permute-done((bf16[256,512]{1,0:T(8,128)(2,1)S(1)}, bf16[256,512]{1,0:T(8,128)(2,1)S(1)}, u32[]{:S(2)}, u32[]{:S(2)}) %collective-permute-start.25) | collective-permute-done | bytes 262176 | tf_op jit(solution)/shard_map/ppermute | solution.py:533
  139.3 2.7 %collective-permute-start.21 = (f32[8,512]{1,0:T(8,128)S(1)}, f32[8,512]{1,0:T(8,128)S(1)}, u32[]{:S(2)}, u32[]{:S(2)}) collective-permute-start(f32[8,512]{1,0:T(8,128)S(1)} %add.38), channel_id=1, source_target_pairs={{0,16},{1,17},{2,18},{3,19},{4,20},{5,21},{6,22},{7,23},{8,24},{9,... | collective-permute-start | bytes 49160 | tf_op jit(solution)/shard_map/ppermute | solution.py:533
  142.0 2.1 %collective-permute-done.21 = f32[8,512]{1,0:T(8,128)S(1)} collective-permute-done((f32[8,512]{1,0:T(8,128)S(1)}, f32[8,512]{1,0:T(8,128)S(1)}, u32[]{:S(2)}, u32[]{:S(2)}) %collective-permute-start.21) | collective-permute-done | bytes 16416 | tf_op jit(solution)/shard_map/ppermute | solution.py:533
  148.0 5.5 %collective-permute-done.35 = bf16[512,512]{1,0:T(8,128)(2,1)S(1)} collective-permute-done((bf16[512,512]{1,0:T(8,128)(2,1)S(1)}, bf16[512,512]{1,0:T(8,128)(2,1)S(1)}, u32[]{:S(2)}, u32[]{:S(2)}) %collective-permute-start.35) | collective-permute-done | bytes 524320 | tf_op jit(solution)/shard_map/ppermute | solution.py:536
  153.6 13.4 %grad_logits.1 = f32[4096,512]{1,0:T(8,128)} custom-call(s32[8]{0:T(128)S(1)} %stack.35.ids_ref, bf16[4096,2048]{1,0:T(8,128)(2,1)S(1)} %bitcast.14, bf16[4096,512]{1,0:T(8,128)(2,1)S(1)} %copy-done.2, bf16[32,4096]{1,0:T(8,128)(2,1)S(1)} %get-tuple-element.53.d_ref, bf16[32,512]{1,0:T(8,128)(2,1)S(1)} %get-tuple-element.54.w_ref, ...), custom_call_target="tpu_custom_call" | custom-call | flops 8589934592 | bytes 29360128 | tf_op jit(solution)/shard_map/grad_logits/pallas_call | solution.py:420
  167.6 11.6 %grad_expression.2.refs_9_ = f32[4096,512]{1,0:T(8,128)} custom-call(bf16[512,512]{1,0:T(8,128)(2,1)S(1)} %collective-permute-done.37.refs_0_, bf16[512,512]{1,0:T(8,128)(2,1)S(1)} %collective-permute-done.4.refs_1_, bf16[512,512]{1,0:T(8,128)(2,1)S(1)} %collective-permute-done.38.refs_2_, bf16[1024,512]{1,0:T(8,128)(2,1)S(1)} %collective-permute-done.39.refs_3_, ...), custom_call_target="tpu_custom_call" | custom-call | flops 7516192768 | bytes 22020096 | tf_op jit(solution)/shard_map/grad_expression/pallas_call | solution.py:496
  179.3 2.5 %grad_expression.3 = f32[4096,512]{1,0:T(8,128)} custom-call(bf16[512,512]{1,0:T(8,128)(2,1)S(1)} %collective-permute-done.30.refs_0_, bf16[512,512]{1,0:T(8,128)(2,1)S(1)} %collective-permute-done.31.refs_1_, bf16[512,512]{1,0:T(8,128)(2,1)S(1)} %collective-permute-done.32.refs_2_, bf16[4096,512]{1,0:T(8,128)(2,1)S(1)} %copy-done.2, ...), custom_call_target="tpu_custom_call", output_to_operand_aliasing={{}: (9, {})} | custom-call | flops 1073741824 | bytes 3145728 | tf_op jit(solution)/shard_map/grad_expression/pallas_call | solution.py:496
  (120 shorter events, 33.6 us)
Async XLA Ops:
  2.8 31.0 %collective-permute-start.4 = (bf16[512,512]{1,0:T(8,128)(2,1)S(1)}, bf16[512,512]{1,0:T(8,128)(2,1)S(1)}, u32[]{:S(2)}, u32[]{:S(2)}) collective-permute-start(bf16[512,512]{1,0:T(8,128)(2,1)S(1)} %exp_first.1), channel_id=1, source_target_pairs={{0,2},{1,3},{2,0},{3,1},{4,6},{5,7},{6,4},{7,5},{8,10},{9,11},{10,... | collective-permute-start | bytes 1572872 | tf_op jit(solution)/shard_map/ppermute | solution.py:536
  20.1 13.7 %collective-permute-start.3 = (bf16[256,512]{1,0:T(8,128)(2,1)S(1)}, bf16[256,512]{1,0:T(8,128)(2,1)S(1)}, u32[]{:S(2)}, u32[]{:S(2)}) collective-permute-start(bf16[256,512]{1,0:T(8,128)(2,1)S(1)} %get-tuple-element.39), channel_id=1, source_target_pairs={{0,4},{1,9},{2,6},{3,11},{4,0},{5,13},{6,2},{7,15},{8,12},{9,1},{1... | collective-permute-start | bytes 786440 | tf_op jit(solution)/shard_map/ppermute | solution.py:533
  28.5 18.5 %collective-permute-start.5 = (bf16[256,512]{1,0:T(8,128)(2,1)S(1)}, bf16[256,512]{1,0:T(8,128)(2,1)S(1)}, u32[]{:S(2)}, u32[]{:S(2)}) collective-permute-start(bf16[256,512]{1,0:T(8,128)(2,1)S(1)} %get-tuple-element.42), channel_id=1, source_target_pairs={{0,4},{1,9},{2,6},{3,11},{4,0},{5,13},{6,2},{7,15},{8,12},{9,1},{1... | collective-permute-start | bytes 786440 | tf_op jit(solution)/shard_map/ppermute | solution.py:533
  30.0 35.2 %collective-permute-start.8 = (bf16[1024,512]{1,0:T(8,128)(2,1)S(1)}, bf16[1024,512]{1,0:T(8,128)(2,1)S(1)}, u32[]{:S(2)}, u32[]{:S(2)}) collective-permute-start(bf16[1024,512]{1,0:T(8,128)(2,1)S(1)} %copy-done.11), channel_id=1, source_target_pairs={{0,2},{1,3},{2,0},{3,1},{4,6},{5,7},{6,4},{7,5},{8,10},{9,11},{10,... | collective-permute-start | bytes 3145736 | tf_op jit(solution)/shard_map/ppermute | solution.py:536
  31.2 15.3 %collective-permute-start.11 = (f32[16,512]{1,0:T(8,128)S(1)}, f32[16,512]{1,0:T(8,128)S(1)}, u32[]{:S(2)}, u32[]{:S(2)}) collective-permute-start(f32[16,512]{1,0:T(8,128)S(1)} %add.32), channel_id=1, source_target_pairs={{0,16},{1,17},{2,18},{3,19},{4,20},{5,21},{6,22},{7,23},{8,24},{9,... | collective-permute-start | bytes 98312 | tf_op jit(solution)/shard_map/ppermute | solution.py:533
  38.5 10.3 %collective-permute-start.6 = (bf16[256,512]{1,0:T(8,128)(2,1)S(1)}, bf16[256,512]{1,0:T(8,128)(2,1)S(1)}, u32[]{:S(2)}, u32[]{:S(2)}) collective-permute-start(bf16[256,512]{1,0:T(8,128)(2,1)S(1)} %get-tuple-element.43), channel_id=1, source_target_pairs={{0,8},{1,5},{2,10},{3,7},{4,12},{5,1},{6,14},{7,3},{8,0},{9,13},{1... | collective-permute-start | bytes 786440 | tf_op jit(solution)/shard_map/ppermute | solution.py:533
  46.5 7.6 %collective-permute-start.1 = (bf16[256,512]{1,0:T(8,128)(2,1)S(1)}, bf16[256,512]{1,0:T(8,128)(2,1)S(1)}, u32[]{:S(2)}, u32[]{:S(2)}) collective-permute-start(bf16[256,512]{1,0:T(8,128)(2,1)S(1)} %get-tuple-element.36), channel_id=1, source_target_pairs={{0,4},{1,9},{2,6},{3,11},{4,0},{5,13},{6,2},{7,15},{8,12},{9,1},{1... | collective-permute-start | bytes 786440 | tf_op jit(solution)/shard_map/ppermute | solution.py:533
  47.0 31.6 %collective-permute-start.16 = (bf16[1024,512]{1,0:T(8,128)(2,1)S(1)}, bf16[1024,512]{1,0:T(8,128)(2,1)S(1)}, u32[]{:S(2)}, u32[]{:S(2)}) collective-permute-start(bf16[1024,512]{1,0:T(8,128)(2,1)S(1)} %copy-done.10), channel_id=1, source_target_pairs={{0,2},{1,3},{2,0},{3,1},{4,6},{5,7},{6,4},{7,5},{8,10},{9,11},{10,... | collective-permute-start | bytes 3145736 | tf_op jit(solution)/shard_map/ppermute | solution.py:536
  50.2 14.9 %collective-permute-start.7 = (bf16[256,512]{1,0:T(8,128)(2,1)S(1)}, bf16[256,512]{1,0:T(8,128)(2,1)S(1)}, u32[]{:S(2)}, u32[]{:S(2)}) collective-permute-start(bf16[256,512]{1,0:T(8,128)(2,1)S(1)} %add_blocks.1), channel_id=1, source_target_pairs={{0,16},{1,17},{2,18},{3,19},{4,20},{5,21},{6,22},{7,23},{8,24},{9,... | collective-permute-start | bytes 786440 | tf_op jit(solution)/shard_map/ppermute | solution.py:533
  51.3 63.3 %collective-permute-start.22 = (bf16[1024,512]{1,0:T(8,128)(2,1)S(1)}, bf16[1024,512]{1,0:T(8,128)(2,1)S(1)}, u32[]{:S(2)}, u32[]{:S(2)}) collective-permute-start(bf16[1024,512]{1,0:T(8,128)(2,1)S(1)} %copy-done.9), channel_id=1, source_target_pairs={{0,2},{1,3},{2,0},{3,1},{4,6},{5,7},{6,4},{7,5},{8,10},{9,11},{10,... | collective-permute-start | bytes 3145736 | tf_op jit(solution)/shard_map/ppermute | solution.py:536
  54.1 62.1 %collective-permute-start.39 = (bf16[1024,512]{1,0:T(8,128)(2,1)S(1)}, bf16[1024,512]{1,0:T(8,128)(2,1)S(1)}, u32[]{:S(2)}, u32[]{:S(2)}) collective-permute-start(bf16[1024,512]{1,0:T(8,128)(2,1)S(1)} %copy-done.11), channel_id=1, source_target_pairs={{0,1},{1,0},{2,3},{3,2},{4,5},{5,4},{6,7},{7,6},{8,9},{9,8},{10,11... | collective-permute-start | bytes 3145736 | tf_op jit(solution)/shard_map/ppermute | solution.py:536
  65.1 7.4 %collective-permute-start.17 = (f32[8,4096]{1,0:T(8,128)S(1)}, f32[8,4096]{1,0:T(8,128)S(1)}, u32[]{:S(2)}, u32[]{:S(2)}) collective-permute-start(f32[8,4096]{1,0:T(8,128)S(1)} %add.34.d_ref), channel_id=1, source_target_pairs={{0,4},{1,5},{2,6},{3,7},{4,0},{5,1},{6,2},{7,3},{8,12},{9,13},{10,... | collective-permute-start | bytes 393224 | tf_op jit(solution)/shard_map/ppermute | solution.py:542
  72.6 23.7 %collective-permute-start.37 = (bf16[512,512]{1,0:T(8,128)(2,1)S(1)}, bf16[512,512]{1,0:T(8,128)(2,1)S(1)}, u32[]{:S(2)}, u32[]{:S(2)}) collective-permute-start(bf16[512,512]{1,0:T(8,128)(2,1)S(1)} %exp_first.1), channel_id=1, source_target_pairs={{0,1},{1,0},{2,3},{3,2},{4,5},{5,4},{6,7},{7,6},{8,9},{9,8},{10,11... | collective-permute-start | bytes 1572872 | tf_op jit(solution)/shard_map/ppermute | solution.py:536
  73.8 38.9 %collective-permute-start.31 = (bf16[512,512]{1,0:T(8,128)(2,1)S(1)}, bf16[512,512]{1,0:T(8,128)(2,1)S(1)}, u32[]{:S(2)}, u32[]{:S(2)}) collective-permute-start(bf16[512,512]{1,0:T(8,128)(2,1)S(1)} %copy-done.12), channel_id=1, source_target_pairs={{0,2},{1,3},{2,0},{3,1},{4,6},{5,7},{6,4},{7,5},{8,10},{9,11},{10,... | collective-permute-start | bytes 1572872 | tf_op jit(solution)/shard_map/ppermute | solution.py:536
  93.7 25.5 %collective-permute-start.23 = (bf16[256,512]{1,0:T(8,128)(2,1)S(1)}, bf16[256,512]{1,0:T(8,128)(2,1)S(1)}, u32[]{:S(2)}, u32[]{:S(2)}) collective-permute-start(bf16[256,512]{1,0:T(8,128)(2,1)S(1)} %get-tuple-element.57.refs_7_), channel_id=1, source_target_pairs={{0,16},{1,17},{2,18},{3,19},{4,20},{5,21},{6,22},{7,23},{8,24},{9,... | collective-permute-start | bytes 786440 | tf_op jit(solution)/shard_map/ppermute | solution.py:533
  96.3 23.4 %collective-permute-start.26 = (bf16[256,512]{1,0:T(8,128)(2,1)S(1)}, bf16[256,512]{1,0:T(8,128)(2,1)S(1)}, u32[]{:S(2)}, u32[]{:S(2)}) collective-permute-start(bf16[256,512]{1,0:T(8,128)(2,1)S(1)} %get-tuple-element.57.refs_7_), channel_id=1, source_target_pairs={{0,8},{1,5},{2,10},{3,7},{4,12},{5,1},{6,14},{7,3},{8,0},{9,13},{1... | collective-permute-start | bytes 786440 | tf_op jit(solution)/shard_map/ppermute | solution.py:533
  112.7 7.8 %collective-permute-start.29 = (bf16[256,512]{1,0:T(8,128)(2,1)S(1)}, bf16[256,512]{1,0:T(8,128)(2,1)S(1)}, u32[]{:S(2)}, u32[]{:S(2)}) collective-permute-start(bf16[256,512]{1,0:T(8,128)(2,1)S(1)} %get-tuple-element.57.refs_7_), channel_id=1, source_target_pairs={{0,4},{1,9},{2,6},{3,11},{4,0},{5,13},{6,2},{7,15},{8,12},{9,1},{1... | collective-permute-start | bytes 786440 | tf_op jit(solution)/shard_map/ppermute | solution.py:533
  116.3 23.1 %collective-permute-start.41 = (bf16[1024,512]{1,0:T(8,128)(2,1)S(1)}, bf16[1024,512]{1,0:T(8,128)(2,1)S(1)}, u32[]{:S(2)}, u32[]{:S(2)}) collective-permute-start(bf16[1024,512]{1,0:T(8,128)(2,1)S(1)} %copy-done.10), channel_id=1, source_target_pairs={{0,1},{1,0},{2,3},{3,2},{4,5},{5,4},{6,7},{7,6},{8,9},{9,8},{10,11... | collective-permute-start | bytes 3145736 | tf_op jit(solution)/shard_map/ppermute | solution.py:536
  119.2 22.8 %collective-permute-start.43 = (bf16[1024,512]{1,0:T(8,128)(2,1)S(1)}, bf16[1024,512]{1,0:T(8,128)(2,1)S(1)}, u32[]{:S(2)}, u32[]{:S(2)}) collective-permute-start(bf16[1024,512]{1,0:T(8,128)(2,1)S(1)} %copy-done.9), channel_id=1, source_target_pairs={{0,1},{1,0},{2,3},{3,2},{4,5},{5,4},{6,7},{7,6},{8,9},{9,8},{10,11... | collective-permute-start | bytes 3145736 | tf_op jit(solution)/shard_map/ppermute | solution.py:536
  119.2 9.2 %collective-permute-start.24 = (bf16[256,512]{1,0:T(8,128)(2,1)S(1)}, bf16[256,512]{1,0:T(8,128)(2,1)S(1)}, u32[]{:S(2)}, u32[]{:S(2)}) collective-permute-start(bf16[256,512]{1,0:T(8,128)(2,1)S(1)} %collective-permute-done.23.refs_6_), channel_id=1, source_target_pairs={{0,8},{1,5},{2,10},{3,7},{4,12},{5,1},{6,14},{7,3},{8,0},{9,13},{1... | collective-permute-start | bytes 786440 | tf_op jit(solution)/shard_map/ppermute | solution.py:533
  119.7 9.0 %collective-permute-start.27 = (bf16[256,512]{1,0:T(8,128)(2,1)S(1)}, bf16[256,512]{1,0:T(8,128)(2,1)S(1)}, u32[]{:S(2)}, u32[]{:S(2)}) collective-permute-start(bf16[256,512]{1,0:T(8,128)(2,1)S(1)} %collective-permute-done.26.refs_5_), channel_id=1, source_target_pairs={{0,4},{1,9},{2,6},{3,11},{4,0},{5,13},{6,2},{7,15},{8,12},{9,1},{1... | collective-permute-start | bytes 786440 | tf_op jit(solution)/shard_map/ppermute | solution.py:533
  120.5 26.1 %collective-permute-start.40 = (bf16[1024,512]{1,0:T(8,128)(2,1)S(1)}, bf16[1024,512]{1,0:T(8,128)(2,1)S(1)}, u32[]{:S(2)}, u32[]{:S(2)}) collective-permute-start(bf16[1024,512]{1,0:T(8,128)(2,1)S(1)} %collective-permute-done.8.refs_4_), channel_id=1, source_target_pairs={{0,1},{1,0},{2,3},{3,2},{4,5},{5,4},{6,7},{7,6},{8,9},{9,8},{10,11... | collective-permute-start | bytes 3145736 | tf_op jit(solution)/shard_map/ppermute | solution.py:536
  128.7 9.0 %collective-permute-start.25 = (bf16[256,512]{1,0:T(8,128)(2,1)S(1)}, bf16[256,512]{1,0:T(8,128)(2,1)S(1)}, u32[]{:S(2)}, u32[]{:S(2)}) collective-permute-start(bf16[256,512]{1,0:T(8,128)(2,1)S(1)} %collective-permute-done.24.refs_4_), channel_id=1, source_target_pairs={{0,4},{1,9},{2,6},{3,11},{4,0},{5,13},{6,2},{7,15},{8,12},{9,1},{1... | collective-permute-start | bytes 786440 | tf_op jit(solution)/shard_map/ppermute | solution.py:533
  137.8 8.2 %collective-permute-start.38 = (bf16[512,512]{1,0:T(8,128)(2,1)S(1)}, bf16[512,512]{1,0:T(8,128)(2,1)S(1)}, u32[]{:S(2)}, u32[]{:S(2)}) collective-permute-start(bf16[512,512]{1,0:T(8,128)(2,1)S(1)} %collective-permute-done.4.refs_1_), channel_id=1, source_target_pairs={{0,1},{1,0},{2,3},{3,2},{4,5},{5,4},{6,7},{7,6},{8,9},{9,8},{10,11... | collective-permute-start | bytes 1572872 | tf_op jit(solution)/shard_map/ppermute | solution.py:536
  138.8 14.8 %collective-permute-start.35 = (bf16[512,512]{1,0:T(8,128)(2,1)S(1)}, bf16[512,512]{1,0:T(8,128)(2,1)S(1)}, u32[]{:S(2)}, u32[]{:S(2)}) collective-permute-start(bf16[512,512]{1,0:T(8,128)(2,1)S(1)} %get-tuple-element.63), channel_id=1, source_target_pairs={{0,2},{1,3},{2,0},{3,1},{4,6},{5,7},{6,4},{7,5},{8,10},{9,11},{10,... | collective-permute-start | bytes 1572872 | tf_op jit(solution)/shard_map/ppermute | solution.py:536
  142.0 25.0 %collective-permute-start.42 = (bf16[1024,512]{1,0:T(8,128)(2,1)S(1)}, bf16[1024,512]{1,0:T(8,128)(2,1)S(1)}, u32[]{:S(2)}, u32[]{:S(2)}) collective-permute-start(bf16[1024,512]{1,0:T(8,128)(2,1)S(1)} %collective-permute-done.16.refs_7_), channel_id=1, source_target_pairs={{0,1},{1,0},{2,3},{3,2},{4,5},{5,4},{6,7},{7,6},{8,9},{9,8},{10,11... | collective-permute-start | bytes 3145736 | tf_op jit(solution)/shard_map/ppermute | solution.py:536
  144.1 23.4 %collective-permute-start.44 = (bf16[1024,512]{1,0:T(8,128)(2,1)S(1)}, bf16[1024,512]{1,0:T(8,128)(2,1)S(1)}, u32[]{:S(2)}, u32[]{:S(2)}) collective-permute-start(bf16[1024,512]{1,0:T(8,128)(2,1)S(1)} %collective-permute-done.22.refs_10_), channel_id=1, source_target_pairs={{0,1},{1,0},{2,3},{3,2},{4,5},{5,4},{6,7},{7,6},{8,9},{9,8},{10,11... | collective-permute-start | bytes 3145736 | tf_op jit(solution)/shard_map/ppermute | solution.py:536
  146.0 21.6 %collective-permute-start.33 = (bf16[512,512]{1,0:T(8,128)(2,1)S(1)}, bf16[512,512]{1,0:T(8,128)(2,1)S(1)}, u32[]{:S(2)}, u32[]{:S(2)}) collective-permute-start(bf16[512,512]{1,0:T(8,128)(2,1)S(1)} %get-tuple-element.61), channel_id=1, source_target_pairs={{0,1},{1,0},{2,3},{3,2},{4,5},{5,4},{6,7},{7,6},{8,9},{9,8},{10,11... | collective-permute-start | bytes 1572872 | tf_op jit(solution)/shard_map/ppermute | solution.py:536
  146.6 21.1 %collective-permute-start.34 = (bf16[512,512]{1,0:T(8,128)(2,1)S(1)}, bf16[512,512]{1,0:T(8,128)(2,1)S(1)}, u32[]{:S(2)}, u32[]{:S(2)}) collective-permute-start(bf16[512,512]{1,0:T(8,128)(2,1)S(1)} %get-tuple-element.62), channel_id=1, source_target_pairs={{0,2},{1,3},{2,0},{3,1},{4,6},{5,7},{6,4},{7,5},{8,10},{9,11},{10,... | collective-permute-start | bytes 1572872 | tf_op jit(solution)/shard_map/ppermute | solution.py:536
  153.5 14.1 %collective-permute-start.36 = (bf16[512,512]{1,0:T(8,128)(2,1)S(1)}, bf16[512,512]{1,0:T(8,128)(2,1)S(1)}, u32[]{:S(2)}, u32[]{:S(2)}) collective-permute-start(bf16[512,512]{1,0:T(8,128)(2,1)S(1)} %collective-permute-done.35), channel_id=1, source_target_pairs={{0,1},{1,0},{2,3},{3,2},{4,5},{5,4},{6,7},{7,6},{8,9},{9,8},{10,11... | collective-permute-start | bytes 1572872 | tf_op jit(solution)/shard_map/ppermute | solution.py:536
  167.0 12.3 %collective-permute-start.30 = (bf16[512,512]{1,0:T(8,128)(2,1)S(1)}, bf16[512,512]{1,0:T(8,128)(2,1)S(1)}, u32[]{:S(2)}, u32[]{:S(2)}) collective-permute-start(bf16[512,512]{1,0:T(8,128)(2,1)S(1)} %copy-done.12), channel_id=1, source_target_pairs={{0,1},{1,0},{2,3},{3,2},{4,5},{5,4},{6,7},{7,6},{8,9},{9,8},{10,11... | collective-permute-start | bytes 1572872 | tf_op jit(solution)/shard_map/ppermute | solution.py:536
  167.5 11.7 %collective-permute-start.32 = (bf16[512,512]{1,0:T(8,128)(2,1)S(1)}, bf16[512,512]{1,0:T(8,128)(2,1)S(1)}, u32[]{:S(2)}, u32[]{:S(2)}) collective-permute-start(bf16[512,512]{1,0:T(8,128)(2,1)S(1)} %collective-permute-done.31.refs_1_), channel_id=1, source_target_pairs={{0,1},{1,0},{2,3},{3,2},{4,5},{5,4},{6,7},{7,6},{8,9},{9,8},{10,11... | collective-permute-start | bytes 1572872 | tf_op jit(solution)/shard_map/ppermute | solution.py:536
  (30 other events, 655.6 us)

commit v3 on v2

--- a/solution.py
+++ b/solution.py
@@ -13,7 +13,7 @@
 f32 = jnp.float32
 bf16 = jnp.bfloat16
 VMEM_LIMIT = 16 << 20
-COST_SHARE = 1.0
+COST_SHARE = 0.05
 NT = (((1,), (1,)), ((), ()))
 TN = (((0,), (0,)), ((), ()))
 
@@ -57,8 +57,7 @@
 
 
 def split_rows(cells):
-    unit = cells // 8
-    return [unit, 2 * unit, 2 * unit, 2 * unit, unit]
+    return [cells // 4] * 4
 
 
 def column_mask(k_ref, group, spots):
@@ -93,71 +92,97 @@
     )(in_hbm(logits), keep_rows)
 
 
-def exp_call(logits, keep_rows, sizes):
+def exp_call(logits, keep_rows, expression, ids, picks, sizes):
     cells, spots = logits.shape
+    block = expression.shape[1] // ids.shape[0]
     tile = 512
     steps = cells // tile
+    slots = min(4, steps)
     starts = [sum(sizes[:c]) for c in range(len(sizes))]
-
-    def body(x_ref, k_ref, *refs):
+    count = len(picks)
+
+    def body(ids_ref, x_ref, k_ref, e_ref, *refs):
         piece_refs = (None, *refs[: len(sizes) - 1])
-        u_ref, s_ref, x_buf, sem, p_sem = refs[len(sizes) - 1 :]
-        fetch = [
-            pltpu.make_async_copy(
-                x_ref.at[pl.ds(t * tile, tile)], x_buf.at[pl.ds(t * tile, tile)], sem.at[t]
+        all_ref, s_ref, *refs = refs[len(sizes) - 1 :]
+        o_refs, (u_buf, x_buf, held, sem, p_sem, a_sem, e_sem) = refs[:count], refs[count:]
+
+        def fetch(t):
+            return pltpu.make_async_copy(
+                x_ref.at[pl.ds(t * tile, tile)], x_buf.at[t % slots], sem.at[t % slots]
             )
-            for t in range(steps)
-        ]
-        for copy in fetch:
-            copy.start()
+
+        for t in range(slots):
+            fetch(t).start()
+        copies = []
+        for q, pick in enumerate(picks):
+            at = pl.ds(pl.multiple_of(ids_ref[pick] * block, block), block)
+            copies.append(pltpu.make_async_copy(e_ref.at[:, at], held.at[q], e_sem.at[q]))
+            copies[q].start()
         total = jnp.zeros((8, spots), f32)
         sent = []
         for t in range(steps):
-            fetch[t].wait()
+            fetch(t).wait()
             for g in range(tile // 128):
                 at = slice(t * tile + g * 128, t * tile + (g + 1) * 128)
-                rise = jnp.exp(x_buf[at, :])
+                rise = jnp.exp(x_buf[t % slots, g * 128 : (g + 1) * 128, :])
                 rise = rise * column_mask(k_ref, t * (tile // 128) + g, spots)
-                u_ref[at, :] = rise.astype(bf16)
+                u_buf[at, :] = rise.astype(bf16)
                 total = total + jnp.sum(rise.reshape(16, 8, spots), axis=0)
+            if t + slots < steps:
+                fetch(t + slots).start()
             for c in range(1, len(sizes)):
                 if starts[c] + sizes[c] == (t + 1) * tile:
                     copy = pltpu.make_async_copy(
-                        u_ref.at[pl.ds(starts[c], sizes[c])], piece_refs[c], p_sem.at[c]
+                        u_buf.at[pl.ds(starts[c], sizes[c])], piece_refs[c], p_sem.at[c]
                     )
                     copy.start()
                     sent.append(copy)
-        s_ref[0:8, :] = total
-        kept = jnp.sum(k_ref[...].astype(f32)) * 0.125
-        s_ref[8:16, :] = jnp.full((8, spots), kept, f32)
+            if t % 2:
+                at = pl.ds((t - 1) * tile, 2 * tile)
+                copy = pltpu.make_async_copy(u_buf.at[at], all_ref.at[at], a_sem.at[t // 2])
+                copy.start()
+                sent.append(copy)
+        kept = jnp.full((1, spots), jnp.sum(k_ref[...].astype(f32)), f32)
+        total = jnp.sum(total, axis=0, keepdims=True)
+        tops = jnp.concatenate([total, kept, jnp.zeros((6, spots), f32)], axis=0)
+        s_ref[...] = tops
+        for q in range(count):
+            copies[q].wait()
+            o_refs[q][0:block, :] = dot(held[q], u_buf[...], TN).astype(bf16)
+            if q == 0:
+                o_refs[0][block : block + 16, :] = packed(tops)
         for copy in sent:
             copy.wait()
 
     return pl.pallas_call(
         body,
-        in_specs=[HBM, VMEM],
-        out_specs=[HBM] * (len(sizes) - 1) + [VMEM] * 2,
-        out_shape=[pltpu.HBM((size, spots), bf16) for size in sizes[1:]]
-        + [shape((cells, spots), bf16), shape((16, spots), f32)],
+        in_specs=[SMEM, HBM, VMEM, HBM],
+        out_specs=[HBM] * len(sizes) + [VMEM] * (1 + count),
+        out_shape=[pltpu.HBM((size, spots), bf16) for size in (*sizes[1:], cells)]
+        + [shape((8, spots), f32)]
+        + [shape((block + 16 * (q == 0), spots), bf16) for q in range(count)],
         scratch_shapes=[
-            pltpu.VMEM((cells, spots), f32),
-            pltpu.SemaphoreType.DMA((steps,)),
+            pltpu.VMEM((cells, spots), bf16),
+            pltpu.VMEM((slots, tile, spots), f32),
+            pltpu.VMEM((count, cells, block), bf16),
+            pltpu.SemaphoreType.DMA((slots,)),
             pltpu.SemaphoreType.DMA((len(sizes),)),
+            pltpu.SemaphoreType.DMA((steps // 2,)),
+            pltpu.SemaphoreType.DMA((count,)),
         ],
         compiler_params=params(),
         cost_estimate=cost(0, 8 * cells * spots),
         name="exp_rows",
-    )(in_hbm(logits), keep_rows)
-
-
-def part_call(expression, mapping, ids, picks, adds, dtypes):
+    )(ids, in_hbm(logits), keep_rows, in_hbm(expression))
+
+
+def part_call(expression, mapping, ids, picks, dtypes):
     cells, spots = mapping.shape
     count = len(picks)
     block = expression.shape[1] // ids.shape[0]
 
     def body(ids_ref, e_ref, u_ref, *refs):
-        a_refs, o_refs = refs[: len(adds)], refs[len(adds) : len(adds) + count]
-        held, sem = refs[len(adds) + count :]
+        o_refs, (held, sem) = refs[:count], refs[count:]
         copies = []
         for q, pick in enumerate(picks):
             at = pl.ds(pl.multiple_of(ids_ref[pick] * block, block), block)
@@ -165,14 +190,11 @@
             copies[q].start()
         for q in range(count):
             copies[q].wait()
-            total = dot(held[q], u_ref[...], TN)
-            if q < len(adds):
-                total = total + a_refs[q][...].astype(f32)
-            o_refs[q][...] = total.astype(dtypes[q])
-
-    return pl.pallas_call(
-        body,
-        in_specs=[SMEM, HBM, VMEM] + [VMEM] * len(adds),
+            o_refs[q][...] = dot(held[q], u_ref[...], TN).astype(dtypes[q])
+
+    return pl.pallas_call(
+        body,
+        in_specs=[SMEM, HBM, VMEM],
         out_specs=[VMEM] * count,
         out_shape=[shape((block, spots), dtype) for dtype in dtypes],
         scratch_shapes=[
@@ -184,7 +206,7 @@
             2 * count * block * cells * spots, 2 * cells * (count * block + spots)
         ),
         name="part",
-    )(ids, in_hbm(expression), mapping, *adds)
+    )(ids, in_hbm(expression), mapping)
 
 
 def add_call(values):
@@ -203,25 +225,66 @@
     )(*values)
 
 
+def packed(tops):
+    rows = jnp.concatenate([part.astype(f32) for part in thirds(tops[0:2, :])], axis=0)
+    return jnp.concatenate([rows, jnp.zeros((10, tops.shape[1]), f32)], axis=0).astype(bf16)
+
+
+def unpacked(rows):
+    rows = rows.astype(f32)
+    two = rows[0:2, :] + rows[2:4, :] + rows[4:6, :]
+    return jnp.concatenate([two, jnp.zeros((6, rows.shape[1]), f32)], axis=0)
+
+
+def relay_call(values, tops):
+    block, spots = values[0].shape
+
+    def body(*refs):
+        *v_refs, tops_ref, o_ref, t_ref = refs
+        total = v_refs[0][...].astype(f32)
+        for ref in v_refs[1:]:
+            total = total + ref[0:block, :].astype(f32)
+        o_ref[0:block, :] = total.astype(bf16)
+        tops_now = tops_ref[...] + unpacked(v_refs[-1][block : block + 16, :])
+        t_ref[...] = tops_now
+        o_ref[block : block + 16, :] = packed(tops_now)
+
+    return pl.pallas_call(
+        body,
+        in_specs=[VMEM] * (len(values) + 1),
+        out_specs=[VMEM] * 2,
+        out_shape=[shape((block + 16, spots), bf16), shape(tops.shape, f32)],
+        compiler_params=params(),
+        cost_estimate=cost(0, 8 * block * spots),
+        name="relay",
+    )(*values, tops)
+
+
 def total_of(tops_ref):
-    return jnp.sum(tops_ref[0:8, :], axis=0, keepdims=True)
+    return tops_ref[0:1, :]
 
 
 def kept_of(tops_ref):
-    return jnp.sum(tops_ref[8:16, 0:1], axis=0, keepdims=True)
+    return tops_ref[1:2, 0:1]
 
 
 def predicted_call(values, tops, target, member):
     block, spots = target.shape
     slides = member.shape[0]
+    more = values[-1].shape[0] > block
 
     def body(*refs):
-        v_refs, (tops_ref, t_ref, m_ref, p_ref, s_ref) = refs[:-5], refs[-5:]
+        v_refs, (tops_ref, t_ref, m_ref, p_ref, near_ref, s_ref, all_ref) = refs[:-7], refs[-7:]
         total = v_refs[0][...].astype(f32)
         for ref in v_refs[1:]:
-            total = total + ref[...].astype(f32)
-        pred = total / total_of(tops_ref)
+            total = total + ref[0:block, :].astype(f32)
+        tops_now = tops_ref[...]
+        if more:
+            tops_now = tops_now + unpacked(v_refs[-1][block : block + 16, :])
+        all_ref[...] = tops_now
+        pred = total / tops_now[0:1, :]
         p_ref[...] = pred
+        near_ref[...] = pred
         target_now = t_ref[...]
         member_low = m_ref[...].astype(bf16)
         for q, value in enumerate((pred * target_now, pred * pred, target_now * target_now)):
@@ -232,7 +295,14 @@
 
     return pl.pallas_call(
         body,
-        out_shape=[shape((block, spots), f32), shape((3 * slides, block), f32)],
+        in_specs=[VMEM] * (len(values) + 3),
+        out_specs=[VMEM] * 4,
+        out_shape=[
+            shape((block, spots), f32),
+            shape((block, spots), f32),
+            shape((3 * slides, block), f32),
+            shape(tops.shape, f32),
+        ],
         compiler_params=params(),
         cost_estimate=cost(0, 16 * block * spots),
         name="predicted",
@@ -433,32 +503,38 @@
 
 
 def expr_call(base, mapping, chunks, grads, tops, start):
-    cells, spots = mapping.shape
-    genes = grads[0].shape[0]
-    count = len(grads)
+    genes, spots = grads[0].shape
+    cells = base.shape[0] if mapping is None else mapping.shape[0]
+    own = 0 if mapping is None else 1
+    count = len(chunks[0])
     tile = 512
     tiles = [(c, t) for c in range(len(chunks)) for t in range(chunks[c][0].shape[0] // tile)]
     slots = min(3, len(tiles))
     flat = [v for chunk in chunks for v in chunk]
 
     def body(*refs):
-        q_refs = refs[: len(flat)]
-        u_ref = refs[len(flat)]
-        g_refs = refs[len(flat) + 1 : len(flat) + 1 + count]
-        tops_ref = refs[len(flat) + 1 + count]
-        o_ref, held, out, in_sem, out_sem = refs[-5:]
+        q_refs, refs = refs[: len(flat)], refs[len(flat) :]
+        g_refs, refs = refs[: len(grads)], refs[len(grads) :]
+        tops_ref, whole_ref, o_ref, held, whole, out, in_sem, whole_sem, out_sem = refs
         scale = expression_scale * kept_of(tops_ref)
 
         def fetch(k):
             c, t = tiles[k]
-            return [
+            copies = [
                 pltpu.make_async_copy(
-                    q_refs[c * (count - 1) + q].at[pl.ds(t * tile, tile)],
+                    q_refs[c * count + q].at[pl.ds(t * tile, tile)],
                     held.at[k % slots, q],
                     in_sem.at[k % slots, q],
                 )
-                for q in range(count - 1)
+                for q in range(count)
             ]
+            at = pl.ds(start + k * tile, tile)
+            copies.append(
+                pltpu.make_async_copy(
+                    whole_ref.at[at], whole.at[k % slots], whole_sem.at[k % slots]
+                )
+            )
+            return copies
 
         def store(k):
             return pltpu.make_async_copy(
@@ -469,15 +545,19 @@
             for copy in fetch(k):
                 copy.start()
         for k in range(len(tiles)):
-            at = slice(start + k * tile, start + (k + 1) * tile)
-            total = dot(u_ref[at, :], g_refs[0][...], NT)
             for copy in fetch(k):
                 copy.wait()
+            total = dot(held[k % slots, 0], g_refs[own][...], NT)
             for q in range(1, count):
-                total = total + dot(held[k % slots, q - 1], g_refs[q][...], NT)
+                total = total + dot(held[k % slots, q], g_refs[own + q][...], NT)
+            if own:
+                total = total + dot(whole[k % slots], g_refs[0][...], NT)
+            total = total * scale
+            if not own:
+                total = total + whole[k % slots]
             if k >= 2:
                 store(k - 2).wait()
-            out[k % 2] = total * scale
+            out[k % 2] = total
             store(k).start()
             if k + slots < len(tiles):
                 for copy in fetch(k + slots):
@@ -485,29 +565,25 @@
         for k in range(max(len(tiles) - 2, 0), len(tiles)):
             store(k).wait()
 
-    operands = [*flat, mapping, *grads, tops]
-    in_specs = [ANY] * len(flat) + [VMEM] * (count + 2)
-    aliases = {}
-    if base is not None:
-        in_specs.append(HBM)
-        operands.append(base)
-        aliases = {len(operands) - 1: 0}
+    operands = [*flat, *grads, tops, in_hbm(mapping) if own else base]
     rows = len(tiles) * tile
     return pl.pallas_call(
         body,
-        in_specs=in_specs,
+        in_specs=[ANY] * len(flat) + [VMEM] * (len(grads) + 1) + [HBM],
         out_specs=HBM,
-        out_shape=shape((cells, genes), f32),
-        input_output_aliases=aliases,
+        out_shape=pltpu.HBM((cells, genes), f32),
+        input_output_aliases={} if own else {len(operands) - 1: 0},
         scratch_shapes=[
-            pltpu.VMEM((slots, count - 1, tile, spots), bf16),
+            pltpu.VMEM((slots, count, tile, spots), bf16),
+            pltpu.VMEM((slots, tile, spots if own else genes), bf16 if own else f32),
             pltpu.VMEM((2, tile, genes), f32),
-            pltpu.SemaphoreType.DMA((slots, count - 1)),
+            pltpu.SemaphoreType.DMA((slots, count)),
+            pltpu.SemaphoreType.DMA((slots,)),
             pltpu.SemaphoreType.DMA((2,)),
         ],
         compiler_params=params(),
         cost_estimate=cost(
-            2 * rows * spots * count * genes, 2 * rows * spots * count + 4 * rows * genes
+            2 * rows * spots * len(grads) * genes, 2 * rows * spots * len(grads) + 4 * rows * genes
         ),
         name="grad_expression",
     )(*operands)
@@ -561,24 +637,16 @@
     def tie(value, others):
         return lax.optimization_barrier((value, *others))[0]
 
-    keep_rows = keep_mask.reshape(cells // 128, 128)
-    sizes = split_rows(cells)
-    starts = [sum(sizes[:c]) for c in range(len(sizes))]
-    pieces = [first_call(logits, keep_rows, sizes[0])]
-    *rest, mapping, sums = exp_call(logits, keep_rows, sizes)
-    pieces += rest
-    gathered = []
-    for piece in pieces:
-        quarters = [None] * m
-        for mask in range(0, m, 2):
-            quarters[mask] = over_spot(piece, mask) if mask else piece
-            quarters[mask + 1] = over_spot(quarters[mask], 1)
-        gathered.append(quarters)
-
-    def arrived(c):
-        return [gathered[c][mask] for mask in range(2, m, 2)]
-
-    tops = sum_cell(sums)
+    last_out = []
+
+    def after(value, others=()):
+        tied = lax.optimization_barrier((value, *last_out, *others))[0]
+        last_out.clear()
+        return tied
+
+    def done(outs):
+        last_out.append(outs[0] if isinstance(outs, (list, tuple)) else outs)
+        return outs
 
     def place_of(code):
         value = me
@@ -595,12 +663,40 @@
 
     ids = jnp.stack([place_of(c) for c in codes(())])
     order = {c[lead:]: q for q, c in enumerate(codes((0,) * lead))}
-
-    def products(first, second, adds, dtypes):
-        return part_call(expression, mapping, ids, [order[first], order[second]], adds, dtypes)
+    slides = jnp.arange(slide_total, dtype=jnp.int32)
+    member = (slide_ids[None, :] == slides[:, None]).astype(f32)
+
+    keep_rows = keep_mask.reshape(cells // 128, 128)
+    sizes = split_rows(cells)
+    starts = [sum(sizes[:c]) for c in range(len(sizes))]
+    pieces = [done(first_call(logits, keep_rows, sizes[0]))]
+    picks = [order[1, 1, 1], order[1, 0, 1]] if not lead and block % 128 == 0 else []
+    outs = exp_call(logits, after(keep_rows), expression, ids, picks, sizes)
+    pieces += outs[: len(sizes) - 1]
+    mapping, sums, *parts = outs[len(sizes) - 1 :]
+    done(sums)
+    gathered = {}
+
+    def send(c, others=()):
+        piece = tie(pieces[c], others)
+        for mask in range(2, m, 2):
+            gathered[c, mask] = over_spot(piece, mask)
+
+    def spread(c):
+        for mask in range(2, m, 2):
+            gathered[c, mask + 1] = over_spot(gathered[c, mask], 1)
+
+    def far(c):
+        return [gathered[c, mask] for mask in range(2, m, 2)]
+
+    def wide(c):
+        return [gathered[c, mask + 1] for mask in range(2, m, 2)]
+
+    send(0)
 
     part, got, step = {}, {}, {}
-    if lead or block % 128:
+    if not picks:
+        tops = sum_cell(sums)
         have = dot(expression, mapping, TN).reshape(n, block, spots)
         have = jnp.take(have, ids, axis=0)
         for k in range(lead):
@@ -614,54 +710,59 @@
         for b in (1, 0):
             part[0, 1, b] = add_call([part[0, 1, b], got[1, 1, b]])
             step[0, 1, b] = across(part[0, 1, b], lead + 1)
-        adds = [part[0, 0, 0], got[1, 0, 0]]
+        part[0, 0, 1] = add_call([part[0, 0, 1], got[1, 0, 1], step[0, 1, 1]])
+        last = across(part[0, 0, 1], lead + 2)
+        send(1)
+        send(2)
+        spread(0)
     else:
-        part[1, 1, 1], part[1, 0, 1] = products((1, 1, 1), (1, 0, 1), [], [bf16] * 2)
-        got[1, 1, 1], got[1, 0, 1] = across(part[1, 1, 1], 0), across(part[1, 0, 1], 0)
-        got[1, 1, 1] = tie(got[1, 1, 1], arrived(0))
-        part[0, 1, 1], part[0, 0, 1] = products(
-            (0, 1, 1), (0, 0, 1), [got[1, 1, 1]], [bf16, f32]
+        part[1, 1, 1], part[1, 0, 1] = parts
+        got[1, 1, 1], got[1, 0, 1] = across(parts[0], 0), across(parts[1], 0)
+
+        def products(first, second, dtype, others):
+            picks = [order[first], order[second]]
+            here = after(ids, others)
+            return done(part_call(expression, mapping, here, picks, [dtype] * 2))
+
+        part[0, 1, 1], part[0, 0, 1] = products((0, 1, 1), (0, 0, 1), f32, [])
+        part[0, 1, 1], tops = done(
+            relay_call([after(part[0, 1, 1], far(0)), got[1, 1, 1]], sums)
         )
+        send(1, [part[0, 1, 1]])
+        spread(0)
         step[0, 1, 1] = across(part[0, 1, 1], 1)
-        part[1, 1, 0], part[1, 0, 0] = products((1, 1, 0), (1, 0, 0), [], [bf16] * 2)
+        part[1, 1, 0], part[1, 0, 0] = products((1, 1, 0), (1, 0, 0), bf16, [])
         got[1, 1, 0], got[1, 0, 0] = across(part[1, 1, 0], 0), across(part[1, 0, 0], 0)
-        part[0, 1, 0], part[0, 0, 0] = products(
-            (0, 1, 0), (0, 0, 0), [got[1, 1, 0], got[1, 0, 0]], [bf16, f32]
+        part[0, 0, 1], tops = done(
+            relay_call([after(part[0, 0, 1]), got[1, 0, 1], step[0, 1, 1]], tops)
         )
+        last = across(part[0, 0, 1], 2)
+        part[0, 1, 0], part[0, 0, 0] = products((0, 1, 0), (0, 0, 0), f32, [])
+        part[0, 1, 0] = done(add_call([after(part[0, 1, 0]), got[1, 1, 0]]))
         step[0, 1, 0] = across(part[0, 1, 0], 1)
-        adds = [part[0, 0, 0]]
-    last = add_call([part[0, 0, 1], got[1, 0, 1], step[0, 1, 1]])
-    last = across(last, lead + 2)
-
-    slides = jnp.arange(slide_total, dtype=jnp.int32)
-    member = (slide_ids[None, :] == slides[:, None]).astype(f32)
-    density, far_density = sum_spot(density_call(mapping, tops, member), True)
-    last = tie(last, [*arrived(1), density])
-    predicted, gene_sums = predicted_call(
-        [*adds, step[0, 1, 0], last], tops, target, member
+        send(2, [part[0, 1, 0]])
+    predicted, predicted_near, gene_sums, tops = done(
+        predicted_call(
+            [part[0, 0, 0], got[1, 0, 0], step[0, 1, 0], last],
+            tops,
+            target,
+            after(member, far(1) + wide(0)),
+        )
     )
     gene_sums, far_sums = sum_spot(gene_sums, True)
-    far_sums = tie(far_sums, arrived(2))
-    grad, ends = grad_call(gene_sums, far_sums, predicted, target, tops, member)
-
-    slope, weight, more = diverge_call(
-        density,
-        far_density,
-        keep_mask[None, :],
-        slide_counts[None, :],
-        mapping,
-        tops,
-        member,
+    density = done(density_call(mapping, tops, after(member)))
+    density, far_density = sum_spot(density, True)
+    beside = over_spot(tie(mapping, [density]), 1)
+    grad, ends = done(
+        grad_call(gene_sums, far_sums, predicted_near, target, tops, after(member))
     )
-    ends = sum_cell(ends + more)
-    mapping_loss = (-ends[1, 0] + density_weight * ends[2, 0]) / (slide_total * genes)
+    send(3, [grad])
 
     have = {(0, 0, 0): grad}
     for k in (2, 1, 0):
         for code in list(have):
             other = tuple(1 if q == k else b for q, b in enumerate(code))
-            source = tie(have[code], [slope]) if (k, code) == (0, (0, 1, 1)) else have[code]
-            have[other] = across(source, lead + k)
+            have[other] = across(have[code], lead + k)
     tail = codes((0,) * lead)
     blocks = [have[c[lead:]] for c in tail]
     if lead:
@@ -670,21 +771,47 @@
             blocks = jnp.concatenate([across(blocks, k), blocks])
         blocks = [blocks[q] for q in range(n)]
 
-    grad_logits = logit_call(
-        expression, blocks, ids, mapping, slope, weight, tie(ends, arrived(3)), tops
+    slope, weight, more = done(
+        diverge_call(
+            density,
+            far_density,
+            keep_mask[None, :],
+            slide_counts[None, :],
+            mapping,
+            tops,
+            after(member, [have[0, 1, 0], beside]),
+        )
     )
-
-    parts = regroup_call(blocks, ids, place[None], m)
+    ends = sum_cell(ends + more)
+    mapping_loss = (-ends[1, 0] + density_weight * ends[2, 0]) / (slide_total * genes)
+
+    spread(1)
+    shares = done(regroup_call(blocks, after(ids, far(2)), place[None], m))
+    spread(2)
     regrouped = [None] * m
     for mask in range(0, m, 2):
-        regrouped[mask] = over_spot(parts[mask], mask) if mask else parts[0]
-        beside = over_spot(parts[mask + 1], mask) if mask else parts[1]
-        regrouped[mask + 1] = over_spot(beside, 1)
-    chunks = [quarters[1:] for quarters in gathered]
-    grad_expression = expr_call(None, mapping, chunks[:-1], regrouped, tops, 0)
-    grad_expression = expr_call(
-        grad_expression, mapping, chunks[-1:], regrouped, tops, starts[-1]
+        regrouped[mask] = over_spot(shares[mask], mask) if mask else shares[0]
+        other = over_spot(shares[mask + 1], mask) if mask else shares[1]
+        regrouped[mask + 1] = over_spot(other, 1)
+
+    grad_logits = done(
+        logit_call(
+            expression,
+            blocks,
+            ids,
+            mapping,
+            slope,
+            weight,
+            after(ends, [*wide(1), *wide(2), regrouped[1]]),
+            tops,
+        )
     )
+    near_part = done(
+        expr_call(None, mapping, [[beside]], regrouped[:2], after(tops, far(3)), 0)
+    )
+    spread(3)
+    rest = [[gathered[c, mask] for mask in range(2, m)] for c in range(4)]
+    grad_expression = expr_call(near_part, None, rest, regrouped[2:], after(tops), 0)
     return (mapping_loss, predicted, grad_logits, grad_expression)
 
 

time: 183 us -> 165 us (0.902)
  waiting for transfers between devices: 77.5 us -> 64.3 us
  starting transfers between devices: 36.4 us -> 31 us
  Pallas kernels: 59 us -> 62.8 us
  local copies, waits for them, and re-layouts: 6.61 us -> 3.55 us
    ppermute x20 -> x17, waiting for transfers between devices: 38.8 us -> 29.4 us  [across(): return lax.ppermute(value, ('cell', 'spot'), pairs)]
    ppermute x21 -> x15, waiting for transfers between devices: 27.1 us -> 21.6 us  [over_spot(): return lax.ppermute(value, 'spot', [(j, j ^ mask) for j in range(m)])]
    ppermute x20 -> x17, starting transfers between devices: 22.8 us -> 19.2 us  [across(): return lax.ppermute(value, ('cell', 'spot'), pairs)]
    pallas_call x8 -> x9, Pallas kernels: 39.6 us -> 43.1 us  [the longest x2 17.7 us: expr_call(): pl.pallas_call(body, in_specs=[ANY] * len(flat) + [VMEM] * (len(grads) +...]
    unnamed x34 -> x28, local copies, waits for them, and re-layouts: 6.01 us -> 2.95 us
    ppermute x21 -> x15, starting transfers between devices: 10.2 us -> 8.2 us  [over_spot(): return lax.ppermute(value, 'spot', [(j, j ^ mask) for j in range(m)])]
  transfers between devices with their start and end apart: 45 -> 36, of which waited for: 19 -> 18; matrix products, arithmetic and copies ran while one was open for 0% -> 0% of each run, Pallas kernels for 30% -> 30%
where the time goes in v3:
time: 165 us
  waiting for transfers between devices  64.3 us (39%)
  Pallas kernels  62.8 us (38%)
  starting transfers between devices  31 us (19%)
  local copies, waits for them, and re-layouts  3.55 us (2%)
  between operations  3.36 us (2%)
    ppermute x17, waiting for transfers between devices, across(): return lax.ppermute(value, ('cell', 'spot'), pairs)  29.4 us
    ppermute x15, waiting for transfers between devices, over_spot(): return lax.ppermute(value, 'spot', [(j, j ^ mask) for j in range(m)])  21.6 us
    ppermute x17, starting transfers between devices, across(): return lax.ppermute(value, ('cell', 'spot'), pairs)  19.2 us
    pallas_call x2, Pallas kernels, expr_call(): pl.pallas_call(body, in_specs=[ANY] * len(flat) + [VMEM] * (len(grads) +...  17.7 us
    pallas_call x3, Pallas kernels, part_call(): pl.pallas_call(body, in_specs=[SMEM, HBM, VMEM], out_specs=[VMEM] * count...  14.6 us
    ppermute x4, waiting for transfers between devices, over_cell(): return lax.ppermute(value, ('cell', 'spot'), pairs)  13.3 us
    pallas_call x1, Pallas kernels, logit_call(): pl.pallas_call(body, grid=(cells // tile,), in_specs=[SMEM, VMEM, VMEM, p...  13.3 us
    pallas_call x1, Pallas kernels, exp_call(): pl.pallas_call(body, in_specs=[SMEM, HBM, VMEM, HBM], out_specs=[HBM] * l...  9.38 us
  transfers between devices with their start and end apart: 36, of which 18 were waited for; matrix products, arithmetic and copies ran while one was open for 0% of the time, Pallas kernels for 30%

profile of v3, /device:TPU:0, one launch (start us, length us, event | category | flops | bytes accessed | tf_op | source)
XLA Modules:
  0.0 165.0 jit_solution(10270994357283917502)
XLA Ops:
  1.4 1.9 %exp_first.1 = bf16[1024,512]{1,0:T(8,128)(2,1)S(1)} custom-call(f32[4096,512]{1,0:T(8,128)} %x_ref.3, s32[32,128]{1,0:T(8,128)S(1)} %bitcast.15), custom_call_target="tpu_custom_call" | custom-call | bytes 157286 | tf_op jit(solution)/shard_map/exp_first/pallas_call | solution.py:83
  3.3 3.0 %collective-permute-start = (bf16[1024,512]{1,0:T(8,128)(2,1)S(1)}, bf16[1024,512]{1,0:T(8,128)(2,1)S(1)}, u32[]{:S(2)}, u32[]{:S(2)}) collective-permute-start(bf16[1024,512]{1,0:T(8,128)(2,1)S(1)} %exp_first.1), channel_id=1, source_target_pairs={{0,2},{1,3},{2,0},{3,1},{4,6},{5,7},{6,4},{7,5},{8,10},{9,11},{10,... | collective-permute-start | bytes 3145736 | tf_op jit(solution)/shard_map/ppermute | solution.py:612
  6.4 9.4 %exp_rows.1 = (bf16[1024,512]{1,0:T(8,128)(2,1)}, bf16[1024,512]{1,0:T(8,128)(2,1)}, bf16[1024,512]{1,0:T(8,128)(2,1)}, bf16[4096,512]{1,0:T(8,128)(2,1)}, f32[8...) custom-call(s32[8]{0:T(128)S(1)} %stack.35.ids_ref, f32[4096,512]{1,0:T(8,128)} %x_ref.3, ...), custom_call_target="tpu_custom_call" | custom-call | bytes 838860 | tf_op jit(solution)/shard_map/exp_rows/pallas_call | solution.py:157
  17.3 2.2 %copy-done = bf16[4096,512]{1,0:T(8,128)(2,1)S(1)} copy-done((bf16[4096,512]{1,0:T(8,128)(2,1)S(1)}, bf16[4096,512]{1,0:T(8,128)(2,1)}, u32[]{:S(2)}) %copy-start) | copy-done | bytes 4194328
  19.5 5.0 %part.3 = (f32[256,512]{1,0:T(8,128)S(1)}, f32[256,512]{1,0:T(8,128)S(1)}) custom-call(s32[8]{0:T(128)S(1)} %stack.35.ids_ref, bf16[4096,2048]{1,0:T(8,128)(2,1)} %e_ref.9, bf16[4096,512]{1,0:T(8,128)(2,1)S(1)} %copy-done), custom_call_target="tpu_custom_call" | custom-call | flops 107374184 | bytes 419430 | tf_op jit(solution)/shard_map/part/pallas_call | solution.py:195
  24.5 5.0 %collective-permute-done.refs_0_ = bf16[1024,512]{1,0:T(8,128)(2,1)S(1)} collective-permute-done((bf16[1024,512]{1,0:T(8,128)(2,1)S(1)}, bf16[1024,512]{1,0:T(8,128)(2,1)S(1)}, u32[]{:S(2)}, u32[]{:S(2)}) %collective-permute-start) | collective-permute-done | bytes 1048608 | tf_op jit(solution)/shard_map/ppermute | solution.py:612
  29.6 1.8 %collective-permute-start.8 = (bf16[1024,512]{1,0:T(8,128)(2,1)S(1)}, bf16[1024,512]{1,0:T(8,128)(2,1)S(1)}, u32[]{:S(2)}, u32[]{:S(2)}) collective-permute-start(bf16[1024,512]{1,0:T(8,128)(2,1)S(1)} %copy-done.9), channel_id=1, source_target_pairs={{0,2},{1,3},{2,0},{3,1},{4,6},{5,7},{6,4},{7,5},{8,10},{9,11},{10,... | collective-permute-start | bytes 3145736 | tf_op jit(solution)/shard_map/ppermute | solution.py:612
  31.4 1.6 collective-permute-start.3
  34.4 4.7 %part.4 = (bf16[256,512]{1,0:T(8,128)(2,1)S(1)}, bf16[256,512]{1,0:T(8,128)(2,1)S(1)}) custom-call(s32[8]{0:T(128)S(1)} %stack.35.ids_ref, bf16[4096,2048]{1,0:T(8,128)(2,1)} %e_ref.9, bf16[4096,512]{1,0:T(8,128)(2,1)S(1)} %copy-done.1), custom_call_target="tpu_custom_call" | custom-call | flops 107374184 | bytes 419430 | tf_op jit(solution)/shard_map/part/pallas_call | solution.py:195
  40.4 2.7 %collective-permute-start.7 = (bf16[272,512]{1,0:T(8,128)(2,1)S(1)}, bf16[272,512]{1,0:T(8,128)(2,1)S(1)}, u32[]{:S(2)}, u32[]{:S(2)}) collective-permute-start(bf16[272,512]{1,0:T(8,128)(2,1)S(1)} %get-tuple-element.66), channel_id=1, source_target_pairs={{0,16},{1,17},{2,18},{3,19},{4,20},{5,21},{6,22},{7,23},{8,24},{9,... | collective-permute-start | bytes 835592 | tf_op jit(solution)/shard_map/ppermute | solution.py:609
  43.0 1.7 %collective-permute-start.4 = (bf16[256,512]{1,0:T(8,128)(2,1)S(1)}, bf16[256,512]{1,0:T(8,128)(2,1)S(1)}, u32[]{:S(2)}, u32[]{:S(2)}) collective-permute-start(bf16[256,512]{1,0:T(8,128)(2,1)S(1)} %get-tuple-element.69), channel_id=1, source_target_pairs={{0,4},{1,9},{2,6},{3,11},{4,0},{5,13},{6,2},{7,15},{8,12},{9,1},{1... | collective-permute-start | bytes 786440 | tf_op jit(solution)/shard_map/ppermute | solution.py:609
  44.8 5.0 %part.5 = (f32[256,512]{1,0:T(8,128)S(1)}, f32[256,512]{1,0:T(8,128)S(1)}) custom-call(s32[8]{0:T(128)S(1)} %stack.35.ids_ref, bf16[4096,2048]{1,0:T(8,128)(2,1)} %e_ref.9, bf16[4096,512]{1,0:T(8,128)(2,1)S(1)} %copy-done.1), custom_call_target="tpu_custom_call" | custom-call | flops 107374184 | bytes 419430 | tf_op jit(solution)/shard_map/part/pallas_call | solution.py:195
  49.9 2.0 %collective-permute-start.6 = (bf16[256,512]{1,0:T(8,128)(2,1)S(1)}, bf16[256,512]{1,0:T(8,128)(2,1)S(1)}, u32[]{:S(2)}, u32[]{:S(2)}) collective-permute-start(bf16[256,512]{1,0:T(8,128)(2,1)S(1)} %add_blocks.1), channel_id=1, source_target_pairs={{0,8},{1,5},{2,10},{3,7},{4,12},{5,1},{6,14},{7,3},{8,0},{9,13},{1... | collective-permute-start | bytes 786440 | tf_op jit(solution)/shard_map/ppermute | solution.py:609
  51.9 2.1 %collective-permute-done.8.refs_2_ = bf16[1024,512]{1,0:T(8,128)(2,1)S(1)} collective-permute-done((bf16[1024,512]{1,0:T(8,128)(2,1)S(1)}, bf16[1024,512]{1,0:T(8,128)(2,1)S(1)}, u32[]{:S(2)}, u32[]{:S(2)}) %collective-permute-start.8) | collective-permute-done | bytes 1048608 | tf_op jit(solution)/shard_map/ppermute | solution.py:612
  54.0 5.3 %collective-permute-done.6.refs_2_ = bf16[256,512]{1,0:T(8,128)(2,1)S(1)} collective-permute-done((bf16[256,512]{1,0:T(8,128)(2,1)S(1)}, bf16[256,512]{1,0:T(8,128)(2,1)S(1)}, u32[]{:S(2)}, u32[]{:S(2)}) %collective-permute-start.6) | collective-permute-done | bytes 262176 | tf_op jit(solution)/shard_map/ppermute | solution.py:609
  63.9 6.5 %collective-permute-done.10 = f32[24,256]{1,0:T(8,128)S(1)} collective-permute-done((f32[24,256]{1,0:T(8,128)S(1)}, f32[24,256]{1,0:T(8,128)S(1)}, u32[]{:S(2)}, u32[]{:S(2)}) %collective-permute-start.10) | collective-permute-done | bytes 24608 | tf_op jit(solution)/shard_map/ppermute | solution.py:612
  71.2 3.0 %collective-permute-done.11 = f32[24,256]{1,0:T(8,128)S(1)} collective-permute-done((f32[24,256]{1,0:T(8,128)S(1)}, f32[24,256]{1,0:T(8,128)S(1)}, u32[]{:S(2)}, u32[]{:S(2)}) %collective-permute-start.11) | collective-permute-done | bytes 24608 | tf_op jit(solution)/shard_map/ppermute | solution.py:618
  74.9 4.1 %collective-permute-done.12.f_ref = f32[24,256]{1,0:T(8,128)S(1)} collective-permute-done((f32[24,256]{1,0:T(8,128)S(1)}, f32[24,256]{1,0:T(8,128)S(1)}, u32[]{:S(2)}, u32[]{:S(2)}) %collective-permute-start.12) | collective-permute-done | bytes 24608 | tf_op jit(solution)/shard_map/ppermute | solution.py:618
  81.1 5.4 %collective-permute-done.14 = f32[8,4096]{1,0:T(8,128)S(1)} collective-permute-done((f32[8,4096]{1,0:T(8,128)S(1)}, f32[8,4096]{1,0:T(8,128)S(1)}, u32[]{:S(2)}, u32[]{:S(2)}) %collective-permute-start.14) | collective-permute-done | bytes 131104 | tf_op jit(solution)/shard_map/ppermute | solution.py:618
  86.4 1.6 collective-permute-start.22
  88.0 1.9 %collective-permute-done.21.refs_4_ = bf16[1024,512]{1,0:T(8,128)(2,1)S(1)} collective-permute-done((bf16[1024,512]{1,0:T(8,128)(2,1)S(1)}, bf16[1024,512]{1,0:T(8,128)(2,1)S(1)}, u32[]{:S(2)}, u32[]{:S(2)}) %collective-permute-start.21) | collective-permute-done | bytes 1048608 | tf_op jit(solution)/shard_map/ppermute | solution.py:612
  92.0 5.0 %collective-permute-done.22.refs_6_ = bf16[256,512]{1,0:T(8,128)(2,1)S(1)} collective-permute-done((bf16[256,512]{1,0:T(8,128)(2,1)S(1)}, bf16[256,512]{1,0:T(8,128)(2,1)S(1)}, u32[]{:S(2)}, u32[]{:S(2)}) %collective-permute-start.22) | collective-permute-done | bytes 262176 | tf_op jit(solution)/shard_map/ppermute | solution.py:609
  98.9 7.3 %collective-permute-done.23.refs_4_ = bf16[256,512]{1,0:T(8,128)(2,1)S(1)} collective-permute-done((bf16[256,512]{1,0:T(8,128)(2,1)S(1)}, bf16[256,512]{1,0:T(8,128)(2,1)S(1)}, u32[]{:S(2)}, u32[]{:S(2)}) %collective-permute-start.23) | collective-permute-done | bytes 262176 | tf_op jit(solution)/shard_map/ppermute | solution.py:609
  106.6 1.6 collective-permute-start.24
  109.7 4.9 %collective-permute-done.31.refs_6_ = bf16[1024,512]{1,0:T(8,128)(2,1)S(1)} collective-permute-done((bf16[1024,512]{1,0:T(8,128)(2,1)S(1)}, bf16[1024,512]{1,0:T(8,128)(2,1)S(1)}, u32[]{:S(2)}, u32[]{:S(2)}) %collective-permute-start.31) | collective-permute-done | bytes 1048608 | tf_op jit(solution)/shard_map/ppermute | solution.py:612
  117.6 3.7 %collective-permute-done.18 = f32[8,512]{1,0:T(8,128)S(1)} collective-permute-done((f32[8,512]{1,0:T(8,128)S(1)}, f32[8,512]{1,0:T(8,128)S(1)}, u32[]{:S(2)}, u32[]{:S(2)}) %collective-permute-start.18) | collective-permute-done | bytes 16416 | tf_op jit(solution)/shard_map/ppermute | solution.py:609
  121.3 3.7 %collective-permute-done.19 = f32[8,512]{1,0:T(8,128)S(1)} collective-permute-done((f32[8,512]{1,0:T(8,128)S(1)}, f32[8,512]{1,0:T(8,128)S(1)}, u32[]{:S(2)}, u32[]{:S(2)}) %collective-permute-start.19) | collective-permute-done | bytes 16416 | tf_op jit(solution)/shard_map/ppermute | solution.py:609
  125.1 2.1 %collective-permute-start.20 = (f32[8,512]{1,0:T(8,128)S(1)}, f32[8,512]{1,0:T(8,128)S(1)}, u32[]{:S(2)}, u32[]{:S(2)}) collective-permute-start(f32[8,512]{1,0:T(8,128)S(1)} %add.26), channel_id=1, source_target_pairs={{0,16},{1,17},{2,18},{3,19},{4,20},{5,21},{6,22},{7,23},{8,24},{9,... | collective-permute-start | bytes 49160 | tf_op jit(solution)/shard_map/ppermute | solution.py:609
  127.1 3.0 %collective-permute-done.20 = f32[8,512]{1,0:T(8,128)S(1)} collective-permute-done((f32[8,512]{1,0:T(8,128)S(1)}, f32[8,512]{1,0:T(8,128)S(1)}, u32[]{:S(2)}, u32[]{:S(2)}) %collective-permute-start.20) | collective-permute-done | bytes 16416 | tf_op jit(solution)/shard_map/ppermute | solution.py:609
  132.8 13.3 %grad_logits.1 = f32[4096,512]{1,0:T(8,128)} custom-call(s32[8]{0:T(128)S(1)} %stack.35.ids_ref, bf16[4096,2048]{1,0:T(8,128)(2,1)S(1)} %bitcast.14, bf16[4096,512]{1,0:T(8,128)(2,1)S(1)} %copy-done.1, bf16[32,4096]{1,0:T(8,128)(2,1)S(1)} %get-tuple-element.86.d_ref, bf16[32,512]{1,0:T(8,128)(2,1)S(1)} %get-tuple-element.87.w_ref, ...), custom_call_target="tpu_custom_call" | custom-call | flops 429496736 | bytes 1468006 | tf_op jit(solution)/shard_map/grad_logits/pallas_call | solution.py:490
  146.1 8.6 %grad_expression.2.refs_11_ = f32[4096,512]{1,0:T(8,128)} custom-call(bf16[4096,512]{1,0:T(8,128)(2,1)S(1)} %collective-permute-done.17.refs_0_, bf16[512,512]{1,0:T(8,128)(2,1)S(1)} %get-tuple-element.91.refs_1_, bf16[512,512]{1,0:T(8,128)(2,1)S(1)} %collective-permute-done.30.refs_2_, f32[8,512]{1,0:T(8,128)S(1)} %get-tuple-element.99.tops_ref.refs_3_.refs_10_, ...), custom_call_target="tpu_custom_call" | custom-call | flops 214748368 | bytes 838860 | tf_op jit(solution)/shard_map/grad_expression/pallas_call | solution.py:570
  154.8 9.1 %grad_expression.3 = f32[4096,512]{1,0:T(8,128)} custom-call(bf16[1024,512]{1,0:T(8,128)(2,1)S(1)} %collective-permute-done.refs_0_, bf16[1024,512]{1,0:T(8,128)(2,1)S(1)} %collective-permute-done.9.refs_1_, bf16[1024,512]{1,0:T(8,128)(2,1)S(1)} %collective-permute-done.8.refs_2_, ...), custom_call_target="tpu_custom_call", output_to_operand_aliasing={{}: (11, {})} | custom-call | flops 214748368 | bytes 838860 | tf_op jit(solution)/shard_map/grad_expression/pallas_call | solution.py:570
  (94 shorter events, 23.5 us)
Async XLA Ops:
  3.3 26.2 %collective-permute-start = (bf16[1024,512]{1,0:T(8,128)(2,1)S(1)}, bf16[1024,512]{1,0:T(8,128)(2,1)S(1)}, u32[]{:S(2)}, u32[]{:S(2)}) collective-permute-start(bf16[1024,512]{1,0:T(8,128)(2,1)S(1)} %exp_first.1), channel_id=1, source_target_pairs={{0,2},{1,3},{2,0},{3,1},{4,6},{5,7},{6,4},{7,5},{8,10},{9,11},{10,... | collective-permute-start | bytes 3145736 | tf_op jit(solution)/shard_map/ppermute | solution.py:612
  15.8 13.7 %collective-permute-start.1 = (bf16[272,512]{1,0:T(8,128)(2,1)S(1)}, bf16[272,512]{1,0:T(8,128)(2,1)S(1)}, u32[]{:S(2)}, u32[]{:S(2)}) collective-permute-start(bf16[272,512]{1,0:T(8,128)(2,1)S(1)} %get-tuple-element.59), channel_id=1, source_target_pairs={{0,4},{1,9},{2,6},{3,11},{4,0},{5,13},{6,2},{7,15},{8,12},{9,1},{1... | collective-permute-start | bytes 835592 | tf_op jit(solution)/shard_map/ppermute | solution.py:609
  29.6 24.4 %collective-permute-start.8 = (bf16[1024,512]{1,0:T(8,128)(2,1)S(1)}, bf16[1024,512]{1,0:T(8,128)(2,1)S(1)}, u32[]{:S(2)}, u32[]{:S(2)}) collective-permute-start(bf16[1024,512]{1,0:T(8,128)(2,1)S(1)} %copy-done.9), channel_id=1, source_target_pairs={{0,2},{1,3},{2,0},{3,1},{4,6},{5,7},{6,4},{7,5},{8,10},{9,11},{10,... | collective-permute-start | bytes 3145736 | tf_op jit(solution)/shard_map/ppermute | solution.py:612
  31.4 22.6 %collective-permute-start.9 = (bf16[1024,512]{1,0:T(8,128)(2,1)S(1)}, bf16[1024,512]{1,0:T(8,128)(2,1)S(1)}, u32[]{:S(2)}, u32[]{:S(2)}) collective-permute-start(bf16[1024,512]{1,0:T(8,128)(2,1)S(1)} %collective-permute-done.refs_0_), channel_id=1, source_target_pairs={{0,1},{1,0},{2,3},{3,2},{4,5},{5,4},{6,7},{7,6},{8,9},{9,8},{10,11... | collective-permute-start | bytes 3145736 | tf_op jit(solution)/shard_map/ppermute | solution.py:612
  31.4 8.9 %collective-permute-start.3 = (bf16[272,512]{1,0:T(8,128)(2,1)S(1)}, bf16[272,512]{1,0:T(8,128)(2,1)S(1)}, u32[]{:S(2)}, u32[]{:S(2)}) collective-permute-start(bf16[272,512]{1,0:T(8,128)(2,1)S(1)} %get-tuple-element.60), channel_id=1, source_target_pairs={{0,8},{1,5},{2,10},{3,7},{4,12},{5,1},{6,14},{7,3},{8,0},{9,13},{1... | collective-permute-start | bytes 835592 | tf_op jit(solution)/shard_map/ppermute | solution.py:609
  32.9 7.3 %collective-permute-start.2 = (bf16[256,512]{1,0:T(8,128)(2,1)S(1)}, bf16[256,512]{1,0:T(8,128)(2,1)S(1)}, u32[]{:S(2)}, u32[]{:S(2)}) collective-permute-start(bf16[256,512]{1,0:T(8,128)(2,1)S(1)} %get-tuple-element.64), channel_id=1, source_target_pairs={{0,4},{1,9},{2,6},{3,11},{4,0},{5,13},{6,2},{7,15},{8,12},{9,1},{1... | collective-permute-start | bytes 786440 | tf_op jit(solution)/shard_map/ppermute | solution.py:609
  39.1 10.7 %collective-permute-start.5 = (bf16[256,512]{1,0:T(8,128)(2,1)S(1)}, bf16[256,512]{1,0:T(8,128)(2,1)S(1)}, u32[]{:S(2)}, u32[]{:S(2)}) collective-permute-start(bf16[256,512]{1,0:T(8,128)(2,1)S(1)} %get-tuple-element.62), channel_id=1, source_target_pairs={{0,4},{1,9},{2,6},{3,11},{4,0},{5,13},{6,2},{7,15},{8,12},{9,1},{1... | collective-permute-start | bytes 786440 | tf_op jit(solution)/shard_map/ppermute | solution.py:609
  40.4 18.9 %collective-permute-start.7 = (bf16[272,512]{1,0:T(8,128)(2,1)S(1)}, bf16[272,512]{1,0:T(8,128)(2,1)S(1)}, u32[]{:S(2)}, u32[]{:S(2)}) collective-permute-start(bf16[272,512]{1,0:T(8,128)(2,1)S(1)} %get-tuple-element.66), channel_id=1, source_target_pairs={{0,16},{1,17},{2,18},{3,19},{4,20},{5,21},{6,22},{7,23},{8,24},{9,... | collective-permute-start | bytes 835592 | tf_op jit(solution)/shard_map/ppermute | solution.py:609
  43.0 10.9 %collective-permute-start.4 = (bf16[256,512]{1,0:T(8,128)(2,1)S(1)}, bf16[256,512]{1,0:T(8,128)(2,1)S(1)}, u32[]{:S(2)}, u32[]{:S(2)}) collective-permute-start(bf16[256,512]{1,0:T(8,128)(2,1)S(1)} %get-tuple-element.69), channel_id=1, source_target_pairs={{0,4},{1,9},{2,6},{3,11},{4,0},{5,13},{6,2},{7,15},{8,12},{9,1},{1... | collective-permute-start | bytes 786440 | tf_op jit(solution)/shard_map/ppermute | solution.py:609
  49.9 9.4 %collective-permute-start.6 = (bf16[256,512]{1,0:T(8,128)(2,1)S(1)}, bf16[256,512]{1,0:T(8,128)(2,1)S(1)}, u32[]{:S(2)}, u32[]{:S(2)}) collective-permute-start(bf16[256,512]{1,0:T(8,128)(2,1)S(1)} %add_blocks.1), channel_id=1, source_target_pairs={{0,8},{1,5},{2,10},{3,7},{4,12},{5,1},{6,14},{7,3},{8,0},{9,13},{1... | collective-permute-start | bytes 786440 | tf_op jit(solution)/shard_map/ppermute | solution.py:609
  63.1 45.1 %collective-permute-start.17 = (bf16[4096,512]{1,0:T(8,128)(2,1)S(1)}, bf16[4096,512]{1,0:T(8,128)(2,1)S(1)}, u32[]{:S(2)}, u32[]{:S(2)}) collective-permute-start(bf16[4096,512]{1,0:T(8,128)(2,1)S(1)} %copy-done.1), channel_id=1, source_target_pairs={{0,1},{1,0},{2,3},{3,2},{4,5},{5,4},{6,7},{7,6},{8,9},{9,8},{10,11... | collective-permute-start | bytes 12582920 | tf_op jit(solution)/shard_map/ppermute | solution.py:612
  63.3 26.5 %collective-permute-start.21 = (bf16[1024,512]{1,0:T(8,128)(2,1)S(1)}, bf16[1024,512]{1,0:T(8,128)(2,1)S(1)}, u32[]{:S(2)}, u32[]{:S(2)}) collective-permute-start(bf16[1024,512]{1,0:T(8,128)(2,1)S(1)} %copy-done.8), channel_id=1, source_target_pairs={{0,2},{1,3},{2,0},{3,1},{4,6},{5,7},{6,4},{7,5},{8,10},{9,11},{10,... | collective-permute-start | bytes 3145736 | tf_op jit(solution)/shard_map/ppermute | solution.py:612
  63.8 6.5 %collective-permute-start.10 = (f32[24,256]{1,0:T(8,128)S(1)}, f32[24,256]{1,0:T(8,128)S(1)}, u32[]{:S(2)}, u32[]{:S(2)}) collective-permute-start(f32[24,256]{1,0:T(8,128)S(1)} %get-tuple-element.75), channel_id=1, source_target_pairs={{0,1},{1,0},{2,3},{3,2},{4,5},{5,4},{6,7},{7,6},{8,9},{9,8},{10,11... | collective-permute-start | bytes 73736 | tf_op jit(solution)/shard_map/ppermute | solution.py:612
  74.2 4.8 %collective-permute-start.12 = (f32[24,256]{1,0:T(8,128)S(1)}, f32[24,256]{1,0:T(8,128)S(1)}, u32[]{:S(2)}, u32[]{:S(2)}) collective-permute-start(f32[24,256]{1,0:T(8,128)S(1)} %collective-permute-done.11), channel_id=1, source_target_pairs={{0,6},{1,7},{2,4},{3,5},{4,2},{5,3},{6,0},{7,1},{8,14},{9,15},{10,... | collective-permute-start | bytes 73736 | tf_op jit(solution)/shard_map/ppermute | solution.py:618
  79.7 34.8 %collective-permute-start.31 = (bf16[1024,512]{1,0:T(8,128)(2,1)S(1)}, bf16[1024,512]{1,0:T(8,128)(2,1)S(1)}, u32[]{:S(2)}, u32[]{:S(2)}) collective-permute-start(bf16[1024,512]{1,0:T(8,128)(2,1)S(1)} %copy-done.7), channel_id=1, source_target_pairs={{0,2},{1,3},{2,0},{3,1},{4,6},{5,7},{6,4},{7,5},{8,10},{9,11},{10,... | collective-permute-start | bytes 3145736 | tf_op jit(solution)/shard_map/ppermute | solution.py:612
  80.3 6.1 %collective-permute-start.14 = (f32[8,4096]{1,0:T(8,128)S(1)}, f32[8,4096]{1,0:T(8,128)S(1)}, u32[]{:S(2)}, u32[]{:S(2)}) collective-permute-start(f32[8,4096]{1,0:T(8,128)S(1)} %add.23.d_ref), channel_id=1, source_target_pairs={{0,4},{1,5},{2,6},{3,7},{4,0},{5,1},{6,2},{7,3},{8,12},{9,13},{10,... | collective-permute-start | bytes 393224 | tf_op jit(solution)/shard_map/ppermute | solution.py:618
  81.1 9.6 %collective-permute-start.16 = (bf16[256,512]{1,0:T(8,128)(2,1)S(1)}, bf16[256,512]{1,0:T(8,128)(2,1)S(1)}, u32[]{:S(2)}, u32[]{:S(2)}) collective-permute-start(bf16[256,512]{1,0:T(8,128)(2,1)S(1)} %get-tuple-element.82.refs_7_), channel_id=1, source_target_pairs={{0,8},{1,5},{2,10},{3,7},{4,12},{5,1},{6,14},{7,3},{8,0},{9,13},{1... | collective-permute-start | bytes 786440 | tf_op jit(solution)/shard_map/ppermute | solution.py:609
  86.4 10.6 %collective-permute-start.22 = (bf16[256,512]{1,0:T(8,128)(2,1)S(1)}, bf16[256,512]{1,0:T(8,128)(2,1)S(1)}, u32[]{:S(2)}, u32[]{:S(2)}) collective-permute-start(bf16[256,512]{1,0:T(8,128)(2,1)S(1)} %get-tuple-element.82.refs_7_), channel_id=1, source_target_pairs={{0,16},{1,17},{2,18},{3,19},{4,20},{5,21},{6,22},{7,23},{8,24},{9,... | collective-permute-start | bytes 786440 | tf_op jit(solution)/shard_map/ppermute | solution.py:609
  89.9 7.2 %collective-permute-start.27 = (bf16[256,512]{1,0:T(8,128)(2,1)S(1)}, bf16[256,512]{1,0:T(8,128)(2,1)S(1)}, u32[]{:S(2)}, u32[]{:S(2)}) collective-permute-start(bf16[256,512]{1,0:T(8,128)(2,1)S(1)} %get-tuple-element.82.refs_7_), channel_id=1, source_target_pairs={{0,4},{1,9},{2,6},{3,11},{4,0},{5,13},{6,2},{7,15},{8,12},{9,1},{1... | collective-permute-start | bytes 786440 | tf_op jit(solution)/shard_map/ppermute | solution.py:609
  90.6 7.4 %collective-permute-start.15 = (f32[8,4096]{1,0:T(8,128)S(1)}, f32[8,4096]{1,0:T(8,128)S(1)}, u32[]{:S(2)}, u32[]{:S(2)}) collective-permute-start(f32[8,4096]{1,0:T(8,128)S(1)} %collective-permute-done.14), channel_id=1, source_target_pairs={{0,6},{1,7},{2,4},{3,5},{4,2},{5,3},{6,0},{7,1},{8,14},{9,15},{10,... | collective-permute-start | bytes 393224 | tf_op jit(solution)/shard_map/ppermute | solution.py:618
  97.0 28.0 %collective-permute-start.28 = (bf16[1024,512]{1,0:T(8,128)(2,1)S(1)}, bf16[1024,512]{1,0:T(8,128)(2,1)S(1)}, u32[]{:S(2)}, u32[]{:S(2)}) collective-permute-start(bf16[1024,512]{1,0:T(8,128)(2,1)S(1)} %collective-permute-done.8.refs_2_), channel_id=1, source_target_pairs={{0,1},{1,0},{2,3},{3,2},{4,5},{5,4},{6,7},{7,6},{8,9},{9,8},{10,11... | collective-permute-start | bytes 3145736 | tf_op jit(solution)/shard_map/ppermute | solution.py:612
  97.0 9.1 %collective-permute-start.23 = (bf16[256,512]{1,0:T(8,128)(2,1)S(1)}, bf16[256,512]{1,0:T(8,128)(2,1)S(1)}, u32[]{:S(2)}, u32[]{:S(2)}) collective-permute-start(bf16[256,512]{1,0:T(8,128)(2,1)S(1)} %collective-permute-done.22.refs_6_), channel_id=1, source_target_pairs={{0,8},{1,5},{2,10},{3,7},{4,12},{5,1},{6,14},{7,3},{8,0},{9,13},{1... | collective-permute-start | bytes 786440 | tf_op jit(solution)/shard_map/ppermute | solution.py:609
  98.1 8.5 %collective-permute-start.25 = (bf16[256,512]{1,0:T(8,128)(2,1)S(1)}, bf16[256,512]{1,0:T(8,128)(2,1)S(1)}, u32[]{:S(2)}, u32[]{:S(2)}) collective-permute-start(bf16[256,512]{1,0:T(8,128)(2,1)S(1)} %collective-permute-done.16.refs_5_), channel_id=1, source_target_pairs={{0,4},{1,9},{2,6},{3,11},{4,0},{5,13},{6,2},{7,15},{8,12},{9,1},{1... | collective-permute-start | bytes 786440 | tf_op jit(solution)/shard_map/ppermute | solution.py:609
  106.2 8.4 %collective-permute-start.26 = (bf16[256,512]{1,0:T(8,128)(2,1)S(1)}, bf16[256,512]{1,0:T(8,128)(2,1)S(1)}, u32[]{:S(2)}, u32[]{:S(2)}) collective-permute-start(bf16[256,512]{1,0:T(8,128)(2,1)S(1)} %collective-permute-done.22.refs_6_), channel_id=1, source_target_pairs={{0,4},{1,9},{2,6},{3,11},{4,0},{5,13},{6,2},{7,15},{8,12},{9,1},{1... | collective-permute-start | bytes 786440 | tf_op jit(solution)/shard_map/ppermute | solution.py:609
  106.6 8.8 %collective-permute-start.24 = (bf16[256,512]{1,0:T(8,128)(2,1)S(1)}, bf16[256,512]{1,0:T(8,128)(2,1)S(1)}, u32[]{:S(2)}, u32[]{:S(2)}) collective-permute-start(bf16[256,512]{1,0:T(8,128)(2,1)S(1)} %collective-permute-done.23.refs_4_), channel_id=1, source_target_pairs={{0,4},{1,9},{2,6},{3,11},{4,0},{5,13},{6,2},{7,15},{8,12},{9,1},{1... | collective-permute-start | bytes 786440 | tf_op jit(solution)/shard_map/ppermute | solution.py:609
  108.2 24.5 %collective-permute-start.29 = (bf16[1024,512]{1,0:T(8,128)(2,1)S(1)}, bf16[1024,512]{1,0:T(8,128)(2,1)S(1)}, u32[]{:S(2)}, u32[]{:S(2)}) collective-permute-start(bf16[1024,512]{1,0:T(8,128)(2,1)S(1)} %collective-permute-done.21.refs_4_), channel_id=1, source_target_pairs={{0,1},{1,0},{2,3},{3,2},{4,5},{5,4},{6,7},{7,6},{8,9},{9,8},{10,11... | collective-permute-start | bytes 3145736 | tf_op jit(solution)/shard_map/ppermute | solution.py:612
  114.6 40.2 %collective-permute-start.32 = (bf16[1024,512]{1,0:T(8,128)(2,1)S(1)}, bf16[1024,512]{1,0:T(8,128)(2,1)S(1)}, u32[]{:S(2)}, u32[]{:S(2)}) collective-permute-start(bf16[1024,512]{1,0:T(8,128)(2,1)S(1)} %collective-permute-done.31.refs_6_), channel_id=1, source_target_pairs={{0,1},{1,0},{2,3},{3,2},{4,5},{5,4},{6,7},{7,6},{8,9},{9,8},{10,11... | collective-permute-start | bytes 3145736 | tf_op jit(solution)/shard_map/ppermute | solution.py:612
  116.3 14.5 %collective-permute-start.34 = (bf16[512,512]{1,0:T(8,128)(2,1)S(1)}, bf16[512,512]{1,0:T(8,128)(2,1)S(1)}, u32[]{:S(2)}, u32[]{:S(2)}) collective-permute-start(bf16[512,512]{1,0:T(8,128)(2,1)S(1)} %get-tuple-element.97), channel_id=1, source_target_pairs={{0,2},{1,3},{2,0},{3,1},{4,6},{5,7},{6,4},{7,5},{8,10},{9,11},{10,... | collective-permute-start | bytes 1572872 | tf_op jit(solution)/shard_map/ppermute | solution.py:612
  125.1 7.7 %collective-permute-start.30 = (bf16[512,512]{1,0:T(8,128)(2,1)S(1)}, bf16[512,512]{1,0:T(8,128)(2,1)S(1)}, u32[]{:S(2)}, u32[]{:S(2)}) collective-permute-start(bf16[512,512]{1,0:T(8,128)(2,1)S(1)} %get-tuple-element.92), channel_id=1, source_target_pairs={{0,1},{1,0},{2,3},{3,2},{4,5},{5,4},{6,7},{7,6},{8,9},{9,8},{10,11... | collective-permute-start | bytes 1572872 | tf_op jit(solution)/shard_map/ppermute | solution.py:612
  125.1 5.1 %collective-permute-start.20 = (f32[8,512]{1,0:T(8,128)S(1)}, f32[8,512]{1,0:T(8,128)S(1)}, u32[]{:S(2)}, u32[]{:S(2)}) collective-permute-start(f32[8,512]{1,0:T(8,128)S(1)} %add.26), channel_id=1, source_target_pairs={{0,16},{1,17},{2,18},{3,19},{4,20},{5,21},{6,22},{7,23},{8,24},{9,... | collective-permute-start | bytes 49160 | tf_op jit(solution)/shard_map/ppermute | solution.py:609
  130.1 24.6 %collective-permute-start.33 = (bf16[512,512]{1,0:T(8,128)(2,1)S(1)}, bf16[512,512]{1,0:T(8,128)(2,1)S(1)}, u32[]{:S(2)}, u32[]{:S(2)}) collective-permute-start(bf16[512,512]{1,0:T(8,128)(2,1)S(1)} %get-tuple-element.96), channel_id=1, source_target_pairs={{0,2},{1,3},{2,0},{3,1},{4,6},{5,7},{6,4},{7,5},{8,10},{9,11},{10,... | collective-permute-start | bytes 1572872 | tf_op jit(solution)/shard_map/ppermute | solution.py:612
  130.9 23.9 %collective-permute-start.35 = (bf16[512,512]{1,0:T(8,128)(2,1)S(1)}, bf16[512,512]{1,0:T(8,128)(2,1)S(1)}, u32[]{:S(2)}, u32[]{:S(2)}) collective-permute-start(bf16[512,512]{1,0:T(8,128)(2,1)S(1)} %collective-permute-done.34), channel_id=1, source_target_pairs={{0,1},{1,0},{2,3},{3,2},{4,5},{5,4},{6,7},{7,6},{8,9},{9,8},{10,11... | collective-permute-start | bytes 1572872 | tf_op jit(solution)/shard_map/ppermute | solution.py:612
  (18 other events, 515.5 us)

commit v4 on v3

--- a/solution.py
+++ b/solution.py
@@ -12,16 +12,16 @@
 norm_eps = 1e-06
 f32 = jnp.float32
 bf16 = jnp.bfloat16
-VMEM_LIMIT = 16 << 20
+VMEM_LIMIT = 20 << 20
 COST_SHARE = 0.05
 NT = (((1,), (1,)), ((), ()))
 TN = (((0,), (0,)), ((), ()))
 
 
-def cost(flops, bytes_accessed):
+def cost(flops, bytes_accessed, share=COST_SHARE):
     return pl.CostEstimate(
-        flops=int(flops * COST_SHARE),
-        bytes_accessed=int(bytes_accessed * COST_SHARE),
+        flops=int(flops * share),
+        bytes_accessed=int(bytes_accessed * share),
         transcendentals=0,
     )
 
@@ -57,7 +57,8 @@
 
 
 def split_rows(cells):
-    return [cells // 4] * 4
+    unit = cells // 64
+    return [share * unit for share in (16, 20, 24, 4)]
 
 
 def column_mask(k_ref, group, spots):
@@ -72,24 +73,33 @@
 def first_call(logits, keep_rows, size):
     spots = logits.shape[1]
 
-    def body(x_ref, k_ref, o_ref, x_buf, sem):
-        copy = pltpu.make_async_copy(x_ref.at[pl.ds(0, size)], x_buf, sem)
-        copy.start()
-        copy.wait()
+    def body(x_ref, k_ref, o_ref, x_buf, k_buf, sem):
+        copies = [pltpu.make_async_copy(k_ref, k_buf, sem.at[0])]
+        for g in range(size // 128):
+            at = pl.ds(g * 128, 128)
+            copies.append(pltpu.make_async_copy(x_ref.at[at], x_buf.at[at], sem.at[g + 1]))
+        for copy in copies:
+            copy.start()
+        copies[0].wait()
         for g in range(size // 128):
             at = slice(g * 128, (g + 1) * 128)
-            o_ref[at, :] = (jnp.exp(x_buf[at, :]) * column_mask(k_ref, g, spots)).astype(bf16)
-
-    return pl.pallas_call(
-        body,
-        in_specs=[HBM, VMEM],
+            copies[g + 1].wait()
+            o_ref[at, :] = (jnp.exp(x_buf[at, :]) * column_mask(k_buf, g, spots)).astype(bf16)
+
+    return pl.pallas_call(
+        body,
+        in_specs=[HBM, HBM],
         out_specs=VMEM,
         out_shape=shape((size, spots), bf16),
-        scratch_shapes=[pltpu.VMEM((size, spots), f32), pltpu.SemaphoreType.DMA],
+        scratch_shapes=[
+            pltpu.VMEM((size, spots), f32),
+            pltpu.VMEM(keep_rows.shape, jnp.int32),
+            pltpu.SemaphoreType.DMA((size // 128 + 1,)),
+        ],
         compiler_params=params(),
         cost_estimate=cost(0, 6 * size * spots),
         name="exp_first",
-    )(in_hbm(logits), keep_rows)
+    )(in_hbm(logits), in_hbm(keep_rows))
 
 
 def exp_call(logits, keep_rows, expression, ids, picks, sizes):
@@ -97,14 +107,17 @@
     block = expression.shape[1] // ids.shape[0]
     tile = 512
     steps = cells // tile
-    slots = min(4, steps)
+    slots = min(3, steps)
     starts = [sum(sizes[:c]) for c in range(len(sizes))]
     count = len(picks)
 
     def body(ids_ref, x_ref, k_ref, e_ref, *refs):
         piece_refs = (None, *refs[: len(sizes) - 1])
         all_ref, s_ref, *refs = refs[len(sizes) - 1 :]
-        o_refs, (u_buf, x_buf, held, sem, p_sem, a_sem, e_sem) = refs[:count], refs[count:]
+        o_refs, refs = refs[:count], refs[count:]
+        u_buf, x_buf, held, acc, k_buf, sem, p_sem, a_sem, e_sem, k_sem = refs
+        keep = pltpu.make_async_copy(k_ref, k_buf, k_sem)
+        keep.start()
 
         def fetch(t):
             return pltpu.make_async_copy(
@@ -113,25 +126,30 @@
 
         for t in range(slots):
             fetch(t).start()
-        copies = []
-        for q, pick in enumerate(picks):
-            at = pl.ds(pl.multiple_of(ids_ref[pick] * block, block), block)
-            copies.append(pltpu.make_async_copy(e_ref.at[:, at], held.at[q], e_sem.at[q]))
-            copies[q].start()
+        half = cells // 2
+
+        def hold(h, q):
+            at = pl.ds(pl.multiple_of(ids_ref[picks[q]] * block, block), block)
+            rows = pl.ds(h * half, half)
+            return pltpu.make_async_copy(e_ref.at[rows, at], held.at[q], e_sem.at[q])
+
+        for q in range(count):
+            hold(0, q).start()
         total = jnp.zeros((8, spots), f32)
         sent = []
+        keep.wait()
         for t in range(steps):
             fetch(t).wait()
             for g in range(tile // 128):
                 at = slice(t * tile + g * 128, t * tile + (g + 1) * 128)
                 rise = jnp.exp(x_buf[t % slots, g * 128 : (g + 1) * 128, :])
-                rise = rise * column_mask(k_ref, t * (tile // 128) + g, spots)
+                rise = rise * column_mask(k_buf, t * (tile // 128) + g, spots)
                 u_buf[at, :] = rise.astype(bf16)
                 total = total + jnp.sum(rise.reshape(16, 8, spots), axis=0)
             if t + slots < steps:
                 fetch(t + slots).start()
             for c in range(1, len(sizes)):
-                if starts[c] + sizes[c] == (t + 1) * tile:
+                if t * tile < starts[c] + sizes[c] <= (t + 1) * tile:
                     copy = pltpu.make_async_copy(
                         u_buf.at[pl.ds(starts[c], sizes[c])], piece_refs[c], p_sem.at[c]
                     )
@@ -142,13 +160,19 @@
                 copy = pltpu.make_async_copy(u_buf.at[at], all_ref.at[at], a_sem.at[t // 2])
                 copy.start()
                 sent.append(copy)
-        kept = jnp.full((1, spots), jnp.sum(k_ref[...].astype(f32)), f32)
+            if t == steps // 2 - 1:
+                for q in range(count):
+                    hold(0, q).wait()
+                    acc[q] = dot(held[q], u_buf[0:half, :], TN)
+                    hold(1, q).start()
+        kept = jnp.full((1, spots), jnp.sum(k_buf[...].astype(f32)), f32)
         total = jnp.sum(total, axis=0, keepdims=True)
         tops = jnp.concatenate([total, kept, jnp.zeros((6, spots), f32)], axis=0)
         s_ref[...] = tops
         for q in range(count):
-            copies[q].wait()
-            o_refs[q][0:block, :] = dot(held[q], u_buf[...], TN).astype(bf16)
+            hold(1, q).wait()
+            term = dot(held[q], u_buf[half:cells, :], TN)
+            o_refs[q][0:block, :] = (acc[q] + term).astype(bf16)
             if q == 0:
                 o_refs[0][block : block + 16, :] = packed(tops)
         for copy in sent:
@@ -156,7 +180,7 @@
 
     return pl.pallas_call(
         body,
-        in_specs=[SMEM, HBM, VMEM, HBM],
+        in_specs=[SMEM, HBM, HBM, HBM],
         out_specs=[HBM] * len(sizes) + [VMEM] * (1 + count),
         out_shape=[pltpu.HBM((size, spots), bf16) for size in (*sizes[1:], cells)]
         + [shape((8, spots), f32)]
@@ -164,16 +188,19 @@
         scratch_shapes=[
             pltpu.VMEM((cells, spots), bf16),
             pltpu.VMEM((slots, tile, spots), f32),
-            pltpu.VMEM((count, cells, block), bf16),
+            pltpu.VMEM((count, cells // 2, block), bf16),
+            pltpu.VMEM((count, block, spots), f32),
+            pltpu.VMEM(keep_rows.shape, jnp.int32),
             pltpu.SemaphoreType.DMA((slots,)),
             pltpu.SemaphoreType.DMA((len(sizes),)),
             pltpu.SemaphoreType.DMA((steps // 2,)),
             pltpu.SemaphoreType.DMA((count,)),
+            pltpu.SemaphoreType.DMA,
         ],
         compiler_params=params(),
         cost_estimate=cost(0, 8 * cells * spots),
         name="exp_rows",
-    )(ids, in_hbm(logits), keep_rows, in_hbm(expression))
+    )(ids, in_hbm(logits), in_hbm(keep_rows), in_hbm(expression))
 
 
 def part_call(expression, mapping, ids, picks, dtypes):
@@ -258,6 +285,21 @@
         cost_estimate=cost(0, 8 * block * spots),
         name="relay",
     )(*values, tops)
+
+
+def hold_call(value, others):
+    def body(*refs):
+        refs[-1][...] = refs[-2][...]
+
+    return pl.pallas_call(
+        body,
+        in_specs=[VMEM] * (1 + len(others)),
+        out_specs=VMEM,
+        out_shape=shape(value.shape, value.dtype),
+        compiler_params=params(),
+        cost_estimate=cost(0, 0),
+        name="hold",
+    )(*others, value)
 
 
 def total_of(tops_ref):
@@ -371,21 +413,26 @@
     cells, spots = mapping.shape
     slides = member.shape[0]
 
-    def body(d_ref, f_ref, k_ref, c_ref, u_ref, tops_ref, m_ref, o_ref, w_ref, e_ref):
+    def body(d_ref, f_ref, k_ref, c_ref, u_ref, tops_ref, m_ref, s_ref, w_ref, e_ref, o_ref, sem):
         keep = k_ref[...].astype(f32)
         kept = kept_of(tops_ref)
         total = total_of(tops_ref)
         safe = jnp.where(keep > 0, d_ref[...] + f_ref[...], 1.0)
         high, low = halves(-density_weight * keep / (kept * safe))
-        o_ref[...] = jnp.concatenate([high, high, low, jnp.zeros_like(low)], axis=0)
+        rest = jnp.concatenate([jnp.ones((8, cells), f32), jnp.zeros((96, cells), f32)], axis=0)
+        parts = [high.astype(f32), high.astype(f32), low.astype(f32), rest]
+        parts = jnp.concatenate(parts, axis=0)
         w_high, w_low = halves(m_ref[...] / total)
         w_ref[...] = jnp.concatenate([w_high, w_low, w_high, jnp.zeros_like(w_low)], axis=0)
         column = jnp.zeros((8, spots), f32)
         chunk = 256
         for r in range(cells // chunk):
             at = slice(r * chunk, (r + 1) * chunk)
-            pulled = dot(o_ref[:, at], w_ref[...], TN) * u_ref[at, :].astype(f32)
+            o_ref[at, :] = parts[:, at].T.astype(bf16)
+            pulled = dot(o_ref[at, 0:32], w_ref[...]) * u_ref[at, :].astype(f32)
             column += jnp.sum(pulled.reshape(chunk // 8, 8, spots), axis=0)
+        store = pltpu.make_async_copy(o_ref, s_ref, sem)
+        store.start()
         column = jnp.sum(column, axis=0, keepdims=True) / total
         logs = jnp.sum(jnp.log(safe), axis=0, keepdims=True)
         logs = -jnp.sum(logs, axis=1, keepdims=True)
@@ -401,16 +448,18 @@
             ],
             axis=0,
         )
+        store.wait()
 
     return pl.pallas_call(
         body,
         in_specs=[VMEM] * 7,
-        out_specs=[VMEM] * 3,
+        out_specs=[HBM, VMEM, VMEM],
         out_shape=[
-            shape((4 * slides, cells), bf16),
+            pltpu.HBM((cells, 128), bf16),
             shape((4 * slides, spots), bf16),
             shape((8, spots), f32),
         ],
+        scratch_shapes=[pltpu.VMEM((cells, 128), bf16), pltpu.SemaphoreType.DMA],
         compiler_params=params(),
         cost_estimate=cost(0, 2 * cells * spots),
         name="diverge",
@@ -423,11 +472,11 @@
     share = count * block // spread
 
     def body(ids_ref, place_ref, *refs):
-        b_refs, o_refs = refs[:count], refs[count : count + spread]
-        held, in_sem, out_sem = refs[count + spread :]
+        b_refs, all_ref, o_refs = refs[:count], refs[count], refs[count + 1 : count + 1 + spread]
+        in_sem, out_sem = refs[count + 1 + spread :]
 
         def rows(start, size):
-            return held.at[pl.ds(pl.multiple_of(start, size), size)]
+            return all_ref.at[pl.ds(pl.multiple_of(start, size), size)]
 
         copies = [
             pltpu.make_async_copy(b_refs[q], rows(ids_ref[q] * block, block), in_sem.at[q])
@@ -449,144 +498,196 @@
     return pl.pallas_call(
         body,
         in_specs=[SMEM, SMEM] + [ANY] * count,
-        out_specs=[HBM] * spread,
-        out_shape=[shape((share, spots), bf16)] * spread,
+        out_specs=[VMEM] + [HBM] * spread,
+        out_shape=[shape((count * block, spots), bf16)]
+        + [shape((share, spots), bf16)] * spread,
         scratch_shapes=[
-            pltpu.VMEM((count * block, spots), bf16),
             pltpu.SemaphoreType.DMA((count,)),
             pltpu.SemaphoreType.DMA((spread,)),
         ],
         compiler_params=params(),
         cost_estimate=cost(0, 4 * count * block * spots),
         name="regroup",
-    )(ids, place, *blocks)
-
-
-def logit_call(expression, blocks, ids, mapping, slope, weight, ends, tops):
+    )(ids, place, blocks[0], *[in_hbm(value) for value in blocks[1:]])
+
+
+def logit_call(expression, grad, mapping, slope, weight, ends, tops, slides):
     cells, genes = expression.shape
-    block, spots = blocks[0].shape
-    count = len(blocks)
-    tile = min(cells, 1024)
-
-    def body(ids_ref, e_ref, u_ref, d_ref, w_ref, ends_ref, tops_ref, *refs):
-        b_refs, (o_ref, held, sem) = refs[:count], refs[count:]
-
-        @pl.when(pl.program_id(0) == 0)
-        def _():
+    spots = grad.shape[1]
+    tile = min(cells, 512)
+    slots = 3
+    runs = [(row, tile) for row in range(0, cells, tile)]
+
+    def body(e_ref, g_ref, u_ref, d_ref, w_ref, ends_ref, tops_ref, *refs):
+        o_ref, l_ref, held, e_buf, u_buf, out, in_sem, out_sem = refs
+
+        def fetch(k):
+            row, size = runs[k]
             copies = []
-            for q in range(count):
-                at = pl.ds(pl.multiple_of(ids_ref[q] * block, block), block)
-                copies.append(pltpu.make_async_copy(b_refs[q], held.at[at], sem.at[q]))
-            for copy in copies:
-                copy.start()
-            for copy in copies:
-                copy.wait()
-
-        at = pl.ds(pl.multiple_of(pl.program_id(0) * tile, tile), tile)
-        acc = dot(e_ref[at, :], held[...])
-        acc += dot(d_ref[...], w_ref[...], TN) - ends_ref[0:1, :]
-        o_ref[...] = u_ref[at, :].astype(f32) * (acc * kept_of(tops_ref))
-
-    return pl.pallas_call(
-        body,
-        grid=(cells // tile,),
-        in_specs=[SMEM, VMEM, VMEM, pl.BlockSpec((slope.shape[0], tile), lambda i: (0, i))]
-        + [VMEM] * 3
-        + [ANY] * count,
-        out_specs=pl.BlockSpec((tile, spots), lambda i: (i, 0)),
-        out_shape=shape((cells, spots), f32),
-        scratch_shapes=[pltpu.VMEM((genes, spots), bf16), pltpu.SemaphoreType.DMA((count,))],
-        compiler_params=params(),
-        cost_estimate=cost(2 * cells * genes * spots, 2 * cells * genes + 6 * cells * spots),
-        name="grad_logits",
-    )(ids, expression, mapping, slope, weight, ends, tops, *blocks)
-
-
-def expr_call(base, mapping, chunks, grads, tops, start):
-    genes, spots = grads[0].shape
-    cells = base.shape[0] if mapping is None else mapping.shape[0]
-    own = 0 if mapping is None else 1
-    count = len(chunks[0])
-    tile = 512
-    tiles = [(c, t) for c in range(len(chunks)) for t in range(chunks[c][0].shape[0] // tile)]
-    slots = min(3, len(tiles))
-    flat = [v for chunk in chunks for v in chunk]
-
-    def body(*refs):
-        q_refs, refs = refs[: len(flat)], refs[len(flat) :]
-        g_refs, refs = refs[: len(grads)], refs[len(grads) :]
-        tops_ref, whole_ref, o_ref, held, whole, out, in_sem, whole_sem, out_sem = refs
-        scale = expression_scale * kept_of(tops_ref)
-
-        def fetch(k):
-            c, t = tiles[k]
-            copies = [
-                pltpu.make_async_copy(
-                    q_refs[c * count + q].at[pl.ds(t * tile, tile)],
-                    held.at[k % slots, q],
-                    in_sem.at[k % slots, q],
-                )
-                for q in range(count)
-            ]
-            at = pl.ds(start + k * tile, tile)
+            to = (k % slots, pl.ds(0, size))
             copies.append(
                 pltpu.make_async_copy(
-                    whole_ref.at[at], whole.at[k % slots], whole_sem.at[k % slots]
+                    e_ref.at[pl.ds(row, size)], e_buf.at[*to, pl.ds(0, genes)], in_sem.at[k % slots, 0]
+                )
+            )
+            copies.append(
+                pltpu.make_async_copy(
+                    u_ref.at[pl.ds(row, size)], u_buf.at[*to], in_sem.at[k % slots, 1]
+                )
+            )
+            copies.append(
+                pltpu.make_async_copy(
+                    d_ref.at[pl.ds(row, size)],
+                    e_buf.at[*to, pl.ds(genes, 128)],
+                    in_sem.at[k % slots, 2],
                 )
             )
             return copies
 
         def store(k):
+            row, size = runs[k]
             return pltpu.make_async_copy(
-                out.at[k % 2], o_ref.at[pl.ds(start + k * tile, tile)], out_sem.at[k % 2]
+                out.at[k % 2, pl.ds(0, size)], o_ref.at[pl.ds(row, size)], out_sem.at[k % 2]
+            )
+
+        for copy in fetch(0):
+            copy.start()
+        held[0:genes, :] = g_ref[...]
+        sums = jnp.concatenate([part.astype(f32) for part in thirds(-ends_ref[0:1, :])], axis=0)
+        sums = jnp.concatenate([sums, jnp.zeros((101, spots), f32)], axis=0)
+        weights = jnp.concatenate([w_ref[0:24, :].astype(f32), sums], axis=0)
+        held[genes : genes + 128, :] = weights.astype(bf16)
+        kept = kept_of(tops_ref)
+        total = density_weight * ends_ref[2:3, 0:1] - ends_ref[1:2, 0:1]
+        l_ref[...] = total / (genes * slides)
+        following = 1
+        for k, (row, size) in enumerate(runs):
+            for copy in fetch(k):
+                copy.wait()
+            while following < min(k + slots, len(runs)):
+                for copy in fetch(following):
+                    copy.start()
+                following += 1
+            if k >= 2:
+                store(k - 2).wait()
+            acc = dot(e_buf[k % slots, 0:size], held[...])
+            out[k % 2, 0:size] = (u_buf[k % slots, 0:size].astype(f32) * kept) * acc
+            store(k).start()
+        for k in range(len(runs) - 2, len(runs)):
+            store(k).wait()
+
+    return pl.pallas_call(
+        body,
+        in_specs=[HBM, VMEM, HBM, HBM] + [VMEM] * 3,
+        out_specs=[HBM, VMEM],
+        out_shape=[pltpu.HBM((cells, spots), f32), shape((1, 1), f32)],
+        scratch_shapes=[
+            pltpu.VMEM((genes + 128, spots), bf16),
+            pltpu.VMEM((slots, tile, genes + 128), bf16),
+            pltpu.VMEM((slots, tile, spots), bf16),
+            pltpu.VMEM((2, tile, spots), f32),
+            pltpu.SemaphoreType.DMA((slots, 3)),
+            pltpu.SemaphoreType.DMA((2,)),
+        ],
+        compiler_params=params(),
+        cost_estimate=cost(
+            2 * cells * genes * spots, 2 * cells * genes + 6 * cells * spots, 0.0
+        ),
+        name="grad_logits",
+    )(in_hbm(expression), grad, in_hbm(mapping), in_hbm(slope), weight, ends, tops)
+
+
+def expr_call(base, mapping, chunks, grads, tops):
+    genes, spots = grads[0].shape
+    cells = mapping.shape[0] if base is None else base.shape[0]
+    count = len(grads)
+    tile = 512
+    own = 0 if mapping is None else 1
+    tiles, c, row = [], 0, 0
+    for t in range(cells // tile):
+        runs, filled = [], 0
+        while filled < tile:
+            size = min(tile - filled, chunks[c][0].shape[0] - row)
+            runs.append((c, row, filled, size))
+            filled, row = filled + size, row + size
+            if row == chunks[c][0].shape[0]:
+                c, row = c + 1, 0
+        tiles.append(runs)
+    most = max(len(runs) for runs in tiles)
+    slots = 3
+    flat = [v for chunk in chunks for v in chunk]
+    far = count - own
+
+    def body(*refs):
+        q_refs, refs = refs[: len(flat)], refs[len(flat) :]
+        g_refs, refs = refs[:count], refs[count:]
+        tops_ref, whole_ref, o_ref, held, g_buf, out, in_sem, out_sem = refs
+        scale = expression_scale * kept_of(tops_ref)
+
+        def fetch(k):
+            pieces = [
+                (own + q, q_refs[c * far + q].at[pl.ds(row, size)], at, size, r)
+                for r, (c, row, at, size) in enumerate(tiles[k])
+                for q in range(far)
+            ]
+            if own:
+                pieces.append((0, whole_ref.at[pl.ds(k * tile, tile)], 0, tile, 0))
+            return [
+                pltpu.make_async_copy(
+                    source,
+                    held.at[k % slots, pl.ds(at, size), pl.ds(q * spots, spots)],
+                    in_sem.at[k % slots, q, r],
+                )
+                for q, source, at, size, r in pieces
+            ]
+
+        def store(k):
+            return pltpu.make_async_copy(
+                out.at[k % 2], o_ref.at[pl.ds(k * tile, tile)], out_sem.at[k % 2]
             )
 
         for k in range(slots):
             for copy in fetch(k):
                 copy.start()
+        for q in range(count):
+            g_buf[:, q * spots : (q + 1) * spots] = g_refs[q][...]
         for k in range(len(tiles)):
             for copy in fetch(k):
                 copy.wait()
-            total = dot(held[k % slots, 0], g_refs[own][...], NT)
-            for q in range(1, count):
-                total = total + dot(held[k % slots, q], g_refs[own + q][...], NT)
+            at = slice(k * tile, (k + 1) * tile)
             if own:
-                total = total + dot(whole[k % slots], g_refs[0][...], NT)
-            total = total * scale
-            if not own:
-                total = total + whole[k % slots]
-            if k >= 2:
-                store(k - 2).wait()
-            out[k % 2] = total
-            store(k).start()
+                o_ref[at, :] = dot(held[k % slots], g_buf[...], NT) * scale
+            else:
+                if k >= 2:
+                    store(k - 2).wait()
+                out[k % 2] = dot(held[k % slots], g_buf[...], NT) * scale + whole_ref[at, :]
+                store(k).start()
             if k + slots < len(tiles):
                 for copy in fetch(k + slots):
                     copy.start()
-        for k in range(max(len(tiles) - 2, 0), len(tiles)):
-            store(k).wait()
-
-    operands = [*flat, *grads, tops, in_hbm(mapping) if own else base]
+        if not own:
+            for k in range(len(tiles) - 2, len(tiles)):
+                store(k).wait()
+
     rows = len(tiles) * tile
     return pl.pallas_call(
         body,
-        in_specs=[ANY] * len(flat) + [VMEM] * (len(grads) + 1) + [HBM],
-        out_specs=HBM,
-        out_shape=pltpu.HBM((cells, genes), f32),
-        input_output_aliases={} if own else {len(operands) - 1: 0},
+        in_specs=[ANY] * len(flat) + [VMEM] * (count + 1) + [HBM if own else VMEM],
+        out_specs=VMEM if own else HBM,
+        out_shape=shape((cells, genes), f32) if own else pltpu.HBM((cells, genes), f32),
         scratch_shapes=[
-            pltpu.VMEM((slots, count, tile, spots), bf16),
-            pltpu.VMEM((slots, tile, spots if own else genes), bf16 if own else f32),
+            pltpu.VMEM((slots, tile, count * spots), bf16),
+            pltpu.VMEM((genes, count * spots), bf16),
             pltpu.VMEM((2, tile, genes), f32),
-            pltpu.SemaphoreType.DMA((slots, count)),
-            pltpu.SemaphoreType.DMA((slots,)),
+            pltpu.SemaphoreType.DMA((slots, count, most)),
             pltpu.SemaphoreType.DMA((2,)),
         ],
         compiler_params=params(),
         cost_estimate=cost(
-            2 * rows * spots * len(grads) * genes, 2 * rows * spots * len(grads) + 4 * rows * genes
+            2 * rows * spots * count * genes, 2 * rows * spots * count + 4 * rows * genes, 0.0
         ),
         name="grad_expression",
-    )(*operands)
+    )(*flat, *grads, tops, in_hbm(mapping) if own else base)
 
 
 def per_device(n, m, logits, expression, target, keep_mask, slide_ids, slide_counts):
@@ -602,10 +703,9 @@
     place = lax.axis_index("spot")
     core = place & 1
 
-    def across(value, k):
-        pairs = [
-            (i * m + j, (i ^ orders[j & 1][k]) * m + j) for i in range(n) for j in range(m)
-        ]
+    def across(value, *levels_of):
+        masks = [sum(order[k] for k in levels_of) for order in orders]
+        pairs = [(i * m + j, (i ^ masks[j & 1]) * m + j) for i in range(n) for j in range(m)]
         return lax.ppermute(value, ("cell", "spot"), pairs)
 
     def over_spot(value, mask):
@@ -622,20 +722,22 @@
             value = value + across(value, k)
         return value
 
-    def sum_spot(value, aside):
-        other = over_spot(value, 1)
+    def sum_spot(value):
+        first = aside = other = over_spot(value, 1)
         mask = 2
         while mask < m:
             value = value + other
-            if aside:
-                other = over_cell(over_cell(value, 1, 0), 1, mask)
-            else:
-                other = over_spot(value, mask)
+            first = value if mask == 2 else first
+            aside = over_cell(value, 1, 0)
+            other = over_cell(aside, 1, mask)
             mask *= 2
-        return value, other
+        return first, value, aside, other
 
     def tie(value, others):
         return lax.optimization_barrier((value, *others))[0]
+
+    def corner(value):
+        return value[:8, :128]
 
     last_out = []
 
@@ -670,8 +772,13 @@
     sizes = split_rows(cells)
     starts = [sum(sizes[:c]) for c in range(len(sizes))]
     pieces = [done(first_call(logits, keep_rows, sizes[0]))]
-    picks = [order[1, 1, 1], order[1, 0, 1]] if not lead and block % 128 == 0 else []
-    outs = exp_call(logits, after(keep_rows), expression, ids, picks, sizes)
+    pipelined = not lead and block % 128 == 0
+    one = jnp.where(core == 1, orders[1][0], orders[0][0])
+    masks = {"111": 7, "101": 4 + one, "diagonal": 3, "011": 7 - one, "001": 4, "z": 2, "x": 1, "own": 0}
+    part_ids = jnp.stack([me ^ mask for mask in masks.values()])
+    slot = {name: q for q, name in enumerate(masks)}
+    picks = [slot[name] for name in ("111", "101", "diagonal")] if pipelined else []
+    outs = exp_call(logits, after(keep_rows), expression, part_ids, picks, sizes)
     pieces += outs[: len(sizes) - 1]
     mapping, sums, *parts = outs[len(sizes) - 1 :]
     done(sums)
@@ -682,9 +789,9 @@
         for mask in range(2, m, 2):
             gathered[c, mask] = over_spot(piece, mask)
 
-    def spread(c):
+    def spread(c, others=()):
         for mask in range(2, m, 2):
-            gathered[c, mask + 1] = over_spot(gathered[c, mask], 1)
+            gathered[c, mask + 1] = over_spot(tie(gathered[c, mask], others), 1)
 
     def far(c):
         return [gathered[c, mask] for mask in range(2, m, 2)]
@@ -712,64 +819,59 @@
             step[0, 1, b] = across(part[0, 1, b], lead + 1)
         part[0, 0, 1] = add_call([part[0, 0, 1], got[1, 0, 1], step[0, 1, 1]])
         last = across(part[0, 0, 1], lead + 2)
+        terms = [part[0, 0, 0], got[1, 0, 0], step[0, 1, 0], last]
         send(1)
         send(2)
         spread(0)
     else:
-        part[1, 1, 1], part[1, 0, 1] = parts
-        got[1, 1, 1], got[1, 0, 1] = across(parts[0], 0), across(parts[1], 0)
-
-        def products(first, second, dtype, others):
-            picks = [order[first], order[second]]
-            here = after(ids, others)
-            return done(part_call(expression, mapping, here, picks, [dtype] * 2))
-
-        part[0, 1, 1], part[0, 0, 1] = products((0, 1, 1), (0, 0, 1), f32, [])
-        part[0, 1, 1], tops = done(
-            relay_call([after(part[0, 1, 1], far(0)), got[1, 1, 1]], sums)
+        got["111"], got["101"] = across(parts[0], 0), across(parts[1], 0)
+        got["diagonal"] = over_cell(parts[2], 2, 0)
+
+        def products(*some, late=()):
+            dtypes = [f32 if name in ("011", "001", "own") else bf16 for name in some]
+            picks = [slot[name] for name in some]
+            outs = done(part_call(expression, mapping, after(part_ids, late), picks, dtypes))
+            part.update(zip(some, outs))
+
+        products("011", "001", "z")
+        part["011"], tops = done(
+            relay_call([after(part["011"], [*far(0), got["101"], got["diagonal"]]), got["111"]], sums)
         )
-        send(1, [part[0, 1, 1]])
-        spread(0)
-        step[0, 1, 1] = across(part[0, 1, 1], 1)
-        part[1, 1, 0], part[1, 0, 0] = products((1, 1, 0), (1, 0, 0), bf16, [])
-        got[1, 1, 0], got[1, 0, 0] = across(part[1, 1, 0], 0), across(part[1, 0, 0], 0)
-        part[0, 0, 1], tops = done(
-            relay_call([after(part[0, 0, 1]), got[1, 0, 1], step[0, 1, 1]], tops)
+        got["011"] = across(part["011"], 1)
+        got["z"] = over_cell(part["z"], 2, 0)
+        send(1)
+        spread(0, [part["011"]])
+        products("x", "own", late=wide(0))
+        part["001"], tops = done(
+            relay_call([after(part["001"]), got["101"], got["011"]], tops)
         )
-        last = across(part[0, 0, 1], 2)
-        part[0, 1, 0], part[0, 0, 0] = products((0, 1, 0), (0, 0, 0), f32, [])
-        part[0, 1, 0] = done(add_call([after(part[0, 1, 0]), got[1, 1, 0]]))
-        step[0, 1, 0] = across(part[0, 1, 0], 1)
-        send(2, [part[0, 1, 0]])
+        last = over_cell(part["001"], 4, 0)
+        part["x"] = done(add_call([after(part["x"], [got["z"]]), got["diagonal"]]))
+        got["x"] = over_cell(part["x"], 1, 0)
+        send(2, [part["x"]])
+        terms = [part["own"], got["x"], got["z"], last]
     predicted, predicted_near, gene_sums, tops = done(
-        predicted_call(
-            [part[0, 0, 0], got[1, 0, 0], step[0, 1, 0], last],
-            tops,
-            target,
-            after(member, far(1) + wide(0)),
+        predicted_call(terms, tops, target, after(member))
+    )
+    _, gene_sums, _, far_sums = sum_spot(gene_sums)
+    grad, ends = done(
+        grad_call(
+            gene_sums, far_sums, predicted_near, target, tops, after(member, far(1))
         )
     )
-    gene_sums, far_sums = sum_spot(gene_sums, True)
+
+    have = {(0, 0, 0): grad}
+    for k in range(3):
+        have[tuple(int(q == k) for q in range(3))] = across(grad, lead + k)
     density = done(density_call(mapping, tops, after(member)))
-    density, far_density = sum_spot(density, True)
-    beside = over_spot(tie(mapping, [density]), 1)
-    grad, ends = done(
-        grad_call(gene_sums, far_sums, predicted_near, target, tops, after(member))
+    _, density, _, far_density = sum_spot(density)
+    have[0, 0, 1] = hold_call(
+        have[0, 0, 1],
+        [far_density, have[1, 0, 0], have[0, 1, 0]],
     )
-    send(3, [grad])
-
-    have = {(0, 0, 0): grad}
-    for k in (2, 1, 0):
-        for code in list(have):
-            other = tuple(1 if q == k else b for q, b in enumerate(code))
-            have[other] = across(have[code], lead + k)
-    tail = codes((0,) * lead)
-    blocks = [have[c[lead:]] for c in tail]
-    if lead:
-        blocks = jnp.stack(blocks)
-        for k in reversed(range(lead)):
-            blocks = jnp.concatenate([across(blocks, k), blocks])
-        blocks = [blocks[q] for q in range(n)]
+    have[1, 1, 0] = across(have[0, 1, 0], lead)
+    have[0, 1, 1] = across(have[0, 0, 1], lead + 1)
+    have[1, 0, 1] = across(have[0, 0, 1], lead)
 
     slope, weight, more = done(
         diverge_call(
@@ -779,40 +881,46 @@
             slide_counts[None, :],
             mapping,
             tops,
-            after(member, [have[0, 1, 0], beside]),
+            after(member, [have[0, 0, 1]]),
         )
     )
-    ends = sum_cell(ends + more)
-    mapping_loss = (-ends[1, 0] + density_weight * ends[2, 0]) / (slide_total * genes)
-
-    spread(1)
-    shares = done(regroup_call(blocks, after(ids, far(2)), place[None], m))
-    spread(2)
-    regrouped = [None] * m
-    for mask in range(0, m, 2):
-        regrouped[mask] = over_spot(shares[mask], mask) if mask else shares[0]
-        other = over_spot(shares[mask + 1], mask) if mask else shares[1]
-        regrouped[mask + 1] = over_spot(other, 1)
-
-    grad_logits = done(
+    ends = ends + more
+    ends = ends + across(ends, 0)
+    have[0, 1, 1] = hold_call(
+        have[0, 1, 1], [*[corner(v) for v in far(2)], have[1, 1, 0], have[1, 0, 1], ends]
+    )
+    send(3, [have[0, 1, 1]])
+    spread(1, [have[0, 1, 1]])
+    spread(2, [have[0, 1, 1]])
+    have[1, 1, 1] = across(have[0, 1, 1], lead)
+    ends = ends + across(ends, 1)
+    most = ends
+    for k in range(2, levels):
+        ends = ends + across(ends, k)
+    tail = codes((0,) * lead)
+    blocks = [have[c[lead:]] for c in tail]
+    if lead:
+        blocks = jnp.stack(blocks)
+        for k in reversed(range(lead)):
+            blocks = jnp.concatenate([across(blocks, k), blocks])
+        blocks = [blocks[q] for q in range(n)]
+
+    whole_grad, *shares = regroup_call(blocks, after(ids, [ends, *far(3), *wide(1), *wide(2)]), place[None], m)
+    done(shares)
+    regrouped = [over_spot(value, mask) if mask else value for mask, value in enumerate(shares)]
+    beside = over_spot(tie(mapping, shares), 1)
+    spread(3, shares)
+    grad_logits, loss = done(
         logit_call(
-            expression,
-            blocks,
-            ids,
-            mapping,
-            slope,
-            weight,
-            after(ends, [*wide(1), *wide(2), regrouped[1]]),
-            tops,
+            expression, whole_grad, mapping, slope, weight, after(ends), tops, slide_total
         )
     )
     near_part = done(
-        expr_call(None, mapping, [[beside]], regrouped[:2], after(tops, far(3)), 0)
+        expr_call(None, mapping, [[beside]], regrouped[:2], after(tops))
     )
-    spread(3)
     rest = [[gathered[c, mask] for mask in range(2, m)] for c in range(4)]
-    grad_expression = expr_call(near_part, None, rest, regrouped[2:], after(tops), 0)
-    return (mapping_loss, predicted, grad_logits, grad_expression)
+    grad_expression = expr_call(near_part, None, rest, regrouped[2:], after(tops))
+    return (loss.reshape(()), predicted, grad_logits, grad_expression)
 
 
 def solution(mesh):

time: 165 us -> 147 us (0.89)
  waiting for transfers between devices: 64.3 us -> 40.7 us
  starting transfers between devices: 31 us -> 37.7 us
  between operations: 3.36 us -> 1.21 us
    ppermute x15 -> x14, waiting for transfers between devices: 21.6 us -> 1.35 us  [over_spot(): return lax.ppermute(value, 'spot', [(j, j ^ mask) for j in range(m)])]
    ppermute x17 -> x13, waiting for transfers between devices: 29.4 us -> 10 us  [across(): return lax.ppermute(value, ('cell', 'spot'), pairs)]
    ppermute x4 -> x8, waiting for transfers between devices: 13.3 us -> 29.3 us  [over_cell(): return lax.ppermute(value, ('cell', 'spot'), pairs)]
    ppermute x4 -> x8, starting transfers between devices: 3.62 us -> 8.82 us  [over_cell(): return lax.ppermute(value, ('cell', 'spot'), pairs)]
    pallas_call x7 -> x9, Pallas kernels: 44.7 us -> 49 us  [the longest x2 16 us: expr_call(): pl.pallas_call(body, in_specs=[ANY] * len(flat) + [VMEM] * (count + 1) +...]
    pallas_call x3 -> x2, Pallas kernels: 14.6 us -> 10.9 us  [part_call(): pl.pallas_call(body, in_specs=[SMEM, HBM, VMEM], out_specs=[VMEM] * count...]
    ppermute x15 -> x14, starting transfers between devices: 8.2 us -> 10.6 us  [over_spot(): return lax.ppermute(value, 'spot', [(j, j ^ mask) for j in range(m)])]
    unnamed x28 -> x36, local copies, waits for them, and re-layouts: 2.95 us -> 3.97 us
  transfers between devices with their start and end apart: 36 -> 35, of which waited for: 18 -> 14; matrix products, arithmetic and copies ran while one was open for 0% -> 0% of each run, Pallas kernels for 30% -> 34%
where the time goes in v4:
time: 147 us
  Pallas kernels  63.5 us (43%)
  waiting for transfers between devices  40.7 us (28%)
  starting transfers between devices  37.7 us (26%)
  local copies, waits for them, and re-layouts  4.14 us (3%)
    ppermute x8, waiting for transfers between devices, over_cell(): return lax.ppermute(value, ('cell', 'spot'), pairs)  29.3 us
    ppermute x13, starting transfers between devices, across(): return lax.ppermute(value, ('cell', 'spot'), pairs)  18.3 us
    pallas_call x2, Pallas kernels, expr_call(): pl.pallas_call(body, in_specs=[ANY] * len(flat) + [VMEM] * (count + 1) +...  16 us
    pallas_call x1, Pallas kernels, logit_call(): pl.pallas_call(body, in_specs=[HBM, VMEM, HBM, HBM] + [VMEM] * 3, out_spe...  14.7 us
    pallas_call x1, Pallas kernels, exp_call(): pl.pallas_call(body, in_specs=[SMEM, HBM, HBM, HBM], out_specs=[HBM] * le...  11 us
    pallas_call x2, Pallas kernels, part_call(): pl.pallas_call(body, in_specs=[SMEM, HBM, VMEM], out_specs=[VMEM] * count...  10.9 us
    ppermute x14, starting transfers between devices, over_spot(): return lax.ppermute(value, 'spot', [(j, j ^ mask) for j in range(m)])  10.6 us
    ppermute x13, waiting for transfers between devices, across(): return lax.ppermute(value, ('cell', 'spot'), pairs)  10 us
  transfers between devices with their start and end apart: 35, of which 14 were waited for; matrix products, arithmetic and copies ran while one was open for 0% of the time, Pallas kernels for 34%

profile of v4, /device:TPU:0, one launch (start us, length us, event | category | flops | bytes accessed | tf_op | source)
XLA Modules:
  0.0 147.2 jit_solution(8833562683238973096)
XLA Ops:
  0.6 1.9 %exp_first.1 = bf16[1024,512]{1,0:T(8,128)(2,1)S(1)} custom-call(f32[4096,512]{1,0:T(8,128)} %x_ref.3, s32[32,128]{1,0:T(8,128)} %bitcast.19), custom_call_target="tpu_custom_call" | custom-call | bytes 157286 | tf_op jit(solution)/shard_map/exp_first/pallas_call | solution.py:89
  2.5 3.0 %collective-permute-start = (bf16[1024,512]{1,0:T(8,128)(2,1)S(1)}, bf16[1024,512]{1,0:T(8,128)(2,1)S(1)}, u32[]{:S(2)}, u32[]{:S(2)}) collective-permute-start(bf16[1024,512]{1,0:T(8,128)(2,1)S(1)} %exp_first.1), channel_id=1, source_target_pairs={{0,2},{1,3},{2,0},{3,1},{4,6},{5,7},{6,4},{7,5},{8,10},{9,11},{10,... | collective-permute-start | bytes 3145736 | tf_op jit(solution)/shard_map/ppermute | solution.py:712
  5.6 11.0 %exp_rows.1 = (bf16[1280,512]{1,0:T(8,128)(2,1)}, bf16[1536,512]{1,0:T(8,128)(2,1)}, bf16[256,512]{1,0:T(8,128)(2,1)}, bf16[4096,512]{1,0:T(8,128)(2,1)}, f32[8,...) custom-call(s32[8]{0:T(128)S(1)} %stack.65.ids_ref, ...), custom_call_target="tpu_custom_call" | custom-call | bytes 838860 | tf_op jit(solution)/shard_map/exp_rows/pallas_call | solution.py:181
  20.1 2.2 %copy-done = bf16[4096,512]{1,0:T(8,128)(2,1)S(1)} copy-done((bf16[4096,512]{1,0:T(8,128)(2,1)S(1)}, bf16[4096,512]{1,0:T(8,128)(2,1)}, u32[]{:S(2)}) %copy-start) | copy-done | bytes 4194328
  22.3 6.2 %part.2 = (f32[256,512]{1,0:T(8,128)S(1)}, f32[256,512]{1,0:T(8,128)S(1)}, bf16[256,512]{1,0:T(8,128)(2,1)S(1)}) custom-call(s32[8]{0:T(128)S(1)} %stack.65.ids_ref, bf16[4096,2048]{1,0:T(8,128)(2,1)} %e_ref.7, bf16[4096,512]{1,0:T(8,128)(2,1)S(1)} %copy-done), custom_call_target="tpu_custom_call" | custom-call | flops 161061280 | bytes 524288 | tf_op jit(solution)/shard_map/part/pallas_call | solution.py:222
  30.8 1.6 %collective-permute-start.5 = (bf16[272,512]{1,0:T(8,128)(2,1)S(1)}, bf16[272,512]{1,0:T(8,128)(2,1)S(1)}, u32[]{:S(2)}, u32[]{:S(2)}) collective-permute-start(bf16[272,512]{1,0:T(8,128)(2,1)S(1)} %get-tuple-element.67), channel_id=1, source_target_pairs={{0,8},{1,5},{2,10},{3,7},{4,12},{5,1},{6,14},{7,3},{8,0},{9,13},{1... | collective-permute-start | bytes 835592 | tf_op jit(solution)/shard_map/ppermute | solution.py:709
  33.8 4.7 %part.3 = (bf16[256,512]{1,0:T(8,128)(2,1)S(1)}, f32[256,512]{1,0:T(8,128)S(1)}) custom-call(s32[8]{0:T(128)S(1)} %stack.65.ids_ref, bf16[4096,2048]{1,0:T(8,128)(2,1)} %e_ref.7, bf16[4096,512]{1,0:T(8,128)(2,1)S(1)} %copy-done.1), custom_call_target="tpu_custom_call" | custom-call | flops 107374184 | bytes 419430 | tf_op jit(solution)/shard_map/part/pallas_call | solution.py:222
  40.1 2.9 %collective-permute-done.6.refs_2_ = bf16[256,512]{1,0:T(8,128)(2,1)S(1)} collective-permute-done((bf16[256,512]{1,0:T(8,128)(2,1)S(1)}, bf16[256,512]{1,0:T(8,128)(2,1)S(1)}, u32[]{:S(2)}, u32[]{:S(2)}) %collective-permute-start.6) | collective-permute-done | bytes 262176 | tf_op jit(solution)/shard_map/ppermute | solution.py:718
  43.0 1.5 %collective-permute-start.22 = (bf16[1536,512]{1,0:T(8,128)(2,1)S(1)}, bf16[1536,512]{1,0:T(8,128)(2,1)S(1)}, u32[]{:S(2)}, u32[]{:S(2)}) collective-permute-start(bf16[1536,512]{1,0:T(8,128)(2,1)S(1)} %copy-done.16), channel_id=1, source_target_pairs={{0,2},{1,3},{2,0},{3,1},{4,6},{5,7},{6,4},{7,5},{8,10},{9,11},{10,... | collective-permute-start | bytes 4718600 | tf_op jit(solution)/shard_map/ppermute | solution.py:712
  44.5 2.7 %collective-permute-start.8 = (bf16[272,512]{1,0:T(8,128)(2,1)S(1)}, bf16[272,512]{1,0:T(8,128)(2,1)S(1)}, u32[]{:S(2)}, u32[]{:S(2)}) collective-permute-start(bf16[272,512]{1,0:T(8,128)(2,1)S(1)} %get-tuple-element.75), channel_id=1, source_target_pairs={{0,16},{1,17},{2,18},{3,19},{4,20},{5,21},{6,22},{7,23},{8,24},{9,... | collective-permute-start | bytes 835592 | tf_op jit(solution)/shard_map/ppermute | solution.py:718
  47.9 5.6 %collective-permute-done.7.refs_1_ = bf16[256,512]{1,0:T(8,128)(2,1)S(1)} collective-permute-done((bf16[256,512]{1,0:T(8,128)(2,1)S(1)}, bf16[256,512]{1,0:T(8,128)(2,1)S(1)}, u32[]{:S(2)}, u32[]{:S(2)}) %collective-permute-start.7) | collective-permute-done | bytes 262176 | tf_op jit(solution)/shard_map/ppermute | solution.py:718
  53.5 3.4 %collective-permute-done.8.refs_3_ = bf16[272,512]{1,0:T(8,128)(2,1)S(1)} collective-permute-done((bf16[272,512]{1,0:T(8,128)(2,1)S(1)}, bf16[272,512]{1,0:T(8,128)(2,1)S(1)}, u32[]{:S(2)}, u32[]{:S(2)}) %collective-permute-start.8) | collective-permute-done | bytes 278560 | tf_op jit(solution)/shard_map/ppermute | solution.py:718
  59.3 3.8 %collective-permute-done.10 = f32[24,256]{1,0:T(8,128)S(1)} collective-permute-done((f32[24,256]{1,0:T(8,128)S(1)}, f32[24,256]{1,0:T(8,128)S(1)}, u32[]{:S(2)}, u32[]{:S(2)}) %collective-permute-start.10) | collective-permute-done | bytes 24608 | tf_op jit(solution)/shard_map/ppermute | solution.py:718
  63.4 4.5 %collective-permute-done.11.f_ref = f32[24,256]{1,0:T(8,128)S(1)} collective-permute-done((f32[24,256]{1,0:T(8,128)S(1)}, f32[24,256]{1,0:T(8,128)S(1)}, u32[]{:S(2)}, u32[]{:S(2)}) %collective-permute-start.11) | collective-permute-done | bytes 24608 | tf_op jit(solution)/shard_map/ppermute | solution.py:718
  68.6 1.5 %density.1 = f32[8,4096]{1,0:T(8,128)S(1)} custom-call(bf16[4096,512]{1,0:T(8,128)(2,1)S(1)} %copy-done.1, f32[8,512]{1,0:T(8,128)S(1)} %get-tuple-element.111.tops_ref.refs_3_.refs_10_, f32[8,512]{1,0:T(8,128)S(1)} %fusion.refs_6_.m_ref), custom_call_target="tpu_custom_call" | custom-call | bytes 209715 | tf_op jit(solution)/shard_map/density/pallas_call | solution.py:401
  70.2 4.1 %collective-permute-start.17 = (bf16[256,512]{1,0:T(8,128)(2,1)S(1)}, bf16[256,512]{1,0:T(8,128)(2,1)S(1)}, u32[]{:S(2)}, u32[]{:S(2)}) collective-permute-start(bf16[256,512]{1,0:T(8,128)(2,1)S(1)} %get-tuple-element.86.refs_7_), channel_id=1, source_target_pairs={{0,8},{1,5},{2,10},{3,7},{4,12},{5,1},{6,14},{7,3},{8,0},{9,13},{1... | collective-permute-start | bytes 786440 | tf_op jit(solution)/shard_map/ppermute | solution.py:709
  74.3 2.1 %collective-permute-start.14 = (f32[8,4096]{1,0:T(8,128)S(1)}, f32[8,4096]{1,0:T(8,128)S(1)}, u32[]{:S(2)}, u32[]{:S(2)}) collective-permute-start(f32[8,4096]{1,0:T(8,128)S(1)} %add.23.d_ref), channel_id=1, source_target_pairs={{0,4},{1,5},{2,6},{3,7},{4,0},{5,1},{6,2},{7,3},{8,12},{9,13},{10,... | collective-permute-start | bytes 393224 | tf_op jit(solution)/shard_map/ppermute | solution.py:718
  76.4 6.1 %collective-permute-done.14 = f32[8,4096]{1,0:T(8,128)S(1)} collective-permute-done((f32[8,4096]{1,0:T(8,128)S(1)}, f32[8,4096]{1,0:T(8,128)S(1)}, u32[]{:S(2)}, u32[]{:S(2)}) %collective-permute-start.14) | collective-permute-done | bytes 131104 | tf_op jit(solution)/shard_map/ppermute | solution.py:718
  83.8 1.8 %collective-permute-done.17.refs_2_.refs_5_ = bf16[256,512]{1,0:T(8,128)(2,1)S(1)} collective-permute-done((bf16[256,512]{1,0:T(8,128)(2,1)S(1)}, bf16[256,512]{1,0:T(8,128)(2,1)S(1)}, u32[]{:S(2)}, u32[]{:S(2)}) %collective-permute-start.17) | collective-permute-done | bytes 262176 | tf_op jit(solution)/shard_map/ppermute | solution.py:709
  85.6 2.9 %collective-permute-done.15.refs_0_.f_ref = f32[8,4096]{1,0:T(8,128)S(1)} collective-permute-done((f32[8,4096]{1,0:T(8,128)S(1)}, f32[8,4096]{1,0:T(8,128)S(1)}, u32[]{:S(2)}, u32[]{:S(2)}) %collective-permute-start.15) | collective-permute-done | bytes 131104 | tf_op jit(solution)/shard_map/ppermute | solution.py:718
  88.6 2.9 %collective-permute-start.25 = (bf16[256,512]{1,0:T(8,128)(2,1)S(1)}, bf16[256,512]{1,0:T(8,128)(2,1)S(1)}, u32[]{:S(2)}, u32[]{:S(2)}) collective-permute-start(bf16[256,512]{1,0:T(8,128)(2,1)S(1)} %hold.2.refs_6_), channel_id=1, source_target_pairs={{0,8},{1,5},{2,10},{3,7},{4,12},{5,1},{6,14},{7,3},{8,0},{9,13},{1... | collective-permute-start | bytes 786440 | tf_op jit(solution)/shard_map/ppermute | solution.py:709
  91.9 2.3 %diverge.1 = (bf16[4096,128]{1,0:T(8,128)(2,1)}, bf16[32,512]{1,0:T(8,128)(2,1)S(1)}, f32[8,512]{1,0:T(8,128)S(1)}) custom-call(f32[8,4096]{1,0:T(8,128)S(1)} %add.23.d_ref, f32[8,4096]{1,0:T(8,128)S(1)} %collective-permute-done.15.refs_0_.f_ref, s32[1,4096]{1,0:T(1,128)S(1)} %bitcast.21, s32[1,8]{1,0:T(1,128)S(1)} %bitcast.22, ...), custom_call_target="tpu_custom_call" | custom-call | bytes 209715 | tf_op jit(solution)/shard_map/diverge/pallas_call | solution.py:453
  94.3 1.7 %collective-permute-start.19 = (f32[8,512]{1,0:T(8,128)S(1)}, f32[8,512]{1,0:T(8,128)S(1)}, u32[]{:S(2)}, u32[]{:S(2)}) collective-permute-start(f32[8,512]{1,0:T(8,128)S(1)} %add.24), channel_id=1, source_target_pairs={{0,4},{1,9},{2,6},{3,11},{4,0},{5,13},{6,2},{7,15},{8,12},{9,1},{1... | collective-permute-start | bytes 49160 | tf_op jit(solution)/shard_map/ppermute | solution.py:709
  96.0 2.1 %collective-permute-done.19 = f32[8,512]{1,0:T(8,128)S(1)} collective-permute-done((f32[8,512]{1,0:T(8,128)S(1)}, f32[8,512]{1,0:T(8,128)S(1)}, u32[]{:S(2)}, u32[]{:S(2)}) %collective-permute-start.19) | collective-permute-done | bytes 16416 | tf_op jit(solution)/shard_map/ppermute | solution.py:709
  101.0 1.6 %collective-permute-start.29 = (bf16[256,512]{1,0:T(8,128)(2,1)}, bf16[256,512]{1,0:T(8,128)(2,1)}, u32[]{:S(2)}, u32[]{:S(2)}) collective-permute-start(bf16[256,512]{1,0:T(8,128)(2,1)} %hold.3.refs_4_), channel_id=1, source_target_pairs={{0,4},{1,9},{2,6},{3,11},{4,0},{5,13},{6,2},{7,15},{8,12},{9,1},{1... | collective-permute-start | bytes 786440 | tf_op jit(solution)/shard_map/ppermute | solution.py:709
  104.0 2.6 %collective-permute-done.20 = f32[8,512]{1,0:T(8,128)S(1)} collective-permute-done((f32[8,512]{1,0:T(8,128)S(1)}, f32[8,512]{1,0:T(8,128)S(1)}, u32[]{:S(2)}, u32[]{:S(2)}) %collective-permute-start.20) | collective-permute-done | bytes 16416 | tf_op jit(solution)/shard_map/ppermute | solution.py:709
  106.5 2.4 %collective-permute-start.21 = (f32[8,512]{1,0:T(8,128)S(1)}, f32[8,512]{1,0:T(8,128)S(1)}, u32[]{:S(2)}, u32[]{:S(2)}) collective-permute-start(f32[8,512]{1,0:T(8,128)S(1)} %add.26), channel_id=1, source_target_pairs={{0,16},{1,17},{2,18},{3,19},{4,20},{5,21},{6,22},{7,23},{8,24},{9,... | collective-permute-start | bytes 49160 | tf_op jit(solution)/shard_map/ppermute | solution.py:709
  109.0 2.1 %collective-permute-done.21 = f32[8,512]{1,0:T(8,128)S(1)} collective-permute-done((f32[8,512]{1,0:T(8,128)S(1)}, f32[8,512]{1,0:T(8,128)S(1)}, u32[]{:S(2)}, u32[]{:S(2)}) %collective-permute-start.21) | collective-permute-done | bytes 16416 | tf_op jit(solution)/shard_map/ppermute | solution.py:709
  111.2 2.3 %regroup.1 = (bf16[2048,512]{1,0:T(8,128)(2,1)S(1)}, bf16[512,512]{1,0:T(8,128)(2,1)S(1)}, bf16[512,512]{1,0:T(8,128)(2,1)S(1)}, bf16[512,512]{1,0:T(8,128)(2,1)S(1)}, bf16[512,512]{1,0:T(8,128)(2,1)S(1)}) custom-call(s32[8]{0:T(128)S(1)} %stack.58.ids_ref, s32[1]{0:T(128)} %bitcast.17.place_ref, bf16[256,512]{1,0:T(8,128)(2,1)} %collective-permute-done.29.refs_0_, ...), custom_call_target="tpu_custom_call" | custom-call | bytes 209715 | tf_op jit(solution)/shard_map/regroup/pallas_call | solution.py:498
  116.2 14.7 %grad_logits.1 = (f32[4096,512]{1,0:T(8,128)}, f32[1,1]{1,0:T(1,128)}) custom-call(bf16[4096,2048]{1,0:T(8,128)(2,1)} %e_ref.7, bf16[2048,512]{1,0:T(8,128)(2,1)S(1)} %get-tuple-element.99.g_ref, bf16[4096,512]{1,0:T(8,128)(2,1)} %get-tuple-element.109.u_ref.refs_4_, bf16[4096,128]{1,0:T(8,128)(2,1)} %get-tuple-element.89.d_ref, ...), custom_call_target="tpu_custom_call" | custom-call | tf_op jit(solution)/shard_map/grad_logits/pallas_call | solution.py:579
  131.0 7.7 %grad_expression.2.refs_11_ = f32[4096,512]{1,0:T(8,128)S(1)} custom-call(bf16[4096,512]{1,0:T(8,128)(2,1)S(1)} %collective-permute-done.33.refs_0_, bf16[512,512]{1,0:T(8,128)(2,1)S(1)} %get-tuple-element.101.refs_1_, bf16[512,512]{1,0:T(8,128)(2,1)S(1)} %collective-permute-done.34.refs_2_, f32[8,512]{1,0:T(8,128)S(1)} %get-tuple-element.111.tops_ref.refs_3_.refs_10_, ...), custom_call_target="tpu_custom_call" | custom-call | tf_op jit(solution)/shard_map/grad_expression/pallas_call | solution.py:673
  138.7 8.3 %grad_expression.3 = f32[4096,512]{1,0:T(8,128)} custom-call(bf16[1024,512]{1,0:T(8,128)(2,1)S(1)} %copy-done.4, bf16[1024,512]{1,0:T(8,128)(2,1)S(1)} %copy-done.6, bf16[1280,512]{1,0:T(8,128)(2,1)} %collective-permute-done.12.refs_2_, bf16[1280,512]{1,0:T(8,128)(2,1)} %collective-permute-done.27.refs_3_, ...), custom_call_target="tpu_custom_call" | custom-call | tf_op jit(solution)/shard_map/grad_expression/pallas_call | solution.py:673
  (101 shorter events, 21.7 us)
Async XLA Ops:
  2.5 26.2 %collective-permute-start = (bf16[1024,512]{1,0:T(8,128)(2,1)S(1)}, bf16[1024,512]{1,0:T(8,128)(2,1)S(1)}, u32[]{:S(2)}, u32[]{:S(2)}) collective-permute-start(bf16[1024,512]{1,0:T(8,128)(2,1)S(1)} %exp_first.1), channel_id=1, source_target_pairs={{0,2},{1,3},{2,0},{3,1},{4,6},{5,7},{6,4},{7,5},{8,10},{9,11},{10,... | collective-permute-start | bytes 3145736 | tf_op jit(solution)/shard_map/ppermute | solution.py:712
  16.7 12.1 %collective-permute-start.3 = (bf16[272,512]{1,0:T(8,128)(2,1)S(1)}, bf16[272,512]{1,0:T(8,128)(2,1)S(1)}, u32[]{:S(2)}, u32[]{:S(2)}) collective-permute-start(bf16[272,512]{1,0:T(8,128)(2,1)S(1)} %get-tuple-element.66), channel_id=1, source_target_pairs={{0,4},{1,9},{2,6},{3,11},{4,0},{5,13},{6,2},{7,15},{8,12},{9,1},{1... | collective-permute-start | bytes 835592 | tf_op jit(solution)/shard_map/ppermute | solution.py:709
  18.0 10.6 %collective-permute-start.1 = (bf16[256,512]{1,0:T(8,128)(2,1)S(1)}, bf16[256,512]{1,0:T(8,128)(2,1)S(1)}, u32[]{:S(2)}, u32[]{:S(2)}) collective-permute-start(bf16[256,512]{1,0:T(8,128)(2,1)S(1)} %get-tuple-element.63), channel_id=1, source_target_pairs={{0,4},{1,9},{2,6},{3,11},{4,0},{5,13},{6,2},{7,15},{8,12},{9,1},{1... | collective-permute-start | bytes 786440 | tf_op jit(solution)/shard_map/ppermute | solution.py:709
  18.8 9.8 %collective-permute-start.2 = (bf16[256,512]{1,0:T(8,128)(2,1)S(1)}, bf16[256,512]{1,0:T(8,128)(2,1)S(1)}, u32[]{:S(2)}, u32[]{:S(2)}) collective-permute-start(bf16[256,512]{1,0:T(8,128)(2,1)S(1)} %get-tuple-element.64), channel_id=1, source_target_pairs={{0,8},{1,9},{2,10},{3,11},{4,12},{5,13},{6,14},{7,15},{8,0},{9,1},... | collective-permute-start | bytes 786440 | tf_op jit(solution)/shard_map/ppermute | solution.py:718
  28.8 4.0 %collective-permute-start.4 = (bf16[1024,512]{1,0:T(8,128)(2,1)S(1)}, bf16[1024,512]{1,0:T(8,128)(2,1)S(1)}, u32[]{:S(2)}, u32[]{:S(2)}) collective-permute-start(bf16[1024,512]{1,0:T(8,128)(2,1)S(1)} %collective-permute-done.refs_0_), channel_id=1, source_target_pairs={{0,1},{1,0},{2,3},{3,2},{4,5},{5,4},{6,7},{7,6},{8,9},{9,8},{10,11... | collective-permute-start | bytes 3145736 | tf_op jit(solution)/shard_map/ppermute | solution.py:712
  30.3 33.2 %collective-permute-start.12 = (bf16[1280,512]{1,0:T(8,128)(2,1)S(1)}, bf16[1280,512]{1,0:T(8,128)(2,1)}, u32[]{:S(2)}, u32[]{:S(2)}) collective-permute-start(bf16[1280,512]{1,0:T(8,128)(2,1)S(1)} %copy-done.17), channel_id=1, source_target_pairs={{0,2},{1,3},{2,0},{3,1},{4,6},{5,7},{6,4},{7,5},{8,10},{9,11},{10,... | collective-permute-start | bytes 3932168 | tf_op jit(solution)/shard_map/ppermute | solution.py:712
  30.8 9.2 %collective-permute-start.5 = (bf16[272,512]{1,0:T(8,128)(2,1)S(1)}, bf16[272,512]{1,0:T(8,128)(2,1)S(1)}, u32[]{:S(2)}, u32[]{:S(2)}) collective-permute-start(bf16[272,512]{1,0:T(8,128)(2,1)S(1)} %get-tuple-element.67), channel_id=1, source_target_pairs={{0,8},{1,5},{2,10},{3,7},{4,12},{5,1},{6,14},{7,3},{8,0},{9,13},{1... | collective-permute-start | bytes 835592 | tf_op jit(solution)/shard_map/ppermute | solution.py:709
  32.3 10.6 %collective-permute-start.6 = (bf16[256,512]{1,0:T(8,128)(2,1)S(1)}, bf16[256,512]{1,0:T(8,128)(2,1)S(1)}, u32[]{:S(2)}, u32[]{:S(2)}) collective-permute-start(bf16[256,512]{1,0:T(8,128)(2,1)S(1)} %get-tuple-element.76), channel_id=1, source_target_pairs={{0,8},{1,9},{2,10},{3,11},{4,12},{5,13},{6,14},{7,15},{8,0},{9,1},... | collective-permute-start | bytes 786440 | tf_op jit(solution)/shard_map/ppermute | solution.py:718
  43.0 55.1 %collective-permute-start.22 = (bf16[1536,512]{1,0:T(8,128)(2,1)S(1)}, bf16[1536,512]{1,0:T(8,128)(2,1)S(1)}, u32[]{:S(2)}, u32[]{:S(2)}) collective-permute-start(bf16[1536,512]{1,0:T(8,128)(2,1)S(1)} %copy-done.16), channel_id=1, source_target_pairs={{0,2},{1,3},{2,0},{3,1},{4,6},{5,7},{6,4},{7,5},{8,10},{9,11},{10,... | collective-permute-start | bytes 4718600 | tf_op jit(solution)/shard_map/ppermute | solution.py:712
  44.5 12.4 %collective-permute-start.8 = (bf16[272,512]{1,0:T(8,128)(2,1)S(1)}, bf16[272,512]{1,0:T(8,128)(2,1)S(1)}, u32[]{:S(2)}, u32[]{:S(2)}) collective-permute-start(bf16[272,512]{1,0:T(8,128)(2,1)S(1)} %get-tuple-element.75), channel_id=1, source_target_pairs={{0,16},{1,17},{2,18},{3,19},{4,20},{5,21},{6,22},{7,23},{8,24},{9,... | collective-permute-start | bytes 835592 | tf_op jit(solution)/shard_map/ppermute | solution.py:718
  47.1 6.4 %collective-permute-start.7 = (bf16[256,512]{1,0:T(8,128)(2,1)S(1)}, bf16[256,512]{1,0:T(8,128)(2,1)S(1)}, u32[]{:S(2)}, u32[]{:S(2)}) collective-permute-start(bf16[256,512]{1,0:T(8,128)(2,1)S(1)} %add_blocks.1), channel_id=1, source_target_pairs={{0,4},{1,5},{2,6},{3,7},{4,0},{5,1},{6,2},{7,3},{8,12},{9,13},{10,... | collective-permute-start | bytes 786440 | tf_op jit(solution)/shard_map/ppermute | solution.py:718
  63.1 4.8 %collective-permute-start.11 = (f32[24,256]{1,0:T(8,128)S(1)}, f32[24,256]{1,0:T(8,128)S(1)}, u32[]{:S(2)}, u32[]{:S(2)}) collective-permute-start(f32[24,256]{1,0:T(8,128)S(1)} %collective-permute-done.10), channel_id=1, source_target_pairs={{0,6},{1,7},{2,4},{3,5},{4,2},{5,3},{6,0},{7,1},{8,14},{9,15},{10,... | collective-permute-start | bytes 73736 | tf_op jit(solution)/shard_map/ppermute | solution.py:718
  70.1 4.2 %collective-permute-start.13 = (f32[8,4096]{1,0:T(8,128)S(1)}, f32[8,4096]{1,0:T(8,128)S(1)}, u32[]{:S(2)}, u32[]{:S(2)}) collective-permute-start(f32[8,4096]{1,0:T(8,128)S(1)} %density.1), channel_id=1, source_target_pairs={{0,1},{1,0},{2,3},{3,2},{4,5},{5,4},{6,7},{7,6},{8,9},{9,8},{10,11... | collective-permute-start | bytes 393224 | tf_op jit(solution)/shard_map/ppermute | solution.py:712
  70.1 15.4 %collective-permute-start.18 = (bf16[256,512]{1,0:T(8,128)(2,1)S(1)}, bf16[256,512]{1,0:T(8,128)(2,1)S(1)}, u32[]{:S(2)}, u32[]{:S(2)}) collective-permute-start(bf16[256,512]{1,0:T(8,128)(2,1)S(1)} %get-tuple-element.86.refs_7_), channel_id=1, source_target_pairs={{0,16},{1,17},{2,18},{3,19},{4,20},{5,21},{6,22},{7,23},{8,24},{9,... | collective-permute-start | bytes 786440 | tf_op jit(solution)/shard_map/ppermute | solution.py:709
  70.2 15.4 %collective-permute-start.17 = (bf16[256,512]{1,0:T(8,128)(2,1)S(1)}, bf16[256,512]{1,0:T(8,128)(2,1)S(1)}, u32[]{:S(2)}, u32[]{:S(2)}) collective-permute-start(bf16[256,512]{1,0:T(8,128)(2,1)S(1)} %get-tuple-element.86.refs_7_), channel_id=1, source_target_pairs={{0,8},{1,5},{2,10},{3,7},{4,12},{5,1},{6,14},{7,3},{8,0},{9,13},{1... | collective-permute-start | bytes 786440 | tf_op jit(solution)/shard_map/ppermute | solution.py:709
  74.3 11.3 %collective-permute-start.16 = (bf16[256,512]{1,0:T(8,128)(2,1)S(1)}, bf16[256,512]{1,0:T(8,128)(2,1)S(1)}, u32[]{:S(2)}, u32[]{:S(2)}) collective-permute-start(bf16[256,512]{1,0:T(8,128)(2,1)S(1)} %get-tuple-element.86.refs_7_), channel_id=1, source_target_pairs={{0,4},{1,9},{2,6},{3,11},{4,0},{5,13},{6,2},{7,15},{8,12},{9,1},{1... | collective-permute-start | bytes 786440 | tf_op jit(solution)/shard_map/ppermute | solution.py:709
  74.3 8.2 %collective-permute-start.14 = (f32[8,4096]{1,0:T(8,128)S(1)}, f32[8,4096]{1,0:T(8,128)S(1)}, u32[]{:S(2)}, u32[]{:S(2)}) collective-permute-start(f32[8,4096]{1,0:T(8,128)S(1)} %add.23.d_ref), channel_id=1, source_target_pairs={{0,4},{1,5},{2,6},{3,7},{4,0},{5,1},{6,2},{7,3},{8,12},{9,13},{10,... | collective-permute-start | bytes 393224 | tf_op jit(solution)/shard_map/ppermute | solution.py:718
  82.6 6.0 %collective-permute-start.15 = (f32[8,4096]{1,0:T(8,128)S(1)}, f32[8,4096]{1,0:T(8,128)S(1)}, u32[]{:S(2)}, u32[]{:S(2)}) collective-permute-start(f32[8,4096]{1,0:T(8,128)S(1)} %collective-permute-done.14), channel_id=1, source_target_pairs={{0,6},{1,7},{2,4},{3,5},{4,2},{5,3},{6,0},{7,1},{8,14},{9,15},{10,... | collective-permute-start | bytes 393224 | tf_op jit(solution)/shard_map/ppermute | solution.py:718
  85.6 12.5 %collective-permute-start.23 = (bf16[256,512]{1,0:T(8,128)(2,1)S(1)}, bf16[256,512]{1,0:T(8,128)(2,1)S(1)}, u32[]{:S(2)}, u32[]{:S(2)}) collective-permute-start(bf16[256,512]{1,0:T(8,128)(2,1)S(1)} %collective-permute-done.17.refs_2_.refs_5_), channel_id=1, source_target_pairs={{0,4},{1,9},{2,6},{3,11},{4,0},{5,13},{6,2},{7,15},{8,12},{9,1},{1... | collective-permute-start | bytes 786440 | tf_op jit(solution)/shard_map/ppermute | solution.py:709
  88.6 9.5 %collective-permute-start.25 = (bf16[256,512]{1,0:T(8,128)(2,1)S(1)}, bf16[256,512]{1,0:T(8,128)(2,1)S(1)}, u32[]{:S(2)}, u32[]{:S(2)}) collective-permute-start(bf16[256,512]{1,0:T(8,128)(2,1)S(1)} %hold.2.refs_6_), channel_id=1, source_target_pairs={{0,8},{1,5},{2,10},{3,7},{4,12},{5,1},{6,14},{7,3},{8,0},{9,13},{1... | collective-permute-start | bytes 786440 | tf_op jit(solution)/shard_map/ppermute | solution.py:709
  91.5 6.6 %collective-permute-start.24 = (bf16[256,512]{1,0:T(8,128)(2,1)S(1)}, bf16[256,512]{1,0:T(8,128)(2,1)S(1)}, u32[]{:S(2)}, u32[]{:S(2)}) collective-permute-start(bf16[256,512]{1,0:T(8,128)(2,1)S(1)} %hold.2.refs_6_), channel_id=1, source_target_pairs={{0,4},{1,9},{2,6},{3,11},{4,0},{5,13},{6,2},{7,15},{8,12},{9,1},{1... | collective-permute-start | bytes 786440 | tf_op jit(solution)/shard_map/ppermute | solution.py:709
  99.6 11.5 %collective-permute-start.28 = (bf16[1536,512]{1,0:T(8,128)(2,1)S(1)}, bf16[1536,512]{1,0:T(8,128)(2,1)S(1)}, u32[]{:S(2)}, u32[]{:S(2)}) collective-permute-start(bf16[1536,512]{1,0:T(8,128)(2,1)S(1)} %collective-permute-done.22.refs_4_), channel_id=1, source_target_pairs={{0,1},{1,0},{2,3},{3,2},{4,5},{5,4},{6,7},{7,6},{8,9},{9,8},{10,11... | collective-permute-start | bytes 4718600 | tf_op jit(solution)/shard_map/ppermute | solution.py:712
  99.6 11.5 %collective-permute-start.27 = (bf16[1280,512]{1,0:T(8,128)(2,1)}, bf16[1280,512]{1,0:T(8,128)(2,1)}, u32[]{:S(2)}, u32[]{:S(2)}) collective-permute-start(bf16[1280,512]{1,0:T(8,128)(2,1)} %collective-permute-done.12.refs_2_), channel_id=1, source_target_pairs={{0,1},{1,0},{2,3},{3,2},{4,5},{5,4},{6,7},{7,6},{8,9},{9,8},{10,11... | collective-permute-start | bytes 3932168 | tf_op jit(solution)/shard_map/ppermute | solution.py:712
  100.2 11.0 %collective-permute-start.26 = (bf16[256,512]{1,0:T(8,128)(2,1)}, bf16[256,512]{1,0:T(8,128)(2,1)}, u32[]{:S(2)}, u32[]{:S(2)}) collective-permute-start(bf16[256,512]{1,0:T(8,128)(2,1)} %get-tuple-element.95), channel_id=1, source_target_pairs={{0,2},{1,3},{2,0},{3,1},{4,6},{5,7},{6,4},{7,5},{8,10},{9,11},{10,... | collective-permute-start | bytes 786440 | tf_op jit(solution)/shard_map/ppermute | solution.py:712
  101.0 10.2 %collective-permute-start.29 = (bf16[256,512]{1,0:T(8,128)(2,1)}, bf16[256,512]{1,0:T(8,128)(2,1)}, u32[]{:S(2)}, u32[]{:S(2)}) collective-permute-start(bf16[256,512]{1,0:T(8,128)(2,1)} %hold.3.refs_4_), channel_id=1, source_target_pairs={{0,4},{1,9},{2,6},{3,11},{4,0},{5,13},{6,2},{7,15},{8,12},{9,1},{1... | collective-permute-start | bytes 786440 | tf_op jit(solution)/shard_map/ppermute | solution.py:709
  102.6 3.9 %collective-permute-start.20 = (f32[8,512]{1,0:T(8,128)S(1)}, f32[8,512]{1,0:T(8,128)S(1)}, u32[]{:S(2)}, u32[]{:S(2)}) collective-permute-start(f32[8,512]{1,0:T(8,128)S(1)} %add.25.refs_3_), channel_id=1, source_target_pairs={{0,8},{1,5},{2,10},{3,7},{4,12},{5,1},{6,14},{7,3},{8,0},{9,13},{1... | collective-permute-start | bytes 49160 | tf_op jit(solution)/shard_map/ppermute | solution.py:709
  106.5 4.6 %collective-permute-start.21 = (f32[8,512]{1,0:T(8,128)S(1)}, f32[8,512]{1,0:T(8,128)S(1)}, u32[]{:S(2)}, u32[]{:S(2)}) collective-permute-start(f32[8,512]{1,0:T(8,128)S(1)} %add.26), channel_id=1, source_target_pairs={{0,16},{1,17},{2,18},{3,19},{4,20},{5,21},{6,22},{7,23},{8,24},{9,... | collective-permute-start | bytes 49160 | tf_op jit(solution)/shard_map/ppermute | solution.py:709
  113.5 17.4 %collective-permute-start.33 = (bf16[4096,512]{1,0:T(8,128)(2,1)}, bf16[4096,512]{1,0:T(8,128)(2,1)S(1)}, u32[]{:S(2)}, u32[]{:S(2)}) collective-permute-start(bf16[4096,512]{1,0:T(8,128)(2,1)} %get-tuple-element.109.u_ref.refs_4_), channel_id=1, source_target_pairs={{0,1},{1,0},{2,3},{3,2},{4,5},{5,4},{6,7},{7,6},{8,9},{9,8},{10,11... | collective-permute-start | bytes 12582920 | tf_op jit(solution)/shard_map/ppermute | solution.py:712
  113.6 17.3 %collective-permute-start.34 = (bf16[512,512]{1,0:T(8,128)(2,1)S(1)}, bf16[512,512]{1,0:T(8,128)(2,1)S(1)}, u32[]{:S(2)}, u32[]{:S(2)}) collective-permute-start(bf16[512,512]{1,0:T(8,128)(2,1)S(1)} %get-tuple-element.105), channel_id=1, source_target_pairs={{0,1},{1,0},{2,3},{3,2},{4,5},{5,4},{6,7},{7,6},{8,9},{9,8},{10,11... | collective-permute-start | bytes 1572872 | tf_op jit(solution)/shard_map/ppermute | solution.py:712
  114.1 24.6 %collective-permute-start.31 = (bf16[512,512]{1,0:T(8,128)(2,1)S(1)}, bf16[512,512]{1,0:T(8,128)(2,1)S(1)}, u32[]{:S(2)}, u32[]{:S(2)}) collective-permute-start(bf16[512,512]{1,0:T(8,128)(2,1)S(1)} %get-tuple-element.106), channel_id=1, source_target_pairs={{0,2},{1,3},{2,0},{3,1},{4,6},{5,7},{6,4},{7,5},{8,10},{9,11},{10,... | collective-permute-start | bytes 1572872 | tf_op jit(solution)/shard_map/ppermute | solution.py:712
  115.3 23.4 %collective-permute-start.32 = (bf16[512,512]{1,0:T(8,128)(2,1)S(1)}, bf16[512,512]{1,0:T(8,128)(2,1)S(1)}, u32[]{:S(2)}, u32[]{:S(2)}) collective-permute-start(bf16[512,512]{1,0:T(8,128)(2,1)S(1)} %get-tuple-element.107), channel_id=1, source_target_pairs={{0,3},{1,2},{2,1},{3,0},{4,7},{5,6},{6,5},{7,4},{8,11},{9,10},{10,... | collective-permute-start | bytes 1572872 | tf_op jit(solution)/shard_map/ppermute | solution.py:712
  115.5 23.1 %collective-permute-start.30 = (bf16[256,512]{1,0:T(8,128)(2,1)}, bf16[256,512]{1,0:T(8,128)(2,1)S(1)}, u32[]{:S(2)}, u32[]{:S(2)}) collective-permute-start(bf16[256,512]{1,0:T(8,128)(2,1)} %collective-permute-done.26.refs_6_), channel_id=1, source_target_pairs={{0,1},{1,0},{2,3},{3,2},{4,5},{5,4},{6,7},{7,6},{8,9},{9,8},{10,11... | collective-permute-start | bytes 786440 | tf_op jit(solution)/shard_map/ppermute | solution.py:712
  (21 other events, 253.9 us)

commit v5 on v4

--- a/solution.py
+++ b/solution.py
@@ -58,7 +58,7 @@
 
 def split_rows(cells):
     unit = cells // 64
-    return [share * unit for share in (16, 20, 24, 4)]
+    return [share * unit for share in (16, 18, 30)]
 
 
 def column_mask(k_ref, group, spots):
@@ -203,12 +203,13 @@
     )(ids, in_hbm(logits), in_hbm(keep_rows), in_hbm(expression))
 
 
-def part_call(expression, mapping, ids, picks, dtypes):
+def part_call(expression, mapping, ids, picks, dtypes, came):
     cells, spots = mapping.shape
     count = len(picks)
     block = expression.shape[1] // ids.shape[0]
 
     def body(ids_ref, e_ref, u_ref, *refs):
+        came_refs, refs = refs[: len(came)], refs[len(came) :]
         o_refs, (held, sem) = refs[:count], refs[count:]
         copies = []
         for q, pick in enumerate(picks):
@@ -217,11 +218,14 @@
             copies[q].start()
         for q in range(count):
             copies[q].wait()
-            o_refs[q][...] = dot(held[q], u_ref[...], TN).astype(dtypes[q])
-
-    return pl.pallas_call(
-        body,
-        in_specs=[SMEM, HBM, VMEM],
+            total = dot(held[q], u_ref[...], TN)
+            for ref in came_refs if q == 0 else ():
+                total = total + ref[...].astype(f32)
+            o_refs[q][...] = total.astype(dtypes[q])
+
+    return pl.pallas_call(
+        body,
+        in_specs=[SMEM, HBM, VMEM] + [VMEM] * len(came),
         out_specs=[VMEM] * count,
         out_shape=[shape((block, spots), dtype) for dtype in dtypes],
         scratch_shapes=[
@@ -233,7 +237,7 @@
             2 * count * block * cells * spots, 2 * cells * (count * block + spots)
         ),
         name="part",
-    )(ids, in_hbm(expression), mapping)
+    )(ids, in_hbm(expression), mapping, *came)
 
 
 def add_call(values):
@@ -597,7 +601,7 @@
     )(in_hbm(expression), grad, in_hbm(mapping), in_hbm(slope), weight, ends, tops)
 
 
-def expr_call(base, mapping, chunks, grads, tops):
+def expr_call(base, mapping, beside, chunks, grads, tops):
     genes, spots = grads[0].shape
     cells = mapping.shape[0] if base is None else base.shape[0]
     count = len(grads)
@@ -616,22 +620,25 @@
     most = max(len(runs) for runs in tiles)
     slots = 3
     flat = [v for chunk in chunks for v in chunk]
-    far = count - own
+    whole = 2 * own
+    far = count - whole
 
     def body(*refs):
         q_refs, refs = refs[: len(flat)], refs[len(flat) :]
         g_refs, refs = refs[:count], refs[count:]
-        tops_ref, whole_ref, o_ref, held, g_buf, out, in_sem, out_sem = refs
+        tops_ref, refs = refs[0], refs[1:]
+        w_refs, refs = refs[: whole or 1], refs[whole or 1 :]
+        o_ref, held, g_buf, out, in_sem, out_sem = refs
         scale = expression_scale * kept_of(tops_ref)
 
         def fetch(k):
             pieces = [
-                (own + q, q_refs[c * far + q].at[pl.ds(row, size)], at, size, r)
+                (whole + q, q_refs[c * far + q].at[pl.ds(row, size)], at, size, r)
                 for r, (c, row, at, size) in enumerate(tiles[k])
                 for q in range(far)
             ]
-            if own:
-                pieces.append((0, whole_ref.at[pl.ds(k * tile, tile)], 0, tile, 0))
+            for q in range(whole):
+                pieces.append((q, w_refs[q].at[pl.ds(k * tile, tile)], 0, tile, 0))
             return [
                 pltpu.make_async_copy(
                     source,
@@ -660,7 +667,7 @@
             else:
                 if k >= 2:
                     store(k - 2).wait()
-                out[k % 2] = dot(held[k % slots], g_buf[...], NT) * scale + whole_ref[at, :]
+                out[k % 2] = dot(held[k % slots], g_buf[...], NT) * scale + w_refs[0][at, :]
                 store(k).start()
             if k + slots < len(tiles):
                 for copy in fetch(k + slots):
@@ -672,7 +679,7 @@
     rows = len(tiles) * tile
     return pl.pallas_call(
         body,
-        in_specs=[ANY] * len(flat) + [VMEM] * (count + 1) + [HBM if own else VMEM],
+        in_specs=[ANY] * len(flat) + [VMEM] * (count + 1) + ([HBM, ANY] if own else [VMEM]),
         out_specs=VMEM if own else HBM,
         out_shape=shape((cells, genes), f32) if own else pltpu.HBM((cells, genes), f32),
         scratch_shapes=[
@@ -687,7 +694,7 @@
             2 * rows * spots * count * genes, 2 * rows * spots * count + 4 * rows * genes, 0.0
         ),
         name="grad_expression",
-    )(*flat, *grads, tops, in_hbm(mapping) if own else base)
+    )(*flat, *grads, tops, *([in_hbm(mapping), beside] if own else [base]))
 
 
 def per_device(n, m, logits, expression, target, keep_mask, slide_ids, slide_counts):
@@ -827,10 +834,10 @@
         got["111"], got["101"] = across(parts[0], 0), across(parts[1], 0)
         got["diagonal"] = over_cell(parts[2], 2, 0)
 
-        def products(*some, late=()):
+        def products(*some, late=(), came=()):
             dtypes = [f32 if name in ("011", "001", "own") else bf16 for name in some]
             picks = [slot[name] for name in some]
-            outs = done(part_call(expression, mapping, after(part_ids, late), picks, dtypes))
+            outs = done(part_call(expression, mapping, after(part_ids, late), picks, dtypes, came))
             part.update(zip(some, outs))
 
         products("011", "001", "z")
@@ -841,14 +848,13 @@
         got["z"] = over_cell(part["z"], 2, 0)
         send(1)
         spread(0, [part["011"]])
-        products("x", "own", late=wide(0))
+        send(2, [part["011"]])
+        products("x", "own", late=wide(0), came=[got["diagonal"]])
         part["001"], tops = done(
             relay_call([after(part["001"]), got["101"], got["011"]], tops)
         )
         last = over_cell(part["001"], 4, 0)
-        part["x"] = done(add_call([after(part["x"], [got["z"]]), got["diagonal"]]))
         got["x"] = over_cell(part["x"], 1, 0)
-        send(2, [part["x"]])
         terms = [part["own"], got["x"], got["z"], last]
     predicted, predicted_near, gene_sums, tops = done(
         predicted_call(terms, tops, target, after(member))
@@ -860,11 +866,11 @@
         )
     )
 
-    have = {(0, 0, 0): grad}
-    for k in range(3):
-        have[tuple(int(q == k) for q in range(3))] = across(grad, lead + k)
+    have = {(0, 0, 0): grad, (0, 0, 1): across(grad, lead + 2)}
     density = done(density_call(mapping, tops, after(member)))
-    _, density, _, far_density = sum_spot(density)
+    first, density, _, far_density = sum_spot(density)
+    near_grad = hold_call(grad, [first])
+    have[0, 1, 0], have[1, 0, 0] = across(near_grad, lead + 1), across(near_grad, lead)
     have[0, 0, 1] = hold_call(
         have[0, 0, 1],
         [far_density, have[1, 0, 0], have[0, 1, 0]],
@@ -887,11 +893,9 @@
     ends = ends + more
     ends = ends + across(ends, 0)
     have[0, 1, 1] = hold_call(
-        have[0, 1, 1], [*[corner(v) for v in far(2)], have[1, 1, 0], have[1, 0, 1], ends]
+        have[0, 1, 1], [have[1, 1, 0], have[1, 0, 1], ends]
     )
-    send(3, [have[0, 1, 1]])
     spread(1, [have[0, 1, 1]])
-    spread(2, [have[0, 1, 1]])
     have[1, 1, 1] = across(have[0, 1, 1], lead)
     ends = ends + across(ends, 1)
     most = ends
@@ -905,21 +909,21 @@
             blocks = jnp.concatenate([across(blocks, k), blocks])
         blocks = [blocks[q] for q in range(n)]
 
-    whole_grad, *shares = regroup_call(blocks, after(ids, [ends, *far(3), *wide(1), *wide(2)]), place[None], m)
+    whole_grad, *shares = regroup_call(blocks, after(ids, [ends, *far(2), *wide(1)]), place[None], m)
     done(shares)
     regrouped = [over_spot(value, mask) if mask else value for mask, value in enumerate(shares)]
     beside = over_spot(tie(mapping, shares), 1)
-    spread(3, shares)
+    spread(2, shares)
     grad_logits, loss = done(
         logit_call(
             expression, whole_grad, mapping, slope, weight, after(ends), tops, slide_total
         )
     )
-    near_part = done(
-        expr_call(None, mapping, [[beside]], regrouped[:2], after(tops))
-    )
-    rest = [[gathered[c, mask] for mask in range(2, m)] for c in range(4)]
-    grad_expression = expr_call(near_part, None, rest, regrouped[2:], after(tops))
+    evens = [[gathered[c, mask] for mask in range(2, m, 2)] for c in range(3)]
+    some = [regrouped[mask] for mask in (0, 1, *range(2, m, 2))]
+    most_of = done(expr_call(None, mapping, beside, evens, some, after(tops)))
+    rest = [wide(c) for c in range(3)]
+    grad_expression = expr_call(most_of, None, None, rest, regrouped[3::2], after(tops))
     return (loss.reshape(()), predicted, grad_logits, grad_expression)
 
 

time: 147 us -> 141 us (0.959)
  waiting for transfers between devices: 40.7 us -> 36.5 us
    ppermute x8, waiting for transfers between devices: 29.3 us -> 25.2 us  [over_cell(): return lax.ppermute(value, ('cell', 'spot'), pairs)]
    ppermute x8, starting transfers between devices: 8.82 us -> 11 us  [over_cell(): return lax.ppermute(value, ('cell', 'spot'), pairs)]
    ppermute x14 -> x12, starting transfers between devices: 10.6 us -> 8.91 us  [over_spot(): return lax.ppermute(value, 'spot', [(j, j ^ mask) for j in range(m)])]
    ppermute x13, waiting for transfers between devices: 10 us -> 8.38 us  [across(): return lax.ppermute(value, ('cell', 'spot'), pairs)]
    ppermute x14 -> x12, waiting for transfers between devices: 1.35 us -> 2.87 us  [over_spot(): return lax.ppermute(value, 'spot', [(j, j ^ mask) for j in range(m)])]
    pallas_call x3 -> x2, Pallas kernels: 11 us -> 11 us  [part_call(): pl.pallas_call(body, in_specs=[SMEM, HBM, VMEM] + [VMEM] * len(came), out...]
  transfers between devices with their start and end apart: 35 -> 33, of which waited for: 14 -> 15; matrix products, arithmetic and copies ran while one was open for 0% -> 0% of each run, Pallas kernels for 34% -> 37%
where the time goes in v5:
time: 141 us
  Pallas kernels  63 us (45%)
  starting transfers between devices  37.7 us (27%)
  waiting for transfers between devices  36.5 us (26%)
  local copies, waits for them, and re-layouts  2.9 us (2%)
    ppermute x8, waiting for transfers between devices, over_cell(): return lax.ppermute(value, ('cell', 'spot'), pairs)  25.2 us
    ppermute x13, starting transfers between devices, across(): return lax.ppermute(value, ('cell', 'spot'), pairs)  17.8 us
    pallas_call x2, Pallas kernels, expr_call(): pl.pallas_call(body, in_specs=[ANY] * len(flat) + [VMEM] * (count + 1) +...  16.2 us
    pallas_call x1, Pallas kernels, logit_call(): pl.pallas_call(body, in_specs=[HBM, VMEM, HBM, HBM] + [VMEM] * 3, out_spe...  14.8 us
    pallas_call x1, Pallas kernels, exp_call(): pl.pallas_call(body, in_specs=[SMEM, HBM, HBM, HBM], out_specs=[HBM] * le...  11 us
    ppermute x8, starting transfers between devices, over_cell(): return lax.ppermute(value, ('cell', 'spot'), pairs)  11 us
    pallas_call x2, Pallas kernels, part_call(): pl.pallas_call(body, in_specs=[SMEM, HBM, VMEM] + [VMEM] * len(came), out...  11 us
    ppermute x12, starting transfers between devices, over_spot(): return lax.ppermute(value, 'spot', [(j, j ^ mask) for j in range(m)])  8.91 us
  transfers between devices with their start and end apart: 33, of which 15 were waited for; matrix products, arithmetic and copies ran while one was open for 0% of the time, Pallas kernels for 37%

profile of v5, /device:TPU:0, one launch (start us, length us, event | category | flops | bytes accessed | tf_op | source)
XLA Modules:
  0.0 141.2 jit_solution(2160405403420986826)
XLA Ops:
  0.6 1.9 %exp_first.1 = bf16[1024,512]{1,0:T(8,128)(2,1)S(1)} custom-call(f32[4096,512]{1,0:T(8,128)} %x_ref.3, s32[32,128]{1,0:T(8,128)} %bitcast.19), custom_call_target="tpu_custom_call" | custom-call | bytes 157286 | tf_op jit(solution)/shard_map/exp_first/pallas_call | solution.py:89
  2.5 3.0 %collective-permute-start = (bf16[1024,512]{1,0:T(8,128)(2,1)S(1)}, bf16[1024,512]{1,0:T(8,128)(2,1)S(1)}, u32[]{:S(2)}, u32[]{:S(2)}) collective-permute-start(bf16[1024,512]{1,0:T(8,128)(2,1)S(1)} %exp_first.1), channel_id=1, source_target_pairs={{0,2},{1,3},{2,0},{3,1},{4,6},{5,7},{6,4},{7,5},{8,10},{9,11},{10,... | collective-permute-start | bytes 3145736 | tf_op jit(solution)/shard_map/ppermute | solution.py:719
  5.6 11.0 %exp_rows.1 = (bf16[1152,512]{1,0:T(8,128)(2,1)}, bf16[1920,512]{1,0:T(8,128)(2,1)}, bf16[4096,512]{1,0:T(8,128)(2,1)}, f32[8,512]{1,0:T(8,128)S(1)}, bf16[272,5...) custom-call(s32[8]{0:T(128)S(1)} %stack.65.ids_ref, f32[4096,512]{1,0:T(8,128)} %x_ref.3, ...), custom_call_target="tpu_custom_call" | custom-call | bytes 838860 | tf_op jit(solution)/shard_map/exp_rows/pallas_call | solution.py:181
  20.1 2.2 %copy-done = bf16[4096,512]{1,0:T(8,128)(2,1)S(1)} copy-done((bf16[4096,512]{1,0:T(8,128)(2,1)S(1)}, bf16[4096,512]{1,0:T(8,128)(2,1)}, u32[]{:S(2)}) %copy-start) | copy-done | bytes 4194328
  22.3 6.3 %part.2 = (f32[256,512]{1,0:T(8,128)S(1)}, f32[256,512]{1,0:T(8,128)S(1)}, bf16[256,512]{1,0:T(8,128)(2,1)S(1)}) custom-call(s32[8]{0:T(128)S(1)} %stack.65.ids_ref, bf16[4096,2048]{1,0:T(8,128)(2,1)} %e_ref.7, bf16[4096,512]{1,0:T(8,128)(2,1)S(1)} %copy-done), custom_call_target="tpu_custom_call" | custom-call | flops 161061280 | bytes 524288 | tf_op jit(solution)/shard_map/part/pallas_call | solution.py:226
  28.8 1.5 %collective-permute-start.4 = (bf16[1024,512]{1,0:T(8,128)(2,1)S(1)}, bf16[1024,512]{1,0:T(8,128)(2,1)S(1)}, u32[]{:S(2)}, u32[]{:S(2)}) collective-permute-start(bf16[1024,512]{1,0:T(8,128)(2,1)S(1)} %collective-permute-done.refs_0_), channel_id=1, source_target_pairs={{0,1},{1,0},{2,3},{3,2},{4,5},{5,4},{6,7},{7,6},{8,9},{9,8},{10,11... | collective-permute-start | bytes 3145736 | tf_op jit(solution)/shard_map/ppermute | solution.py:719
  30.8 1.6 %collective-permute-start.7 = (bf16[272,512]{1,0:T(8,128)(2,1)S(1)}, bf16[272,512]{1,0:T(8,128)(2,1)S(1)}, u32[]{:S(2)}, u32[]{:S(2)}) collective-permute-start(bf16[272,512]{1,0:T(8,128)(2,1)S(1)} %get-tuple-element.63), channel_id=1, source_target_pairs={{0,8},{1,5},{2,10},{3,7},{4,12},{5,1},{6,14},{7,3},{8,0},{9,13},{1... | collective-permute-start | bytes 835592 | tf_op jit(solution)/shard_map/ppermute | solution.py:716
  32.5 4.7 %part.3 = (bf16[256,512]{1,0:T(8,128)(2,1)S(1)}, f32[256,512]{1,0:T(8,128)S(1)}) custom-call(s32[8]{0:T(128)S(1)} %stack.65.ids_ref, bf16[4096,2048]{1,0:T(8,128)(2,1)} %e_ref.7, bf16[4096,512]{1,0:T(8,128)(2,1)S(1)} %copy-done.1, bf16[256,512]{1,0:T(8,128)(2,1)S(1)} %collective-permute-done.2.refs_0_), custom_call_target="tpu_custom_call" | custom-call | flops 107374184 | bytes 419430 | tf_op jit(solution)/shard_map/part/pallas_call | solution.py:226
  37.4 2.7 %collective-permute-start.8 = (bf16[272,512]{1,0:T(8,128)(2,1)S(1)}, bf16[272,512]{1,0:T(8,128)(2,1)S(1)}, u32[]{:S(2)}, u32[]{:S(2)}) collective-permute-start(bf16[272,512]{1,0:T(8,128)(2,1)S(1)} %get-tuple-element.72), channel_id=1, source_target_pairs={{0,16},{1,17},{2,18},{3,19},{4,20},{5,21},{6,22},{7,23},{8,24},{9,... | collective-permute-start | bytes 835592 | tf_op jit(solution)/shard_map/ppermute | solution.py:725
  40.1 1.6 %collective-permute-start.6 = (bf16[256,512]{1,0:T(8,128)(2,1)S(1)}, bf16[256,512]{1,0:T(8,128)(2,1)S(1)}, u32[]{:S(2)}, u32[]{:S(2)}) collective-permute-start(bf16[256,512]{1,0:T(8,128)(2,1)S(1)} %get-tuple-element.68), channel_id=1, source_target_pairs={{0,8},{1,9},{2,10},{3,11},{4,12},{5,13},{6,14},{7,15},{8,0},{9,1},... | collective-permute-start | bytes 786440 | tf_op jit(solution)/shard_map/ppermute | solution.py:725
  41.7 1.5 %collective-permute-start.5 = (bf16[256,512]{1,0:T(8,128)(2,1)S(1)}, bf16[256,512]{1,0:T(8,128)(2,1)S(1)}, u32[]{:S(2)}, u32[]{:S(2)}) collective-permute-start(bf16[256,512]{1,0:T(8,128)(2,1)S(1)} %get-tuple-element.67), channel_id=1, source_target_pairs={{0,4},{1,5},{2,6},{3,7},{4,0},{5,1},{6,2},{7,3},{8,12},{9,13},{10,... | collective-permute-start | bytes 786440 | tf_op jit(solution)/shard_map/ppermute | solution.py:725
  43.1 1.4 %collective-permute-start.22 = (bf16[1920,512]{1,0:T(8,128)(2,1)}, bf16[1920,512]{1,0:T(8,128)(2,1)S(1)}, u32[]{:S(2)}, u32[]{:S(2)}) collective-permute-start(bf16[1920,512]{1,0:T(8,128)(2,1)} %get-tuple-element.88), channel_id=1, source_target_pairs={{0,2},{1,3},{2,0},{3,1},{4,6},{5,7},{6,4},{7,5},{8,10},{9,11},{10,... | collective-permute-start | bytes 5898248 | tf_op jit(solution)/shard_map/ppermute | solution.py:719
  44.6 7.5 %collective-permute-done.6.refs_2_ = bf16[256,512]{1,0:T(8,128)(2,1)S(1)} collective-permute-done((bf16[256,512]{1,0:T(8,128)(2,1)S(1)}, bf16[256,512]{1,0:T(8,128)(2,1)S(1)}, u32[]{:S(2)}, u32[]{:S(2)}) %collective-permute-start.6) | collective-permute-done | bytes 262176 | tf_op jit(solution)/shard_map/ppermute | solution.py:725
  57.0 2.5 %collective-permute-done.10 = f32[24,256]{1,0:T(8,128)S(1)} collective-permute-done((f32[24,256]{1,0:T(8,128)S(1)}, f32[24,256]{1,0:T(8,128)S(1)}, u32[]{:S(2)}, u32[]{:S(2)}) %collective-permute-start.10) | collective-permute-done | bytes 24608 | tf_op jit(solution)/shard_map/ppermute | solution.py:725
  60.9 3.4 %collective-permute-done.11.f_ref = f32[24,256]{1,0:T(8,128)S(1)} collective-permute-done((f32[24,256]{1,0:T(8,128)S(1)}, f32[24,256]{1,0:T(8,128)S(1)}, u32[]{:S(2)}, u32[]{:S(2)}) %collective-permute-start.11) | collective-permute-done | bytes 24608 | tf_op jit(solution)/shard_map/ppermute | solution.py:725
  65.0 1.5 %density.1 = f32[8,4096]{1,0:T(8,128)S(1)} custom-call(bf16[4096,512]{1,0:T(8,128)(2,1)S(1)} %copy-done.1, f32[8,512]{1,0:T(8,128)S(1)} %get-tuple-element.103.tops_ref.refs_6_.refs_4_, f32[8,512]{1,0:T(8,128)S(1)} %fusion.refs_6_.m_ref), custom_call_target="tpu_custom_call" | custom-call | bytes 209715 | tf_op jit(solution)/shard_map/density/pallas_call | solution.py:405
  67.9 1.4 %collective-permute-start.17 = (bf16[256,512]{1,0:T(8,128)(2,1)S(1)}, bf16[256,512]{1,0:T(8,128)(2,1)S(1)}, u32[]{:S(2)}, u32[]{:S(2)}) collective-permute-start(bf16[256,512]{1,0:T(8,128)(2,1)S(1)} %hold.3), channel_id=1, source_target_pairs={{0,8},{1,5},{2,10},{3,7},{4,12},{5,1},{6,14},{7,3},{8,0},{9,13},{1... | collective-permute-start | bytes 786440 | tf_op jit(solution)/shard_map/ppermute | solution.py:716
  69.3 2.7 %collective-permute-start.18 = (bf16[256,512]{1,0:T(8,128)(2,1)S(1)}, bf16[256,512]{1,0:T(8,128)(2,1)S(1)}, u32[]{:S(2)}, u32[]{:S(2)}) collective-permute-start(bf16[256,512]{1,0:T(8,128)(2,1)S(1)} %get-tuple-element.81.refs_1_.refs_7_), channel_id=1, source_target_pairs={{0,16},{1,17},{2,18},{3,19},{4,20},{5,21},{6,22},{7,23},{8,24},{9,... | collective-permute-start | bytes 786440 | tf_op jit(solution)/shard_map/ppermute | solution.py:716
  71.9 1.5 %collective-permute-start.16 = (bf16[256,512]{1,0:T(8,128)(2,1)S(1)}, bf16[256,512]{1,0:T(8,128)(2,1)S(1)}, u32[]{:S(2)}, u32[]{:S(2)}) collective-permute-start(bf16[256,512]{1,0:T(8,128)(2,1)S(1)} %hold.3), channel_id=1, source_target_pairs={{0,4},{1,9},{2,6},{3,11},{4,0},{5,13},{6,2},{7,15},{8,12},{9,1},{1... | collective-permute-start | bytes 786440 | tf_op jit(solution)/shard_map/ppermute | solution.py:716
  74.0 7.2 %collective-permute-done.14 = f32[8,4096]{1,0:T(8,128)S(1)} collective-permute-done((f32[8,4096]{1,0:T(8,128)S(1)}, f32[8,4096]{1,0:T(8,128)S(1)}, u32[]{:S(2)}, u32[]{:S(2)}) %collective-permute-start.14) | collective-permute-done | bytes 131104 | tf_op jit(solution)/shard_map/ppermute | solution.py:725
  81.7 1.6 %collective-permute-start.23 = (bf16[256,512]{1,0:T(8,128)(2,1)S(1)}, bf16[256,512]{1,0:T(8,128)(2,1)S(1)}, u32[]{:S(2)}, u32[]{:S(2)}) collective-permute-start(bf16[256,512]{1,0:T(8,128)(2,1)S(1)} %collective-permute-done.17.refs_2_.refs_5_), channel_id=1, source_target_pairs={{0,4},{1,9},{2,6},{3,11},{4,0},{5,13},{6,2},{7,15},{8,12},{9,1},{1... | collective-permute-start | bytes 786440 | tf_op jit(solution)/shard_map/ppermute | solution.py:716
  84.0 3.5 %collective-permute-done.15.refs_0_.f_ref = f32[8,4096]{1,0:T(8,128)S(1)} collective-permute-done((f32[8,4096]{1,0:T(8,128)S(1)}, f32[8,4096]{1,0:T(8,128)S(1)}, u32[]{:S(2)}, u32[]{:S(2)}) %collective-permute-start.15) | collective-permute-done | bytes 131104 | tf_op jit(solution)/shard_map/ppermute | solution.py:725
  88.8 2.3 %diverge.1 = (bf16[4096,128]{1,0:T(8,128)(2,1)}, bf16[32,512]{1,0:T(8,128)(2,1)S(1)}, f32[8,512]{1,0:T(8,128)S(1)}) custom-call(f32[8,4096]{1,0:T(8,128)S(1)} %add.23.refs_0_.d_ref, f32[8,4096]{1,0:T(8,128)S(1)} %collective-permute-done.15.refs_0_.f_ref, s32[1,4096]{1,0:T(1,128)S(1)} %bitcast.21, s32[1,8]{1,0:T(1,128)S(1)} %bitcast.22, ...), custom_call_target="tpu_custom_call" | custom-call | bytes 209715 | tf_op jit(solution)/shard_map/diverge/pallas_call | solution.py:457
  92.0 3.0 %collective-permute-done.19 = f32[8,512]{1,0:T(8,128)S(1)} collective-permute-done((f32[8,512]{1,0:T(8,128)S(1)}, f32[8,512]{1,0:T(8,128)S(1)}, u32[]{:S(2)}, u32[]{:S(2)}) %collective-permute-start.19) | collective-permute-done | bytes 16416 | tf_op jit(solution)/shard_map/ppermute | solution.py:716
  96.5 2.0 %collective-permute-start.20 = (f32[8,512]{1,0:T(8,128)S(1)}, f32[8,512]{1,0:T(8,128)S(1)}, u32[]{:S(2)}, u32[]{:S(2)}) collective-permute-start(f32[8,512]{1,0:T(8,128)S(1)} %add.25.refs_2_), channel_id=1, source_target_pairs={{0,8},{1,5},{2,10},{3,7},{4,12},{5,1},{6,14},{7,3},{8,0},{9,13},{1... | collective-permute-start | bytes 49160 | tf_op jit(solution)/shard_map/ppermute | solution.py:716
  98.6 1.9 %collective-permute-done.20 = f32[8,512]{1,0:T(8,128)S(1)} collective-permute-done((f32[8,512]{1,0:T(8,128)S(1)}, f32[8,512]{1,0:T(8,128)S(1)}, u32[]{:S(2)}, u32[]{:S(2)}) %collective-permute-start.20) | collective-permute-done | bytes 16416 | tf_op jit(solution)/shard_map/ppermute | solution.py:716
  100.5 2.0 %collective-permute-start.21 = (f32[8,512]{1,0:T(8,128)S(1)}, f32[8,512]{1,0:T(8,128)S(1)}, u32[]{:S(2)}, u32[]{:S(2)}) collective-permute-start(f32[8,512]{1,0:T(8,128)S(1)} %add.26), channel_id=1, source_target_pairs={{0,16},{1,17},{2,18},{3,19},{4,20},{5,21},{6,22},{7,23},{8,24},{9,... | collective-permute-start | bytes 49160 | tf_op jit(solution)/shard_map/ppermute | solution.py:716
  102.5 2.6 %collective-permute-done.21 = f32[8,512]{1,0:T(8,128)S(1)} collective-permute-done((f32[8,512]{1,0:T(8,128)S(1)}, f32[8,512]{1,0:T(8,128)S(1)}, u32[]{:S(2)}, u32[]{:S(2)}) %collective-permute-start.21) | collective-permute-done | bytes 16416 | tf_op jit(solution)/shard_map/ppermute | solution.py:716
  105.1 2.3 %regroup.1 = (bf16[2048,512]{1,0:T(8,128)(2,1)S(1)}, bf16[512,512]{1,0:T(8,128)(2,1)S(1)}, bf16[512,512]{1,0:T(8,128)(2,1)S(1)}, bf16[512,512]{1,0:T(8,128)(2,1)S(1)}, bf16[512,512]{1,0:T(8,128)(2,1)S(1)}) custom-call(s32[8]{0:T(128)S(1)} %stack.58.ids_ref, s32[1]{0:T(128)} %bitcast.17.place_ref, bf16[256,512]{1,0:T(8,128)(2,1)} %collective-permute-done.27.refs_0_, ...), custom_call_target="tpu_custom_call" | custom-call | bytes 209715 | tf_op jit(solution)/shard_map/regroup/pallas_call | solution.py:502
  109.9 14.8 %grad_logits.1 = (f32[4096,512]{1,0:T(8,128)}, f32[1,1]{1,0:T(1,128)}) custom-call(bf16[4096,2048]{1,0:T(8,128)(2,1)} %e_ref.7, bf16[2048,512]{1,0:T(8,128)(2,1)S(1)} %get-tuple-element.91.g_ref, bf16[4096,512]{1,0:T(8,128)(2,1)} %get-tuple-element.102.u_ref.refs_7_, bf16[4096,128]{1,0:T(8,128)(2,1)} %get-tuple-element.84.d_ref, ...), custom_call_target="tpu_custom_call" | custom-call | tf_op jit(solution)/shard_map/grad_logits/pallas_call | solution.py:583
  124.7 9.8 %grad_expression.2.refs_5_ = f32[4096,512]{1,0:T(8,128)S(1)} custom-call(bf16[1024,512]{1,0:T(8,128)(2,1)S(1)} %copy-done.4, bf16[1152,512]{1,0:T(8,128)(2,1)S(1)} %collective-permute-done.12.refs_1_, bf16[1920,512]{1,0:T(8,128)(2,1)S(1)} %collective-permute-done.22.refs_2_, bf16[512,512]{1,0:T(8,128)(2,1)S(1)} %get-tuple-element.93.refs_3_, ...), custom_call_target="tpu_custom_call" | custom-call | tf_op jit(solution)/shard_map/grad_expression/pallas_call | solution.py:680
  134.6 6.5 %grad_expression.3 = f32[4096,512]{1,0:T(8,128)} custom-call(bf16[1024,512]{1,0:T(8,128)(2,1)S(1)} %copy-done.6, bf16[1152,512]{1,0:T(8,128)(2,1)} %collective-permute-done.26.refs_1_, bf16[1920,512]{1,0:T(8,128)(2,1)S(1)} %collective-permute-done.28.refs_2_, bf16[512,512]{1,0:T(8,128)(2,1)S(1)} %collective-permute-done.29.refs_3_, ...), custom_call_target="tpu_custom_call" | custom-call | tf_op jit(solution)/shard_map/grad_expression/pallas_call | solution.py:680
  (96 shorter events, 21.1 us)
Async XLA Ops:
  2.5 26.2 %collective-permute-start = (bf16[1024,512]{1,0:T(8,128)(2,1)S(1)}, bf16[1024,512]{1,0:T(8,128)(2,1)S(1)}, u32[]{:S(2)}, u32[]{:S(2)}) collective-permute-start(bf16[1024,512]{1,0:T(8,128)(2,1)S(1)} %exp_first.1), channel_id=1, source_target_pairs={{0,2},{1,3},{2,0},{3,1},{4,6},{5,7},{6,4},{7,5},{8,10},{9,11},{10,... | collective-permute-start | bytes 3145736 | tf_op jit(solution)/shard_map/ppermute | solution.py:719
  16.7 12.1 %collective-permute-start.3 = (bf16[272,512]{1,0:T(8,128)(2,1)S(1)}, bf16[272,512]{1,0:T(8,128)(2,1)S(1)}, u32[]{:S(2)}, u32[]{:S(2)}) collective-permute-start(bf16[272,512]{1,0:T(8,128)(2,1)S(1)} %get-tuple-element.62), channel_id=1, source_target_pairs={{0,4},{1,9},{2,6},{3,11},{4,0},{5,13},{6,2},{7,15},{8,12},{9,1},{1... | collective-permute-start | bytes 835592 | tf_op jit(solution)/shard_map/ppermute | solution.py:716
  18.0 10.6 %collective-permute-start.1 = (bf16[256,512]{1,0:T(8,128)(2,1)S(1)}, bf16[256,512]{1,0:T(8,128)(2,1)S(1)}, u32[]{:S(2)}, u32[]{:S(2)}) collective-permute-start(bf16[256,512]{1,0:T(8,128)(2,1)S(1)} %get-tuple-element.59), channel_id=1, source_target_pairs={{0,4},{1,9},{2,6},{3,11},{4,0},{5,13},{6,2},{7,15},{8,12},{9,1},{1... | collective-permute-start | bytes 786440 | tf_op jit(solution)/shard_map/ppermute | solution.py:716
  18.8 9.8 %collective-permute-start.2 = (bf16[256,512]{1,0:T(8,128)(2,1)S(1)}, bf16[256,512]{1,0:T(8,128)(2,1)S(1)}, u32[]{:S(2)}, u32[]{:S(2)}) collective-permute-start(bf16[256,512]{1,0:T(8,128)(2,1)S(1)} %get-tuple-element.60), channel_id=1, source_target_pairs={{0,8},{1,9},{2,10},{3,11},{4,12},{5,13},{6,14},{7,15},{8,0},{9,1},... | collective-permute-start | bytes 786440 | tf_op jit(solution)/shard_map/ppermute | solution.py:725
  28.8 3.7 %collective-permute-start.4 = (bf16[1024,512]{1,0:T(8,128)(2,1)S(1)}, bf16[1024,512]{1,0:T(8,128)(2,1)S(1)}, u32[]{:S(2)}, u32[]{:S(2)}) collective-permute-start(bf16[1024,512]{1,0:T(8,128)(2,1)S(1)} %collective-permute-done.refs_0_), channel_id=1, source_target_pairs={{0,1},{1,0},{2,3},{3,2},{4,5},{5,4},{6,7},{7,6},{8,9},{9,8},{10,11... | collective-permute-start | bytes 3145736 | tf_op jit(solution)/shard_map/ppermute | solution.py:719
  30.3 30.6 %collective-permute-start.12 = (bf16[1152,512]{1,0:T(8,128)(2,1)S(1)}, bf16[1152,512]{1,0:T(8,128)(2,1)S(1)}, u32[]{:S(2)}, u32[]{:S(2)}) collective-permute-start(bf16[1152,512]{1,0:T(8,128)(2,1)S(1)} %copy-done.17), channel_id=1, source_target_pairs={{0,2},{1,3},{2,0},{3,1},{4,6},{5,7},{6,4},{7,5},{8,10},{9,11},{10,... | collective-permute-start | bytes 3538952 | tf_op jit(solution)/shard_map/ppermute | solution.py:719
  30.8 6.5 %collective-permute-start.7 = (bf16[272,512]{1,0:T(8,128)(2,1)S(1)}, bf16[272,512]{1,0:T(8,128)(2,1)S(1)}, u32[]{:S(2)}, u32[]{:S(2)}) collective-permute-start(bf16[272,512]{1,0:T(8,128)(2,1)S(1)} %get-tuple-element.63), channel_id=1, source_target_pairs={{0,8},{1,5},{2,10},{3,7},{4,12},{5,1},{6,14},{7,3},{8,0},{9,13},{1... | collective-permute-start | bytes 835592 | tf_op jit(solution)/shard_map/ppermute | solution.py:716
  37.4 15.8 %collective-permute-start.8 = (bf16[272,512]{1,0:T(8,128)(2,1)S(1)}, bf16[272,512]{1,0:T(8,128)(2,1)S(1)}, u32[]{:S(2)}, u32[]{:S(2)}) collective-permute-start(bf16[272,512]{1,0:T(8,128)(2,1)S(1)} %get-tuple-element.72), channel_id=1, source_target_pairs={{0,16},{1,17},{2,18},{3,19},{4,20},{5,21},{6,22},{7,23},{8,24},{9,... | collective-permute-start | bytes 835592 | tf_op jit(solution)/shard_map/ppermute | solution.py:725
  40.1 12.0 %collective-permute-start.6 = (bf16[256,512]{1,0:T(8,128)(2,1)S(1)}, bf16[256,512]{1,0:T(8,128)(2,1)S(1)}, u32[]{:S(2)}, u32[]{:S(2)}) collective-permute-start(bf16[256,512]{1,0:T(8,128)(2,1)S(1)} %get-tuple-element.68), channel_id=1, source_target_pairs={{0,8},{1,9},{2,10},{3,11},{4,12},{5,13},{6,14},{7,15},{8,0},{9,1},... | collective-permute-start | bytes 786440 | tf_op jit(solution)/shard_map/ppermute | solution.py:725
  41.7 10.5 %collective-permute-start.5 = (bf16[256,512]{1,0:T(8,128)(2,1)S(1)}, bf16[256,512]{1,0:T(8,128)(2,1)S(1)}, u32[]{:S(2)}, u32[]{:S(2)}) collective-permute-start(bf16[256,512]{1,0:T(8,128)(2,1)S(1)} %get-tuple-element.67), channel_id=1, source_target_pairs={{0,4},{1,5},{2,6},{3,7},{4,0},{5,1},{6,2},{7,3},{8,12},{9,13},{10,... | collective-permute-start | bytes 786440 | tf_op jit(solution)/shard_map/ppermute | solution.py:725
  43.1 62.0 %collective-permute-start.22 = (bf16[1920,512]{1,0:T(8,128)(2,1)}, bf16[1920,512]{1,0:T(8,128)(2,1)S(1)}, u32[]{:S(2)}, u32[]{:S(2)}) collective-permute-start(bf16[1920,512]{1,0:T(8,128)(2,1)} %get-tuple-element.88), channel_id=1, source_target_pairs={{0,2},{1,3},{2,0},{3,1},{4,6},{5,7},{6,4},{7,5},{8,10},{9,11},{10,... | collective-permute-start | bytes 5898248 | tf_op jit(solution)/shard_map/ppermute | solution.py:719
  55.6 3.8 %collective-permute-start.10 = (f32[24,256]{1,0:T(8,128)S(1)}, f32[24,256]{1,0:T(8,128)S(1)}, u32[]{:S(2)}, u32[]{:S(2)}) collective-permute-start(f32[24,256]{1,0:T(8,128)S(1)} %add.22.s_ref), channel_id=1, source_target_pairs={{0,4},{1,5},{2,6},{3,7},{4,0},{5,1},{6,2},{7,3},{8,12},{9,13},{10,... | collective-permute-start | bytes 73736 | tf_op jit(solution)/shard_map/ppermute | solution.py:725
  59.4 4.8 %collective-permute-start.11 = (f32[24,256]{1,0:T(8,128)S(1)}, f32[24,256]{1,0:T(8,128)S(1)}, u32[]{:S(2)}, u32[]{:S(2)}) collective-permute-start(f32[24,256]{1,0:T(8,128)S(1)} %collective-permute-done.10), channel_id=1, source_target_pairs={{0,6},{1,7},{2,4},{3,5},{4,2},{5,3},{6,0},{7,1},{8,14},{9,15},{10,... | collective-permute-start | bytes 73736 | tf_op jit(solution)/shard_map/ppermute | solution.py:725
  66.4 1.4 collective-permute-start.13
  67.9 13.8 %collective-permute-start.17 = (bf16[256,512]{1,0:T(8,128)(2,1)S(1)}, bf16[256,512]{1,0:T(8,128)(2,1)S(1)}, u32[]{:S(2)}, u32[]{:S(2)}) collective-permute-start(bf16[256,512]{1,0:T(8,128)(2,1)S(1)} %hold.3), channel_id=1, source_target_pairs={{0,8},{1,5},{2,10},{3,7},{4,12},{5,1},{6,14},{7,3},{8,0},{9,13},{1... | collective-permute-start | bytes 786440 | tf_op jit(solution)/shard_map/ppermute | solution.py:716
  69.3 14.7 %collective-permute-start.18 = (bf16[256,512]{1,0:T(8,128)(2,1)S(1)}, bf16[256,512]{1,0:T(8,128)(2,1)S(1)}, u32[]{:S(2)}, u32[]{:S(2)}) collective-permute-start(bf16[256,512]{1,0:T(8,128)(2,1)S(1)} %get-tuple-element.81.refs_1_.refs_7_), channel_id=1, source_target_pairs={{0,16},{1,17},{2,18},{3,19},{4,20},{5,21},{6,22},{7,23},{8,24},{9,... | collective-permute-start | bytes 786440 | tf_op jit(solution)/shard_map/ppermute | solution.py:716
  71.9 12.1 %collective-permute-start.16 = (bf16[256,512]{1,0:T(8,128)(2,1)S(1)}, bf16[256,512]{1,0:T(8,128)(2,1)S(1)}, u32[]{:S(2)}, u32[]{:S(2)}) collective-permute-start(bf16[256,512]{1,0:T(8,128)(2,1)S(1)} %hold.3), channel_id=1, source_target_pairs={{0,4},{1,9},{2,6},{3,11},{4,0},{5,13},{6,2},{7,15},{8,12},{9,1},{1... | collective-permute-start | bytes 786440 | tf_op jit(solution)/shard_map/ppermute | solution.py:716
  73.4 7.7 %collective-permute-start.14 = (f32[8,4096]{1,0:T(8,128)S(1)}, f32[8,4096]{1,0:T(8,128)S(1)}, u32[]{:S(2)}, u32[]{:S(2)}) collective-permute-start(f32[8,4096]{1,0:T(8,128)S(1)} %add.23.refs_0_.d_ref), channel_id=1, source_target_pairs={{0,4},{1,5},{2,6},{3,7},{4,0},{5,1},{6,2},{7,3},{8,12},{9,13},{10,... | collective-permute-start | bytes 393224 | tf_op jit(solution)/shard_map/ppermute | solution.py:725
  81.1 6.3 %collective-permute-start.15 = (f32[8,4096]{1,0:T(8,128)S(1)}, f32[8,4096]{1,0:T(8,128)S(1)}, u32[]{:S(2)}, u32[]{:S(2)}) collective-permute-start(f32[8,4096]{1,0:T(8,128)S(1)} %collective-permute-done.14), channel_id=1, source_target_pairs={{0,6},{1,7},{2,4},{3,5},{4,2},{5,3},{6,0},{7,1},{8,14},{9,15},{10,... | collective-permute-start | bytes 393224 | tf_op jit(solution)/shard_map/ppermute | solution.py:725
  81.7 13.3 %collective-permute-start.23 = (bf16[256,512]{1,0:T(8,128)(2,1)S(1)}, bf16[256,512]{1,0:T(8,128)(2,1)S(1)}, u32[]{:S(2)}, u32[]{:S(2)}) collective-permute-start(bf16[256,512]{1,0:T(8,128)(2,1)S(1)} %collective-permute-done.17.refs_2_.refs_5_), channel_id=1, source_target_pairs={{0,4},{1,9},{2,6},{3,11},{4,0},{5,13},{6,2},{7,15},{8,12},{9,1},{1... | collective-permute-start | bytes 786440 | tf_op jit(solution)/shard_map/ppermute | solution.py:716
  87.5 7.5 %collective-permute-start.24 = (bf16[256,512]{1,0:T(8,128)(2,1)S(1)}, bf16[256,512]{1,0:T(8,128)(2,1)S(1)}, u32[]{:S(2)}, u32[]{:S(2)}) collective-permute-start(bf16[256,512]{1,0:T(8,128)(2,1)S(1)} %hold.4.refs_6_), channel_id=1, source_target_pairs={{0,4},{1,9},{2,6},{3,11},{4,0},{5,13},{6,2},{7,15},{8,12},{9,1},{1... | collective-permute-start | bytes 786440 | tf_op jit(solution)/shard_map/ppermute | solution.py:716
  88.8 6.4 %collective-permute-start.25 = (bf16[256,512]{1,0:T(8,128)(2,1)S(1)}, bf16[256,512]{1,0:T(8,128)(2,1)S(1)}, u32[]{:S(2)}, u32[]{:S(2)}) collective-permute-start(bf16[256,512]{1,0:T(8,128)(2,1)S(1)} %hold.4.refs_6_), channel_id=1, source_target_pairs={{0,8},{1,5},{2,10},{3,7},{4,12},{5,1},{6,14},{7,3},{8,0},{9,13},{1... | collective-permute-start | bytes 786440 | tf_op jit(solution)/shard_map/ppermute | solution.py:716
  91.2 3.8 %collective-permute-start.19 = (f32[8,512]{1,0:T(8,128)S(1)}, f32[8,512]{1,0:T(8,128)S(1)}, u32[]{:S(2)}, u32[]{:S(2)}) collective-permute-start(f32[8,512]{1,0:T(8,128)S(1)} %add.24), channel_id=1, source_target_pairs={{0,4},{1,9},{2,6},{3,11},{4,0},{5,13},{6,2},{7,15},{8,12},{9,1},{1... | collective-permute-start | bytes 49160 | tf_op jit(solution)/shard_map/ppermute | solution.py:716
  95.7 9.4 %collective-permute-start.26 = (bf16[1152,512]{1,0:T(8,128)(2,1)S(1)}, bf16[1152,512]{1,0:T(8,128)(2,1)}, u32[]{:S(2)}, u32[]{:S(2)}) collective-permute-start(bf16[1152,512]{1,0:T(8,128)(2,1)S(1)} %collective-permute-done.12.refs_1_), channel_id=1, source_target_pairs={{0,1},{1,0},{2,3},{3,2},{4,5},{5,4},{6,7},{7,6},{8,9},{9,8},{10,11... | collective-permute-start | bytes 3538952 | tf_op jit(solution)/shard_map/ppermute | solution.py:719
  95.7 9.4 %collective-permute-start.27 = (bf16[256,512]{1,0:T(8,128)(2,1)S(1)}, bf16[256,512]{1,0:T(8,128)(2,1)}, u32[]{:S(2)}, u32[]{:S(2)}) collective-permute-start(bf16[256,512]{1,0:T(8,128)(2,1)S(1)} %hold.5.refs_4_), channel_id=1, source_target_pairs={{0,4},{1,9},{2,6},{3,11},{4,0},{5,13},{6,2},{7,15},{8,12},{9,1},{1... | collective-permute-start | bytes 786440 | tf_op jit(solution)/shard_map/ppermute | solution.py:716
  96.5 3.9 %collective-permute-start.20 = (f32[8,512]{1,0:T(8,128)S(1)}, f32[8,512]{1,0:T(8,128)S(1)}, u32[]{:S(2)}, u32[]{:S(2)}) collective-permute-start(f32[8,512]{1,0:T(8,128)S(1)} %add.25.refs_2_), channel_id=1, source_target_pairs={{0,8},{1,5},{2,10},{3,7},{4,12},{5,1},{6,14},{7,3},{8,0},{9,13},{1... | collective-permute-start | bytes 49160 | tf_op jit(solution)/shard_map/ppermute | solution.py:716
  100.5 4.6 %collective-permute-start.21 = (f32[8,512]{1,0:T(8,128)S(1)}, f32[8,512]{1,0:T(8,128)S(1)}, u32[]{:S(2)}, u32[]{:S(2)}) collective-permute-start(f32[8,512]{1,0:T(8,128)S(1)} %add.26), channel_id=1, source_target_pairs={{0,16},{1,17},{2,18},{3,19},{4,20},{5,21},{6,22},{7,23},{8,24},{9,... | collective-permute-start | bytes 49160 | tf_op jit(solution)/shard_map/ppermute | solution.py:716
  107.5 17.3 %collective-permute-start.32 = (bf16[4096,512]{1,0:T(8,128)(2,1)}, bf16[4096,512]{1,0:T(8,128)(2,1)S(1)}, u32[]{:S(2)}, u32[]{:S(2)}) collective-permute-start(bf16[4096,512]{1,0:T(8,128)(2,1)} %get-tuple-element.102.u_ref.refs_7_), channel_id=1, source_target_pairs={{0,1},{1,0},{2,3},{3,2},{4,5},{5,4},{6,7},{7,6},{8,9},{9,8},{10,11... | collective-permute-start | bytes 12582920 | tf_op jit(solution)/shard_map/ppermute | solution.py:719
  107.5 27.0 %collective-permute-start.28 = (bf16[1920,512]{1,0:T(8,128)(2,1)S(1)}, bf16[1920,512]{1,0:T(8,128)(2,1)S(1)}, u32[]{:S(2)}, u32[]{:S(2)}) collective-permute-start(bf16[1920,512]{1,0:T(8,128)(2,1)S(1)} %collective-permute-done.22.refs_2_), channel_id=1, source_target_pairs={{0,1},{1,0},{2,3},{3,2},{4,5},{5,4},{6,7},{7,6},{8,9},{9,8},{10,11... | collective-permute-start | bytes 5898248 | tf_op jit(solution)/shard_map/ppermute | solution.py:719
  108.0 16.7 %collective-permute-start.30 = (bf16[512,512]{1,0:T(8,128)(2,1)S(1)}, bf16[512,512]{1,0:T(8,128)(2,1)S(1)}, u32[]{:S(2)}, u32[]{:S(2)}) collective-permute-start(bf16[512,512]{1,0:T(8,128)(2,1)S(1)} %get-tuple-element.97), channel_id=1, source_target_pairs={{0,1},{1,0},{2,3},{3,2},{4,5},{5,4},{6,7},{7,6},{8,9},{9,8},{10,11... | collective-permute-start | bytes 1572872 | tf_op jit(solution)/shard_map/ppermute | solution.py:719
  108.1 16.6 %collective-permute-start.31 = (bf16[512,512]{1,0:T(8,128)(2,1)S(1)}, bf16[512,512]{1,0:T(8,128)(2,1)S(1)}, u32[]{:S(2)}, u32[]{:S(2)}) collective-permute-start(bf16[512,512]{1,0:T(8,128)(2,1)S(1)} %get-tuple-element.98), channel_id=1, source_target_pairs={{0,2},{1,3},{2,0},{3,1},{4,6},{5,7},{6,4},{7,5},{8,10},{9,11},{10,... | collective-permute-start | bytes 1572872 | tf_op jit(solution)/shard_map/ppermute | solution.py:719
  109.4 25.1 %collective-permute-start.29 = (bf16[512,512]{1,0:T(8,128)(2,1)S(1)}, bf16[512,512]{1,0:T(8,128)(2,1)S(1)}, u32[]{:S(2)}, u32[]{:S(2)}) collective-permute-start(bf16[512,512]{1,0:T(8,128)(2,1)S(1)} %get-tuple-element.99), channel_id=1, source_target_pairs={{0,3},{1,2},{2,1},{3,0},{4,7},{5,6},{6,5},{7,4},{8,11},{9,10},{10,... | collective-permute-start | bytes 1572872 | tf_op jit(solution)/shard_map/ppermute | solution.py:719
  (19 other events, 236.3 us)

commit v6 on v5

--- a/solution.py
+++ b/solution.py
@@ -551,7 +551,7 @@
         def store(k):
             row, size = runs[k]
             return pltpu.make_async_copy(
-                out.at[k % 2, pl.ds(0, size)], o_ref.at[pl.ds(row, size)], out_sem.at[k % 2]
+                out.at[k % 3, pl.ds(0, size)], o_ref.at[pl.ds(row, size)], out_sem.at[k % 3]
             )
 
         for copy in fetch(0):
@@ -572,12 +572,12 @@
                 for copy in fetch(following):
                     copy.start()
                 following += 1
-            if k >= 2:
-                store(k - 2).wait()
+            if k >= 3:
+                store(k - 3).wait()
             acc = dot(e_buf[k % slots, 0:size], held[...])
-            out[k % 2, 0:size] = (u_buf[k % slots, 0:size].astype(f32) * kept) * acc
+            out[k % 3, 0:size] = (u_buf[k % slots, 0:size].astype(f32) * kept) * acc
             store(k).start()
-        for k in range(len(runs) - 2, len(runs)):
+        for k in range(len(runs) - 3, len(runs)):
             store(k).wait()
 
     return pl.pallas_call(
@@ -589,9 +589,9 @@
             pltpu.VMEM((genes + 128, spots), bf16),
             pltpu.VMEM((slots, tile, genes + 128), bf16),
             pltpu.VMEM((slots, tile, spots), bf16),
-            pltpu.VMEM((2, tile, spots), f32),
+            pltpu.VMEM((3, tile, spots), f32),
             pltpu.SemaphoreType.DMA((slots, 3)),
-            pltpu.SemaphoreType.DMA((2,)),
+            pltpu.SemaphoreType.DMA((3,)),
         ],
         compiler_params=params(),
         cost_estimate=cost(
@@ -650,7 +650,7 @@
 
         def store(k):
             return pltpu.make_async_copy(
-                out.at[k % 2], o_ref.at[pl.ds(k * tile, tile)], out_sem.at[k % 2]
+                out.at[k % 3], o_ref.at[pl.ds(k * tile, tile)], out_sem.at[k % 3]
             )
 
         for k in range(slots):
@@ -665,15 +665,15 @@
             if own:
                 o_ref[at, :] = dot(held[k % slots], g_buf[...], NT) * scale
             else:
-                if k >= 2:
-                    store(k - 2).wait()
-                out[k % 2] = dot(held[k % slots], g_buf[...], NT) * scale + w_refs[0][at, :]
+                if k >= 3:
+                    store(k - 3).wait()
+                out[k % 3] = dot(held[k % slots], g_buf[...], NT) * scale + w_refs[0][at, :]
                 store(k).start()
             if k + slots < len(tiles):
                 for copy in fetch(k + slots):
                     copy.start()
         if not own:
-            for k in range(len(tiles) - 2, len(tiles)):
+            for k in range(len(tiles) - 3, len(tiles)):
                 store(k).wait()
 
     rows = len(tiles) * tile
@@ -685,9 +685,9 @@
         scratch_shapes=[
             pltpu.VMEM((slots, tile, count * spots), bf16),
             pltpu.VMEM((genes, count * spots), bf16),
-            pltpu.VMEM((2, tile, genes), f32),
+            pltpu.VMEM((3, tile, genes), f32),
             pltpu.SemaphoreType.DMA((slots, count, most)),
-            pltpu.SemaphoreType.DMA((2,)),
+            pltpu.SemaphoreType.DMA((3,)),
         ],
         compiler_params=params(),
         cost_estimate=cost(

time: 141 us -> 140 us (level)
  no operation moved by 1% of the time
where the time goes in v6:
time: 140 us
  Pallas kernels  61.8 us (44%)
  starting transfers between devices  37.7 us (27%)
  waiting for transfers between devices  36.5 us (26%)
  local copies, waits for them, and re-layouts  2.9 us (2%)
    ppermute x8, waiting for transfers between devices, over_cell(): return lax.ppermute(value, ('cell', 'spot'), pairs)  25.2 us
    ppermute x13, starting transfers between devices, across(): return lax.ppermute(value, ('cell', 'spot'), pairs)  17.8 us
    pallas_call x2, Pallas kernels, expr_call(): pl.pallas_call(body, in_specs=[ANY] * len(flat) + [VMEM] * (count + 1) +...  15 us
    pallas_call x1, Pallas kernels, logit_call(): pl.pallas_call(body, in_specs=[HBM, VMEM, HBM, HBM] + [VMEM] * 3, out_spe...  14.8 us
    pallas_call x1, Pallas kernels, exp_call(): pl.pallas_call(body, in_specs=[SMEM, HBM, HBM, HBM], out_specs=[HBM] * le...  11 us
    ppermute x8, starting transfers between devices, over_cell(): return lax.ppermute(value, ('cell', 'spot'), pairs)  11 us
    pallas_call x2, Pallas kernels, part_call(): pl.pallas_call(body, in_specs=[SMEM, HBM, VMEM] + [VMEM] * len(came), out...  11 us
    ppermute x12, starting transfers between devices, over_spot(): return lax.ppermute(value, 'spot', [(j, j ^ mask) for j in range(m)])  8.91 us
  transfers between devices with their start and end apart: 33, of which 15 were waited for; matrix products, arithmetic and copies ran while one was open for 0% of the time, Pallas kernels for 37%

profile of v6, /device:TPU:0, one launch (start us, length us, event | category | flops | bytes accessed | tf_op | source)
XLA Modules:
  0.0 140.0 jit_solution(10041558276060588201)
XLA Ops:
  0.6 1.9 %exp_first.1 = bf16[1024,512]{1,0:T(8,128)(2,1)S(1)} custom-call(f32[4096,512]{1,0:T(8,128)} %x_ref.3, s32[32,128]{1,0:T(8,128)} %bitcast.19), custom_call_target="tpu_custom_call" | custom-call | bytes 157286 | tf_op jit(solution)/shard_map/exp_first/pallas_call | solution.py:89
  2.5 3.0 %collective-permute-start = (bf16[1024,512]{1,0:T(8,128)(2,1)S(1)}, bf16[1024,512]{1,0:T(8,128)(2,1)S(1)}, u32[]{:S(2)}, u32[]{:S(2)}) collective-permute-start(bf16[1024,512]{1,0:T(8,128)(2,1)S(1)} %exp_first.1), channel_id=1, source_target_pairs={{0,2},{1,3},{2,0},{3,1},{4,6},{5,7},{6,4},{7,5},{8,10},{9,11},{10,... | collective-permute-start | bytes 3145736 | tf_op jit(solution)/shard_map/ppermute | solution.py:719
  5.6 11.0 %exp_rows.1 = (bf16[1152,512]{1,0:T(8,128)(2,1)}, bf16[1920,512]{1,0:T(8,128)(2,1)}, bf16[4096,512]{1,0:T(8,128)(2,1)}, f32[8,512]{1,0:T(8,128)S(1)}, bf16[272,5...) custom-call(s32[8]{0:T(128)S(1)} %stack.65.ids_ref, f32[4096,512]{1,0:T(8,128)} %x_ref.3, ...), custom_call_target="tpu_custom_call" | custom-call | bytes 838860 | tf_op jit(solution)/shard_map/exp_rows/pallas_call | solution.py:181
  20.1 2.2 %copy-done = bf16[4096,512]{1,0:T(8,128)(2,1)S(1)} copy-done((bf16[4096,512]{1,0:T(8,128)(2,1)S(1)}, bf16[4096,512]{1,0:T(8,128)(2,1)}, u32[]{:S(2)}) %copy-start) | copy-done | bytes 4194328
  22.3 6.3 %part.2 = (f32[256,512]{1,0:T(8,128)S(1)}, f32[256,512]{1,0:T(8,128)S(1)}, bf16[256,512]{1,0:T(8,128)(2,1)S(1)}) custom-call(s32[8]{0:T(128)S(1)} %stack.65.ids_ref, bf16[4096,2048]{1,0:T(8,128)(2,1)} %e_ref.7, bf16[4096,512]{1,0:T(8,128)(2,1)S(1)} %copy-done), custom_call_target="tpu_custom_call" | custom-call | flops 161061280 | bytes 524288 | tf_op jit(solution)/shard_map/part/pallas_call | solution.py:226
  28.8 1.5 %collective-permute-start.4 = (bf16[1024,512]{1,0:T(8,128)(2,1)S(1)}, bf16[1024,512]{1,0:T(8,128)(2,1)S(1)}, u32[]{:S(2)}, u32[]{:S(2)}) collective-permute-start(bf16[1024,512]{1,0:T(8,128)(2,1)S(1)} %collective-permute-done.refs_0_), channel_id=1, source_target_pairs={{0,1},{1,0},{2,3},{3,2},{4,5},{5,4},{6,7},{7,6},{8,9},{9,8},{10,11... | collective-permute-start | bytes 3145736 | tf_op jit(solution)/shard_map/ppermute | solution.py:719
  30.8 1.6 %collective-permute-start.7 = (bf16[272,512]{1,0:T(8,128)(2,1)S(1)}, bf16[272,512]{1,0:T(8,128)(2,1)S(1)}, u32[]{:S(2)}, u32[]{:S(2)}) collective-permute-start(bf16[272,512]{1,0:T(8,128)(2,1)S(1)} %get-tuple-element.63), channel_id=1, source_target_pairs={{0,8},{1,5},{2,10},{3,7},{4,12},{5,1},{6,14},{7,3},{8,0},{9,13},{1... | collective-permute-start | bytes 835592 | tf_op jit(solution)/shard_map/ppermute | solution.py:716
  32.5 4.7 %part.3 = (bf16[256,512]{1,0:T(8,128)(2,1)S(1)}, f32[256,512]{1,0:T(8,128)S(1)}) custom-call(s32[8]{0:T(128)S(1)} %stack.65.ids_ref, bf16[4096,2048]{1,0:T(8,128)(2,1)} %e_ref.7, bf16[4096,512]{1,0:T(8,128)(2,1)S(1)} %copy-done.1, bf16[256,512]{1,0:T(8,128)(2,1)S(1)} %collective-permute-done.2.refs_0_), custom_call_target="tpu_custom_call" | custom-call | flops 107374184 | bytes 419430 | tf_op jit(solution)/shard_map/part/pallas_call | solution.py:226
  37.4 2.7 %collective-permute-start.8 = (bf16[272,512]{1,0:T(8,128)(2,1)S(1)}, bf16[272,512]{1,0:T(8,128)(2,1)S(1)}, u32[]{:S(2)}, u32[]{:S(2)}) collective-permute-start(bf16[272,512]{1,0:T(8,128)(2,1)S(1)} %get-tuple-element.72), channel_id=1, source_target_pairs={{0,16},{1,17},{2,18},{3,19},{4,20},{5,21},{6,22},{7,23},{8,24},{9,... | collective-permute-start | bytes 835592 | tf_op jit(solution)/shard_map/ppermute | solution.py:725
  40.1 1.6 %collective-permute-start.6 = (bf16[256,512]{1,0:T(8,128)(2,1)S(1)}, bf16[256,512]{1,0:T(8,128)(2,1)S(1)}, u32[]{:S(2)}, u32[]{:S(2)}) collective-permute-start(bf16[256,512]{1,0:T(8,128)(2,1)S(1)} %get-tuple-element.68), channel_id=1, source_target_pairs={{0,8},{1,9},{2,10},{3,11},{4,12},{5,13},{6,14},{7,15},{8,0},{9,1},... | collective-permute-start | bytes 786440 | tf_op jit(solution)/shard_map/ppermute | solution.py:725
  41.7 1.5 %collective-permute-start.5 = (bf16[256,512]{1,0:T(8,128)(2,1)S(1)}, bf16[256,512]{1,0:T(8,128)(2,1)S(1)}, u32[]{:S(2)}, u32[]{:S(2)}) collective-permute-start(bf16[256,512]{1,0:T(8,128)(2,1)S(1)} %get-tuple-element.67), channel_id=1, source_target_pairs={{0,4},{1,5},{2,6},{3,7},{4,0},{5,1},{6,2},{7,3},{8,12},{9,13},{10,... | collective-permute-start | bytes 786440 | tf_op jit(solution)/shard_map/ppermute | solution.py:725
  43.1 1.4 %collective-permute-start.22 = (bf16[1920,512]{1,0:T(8,128)(2,1)}, bf16[1920,512]{1,0:T(8,128)(2,1)S(1)}, u32[]{:S(2)}, u32[]{:S(2)}) collective-permute-start(bf16[1920,512]{1,0:T(8,128)(2,1)} %get-tuple-element.88), channel_id=1, source_target_pairs={{0,2},{1,3},{2,0},{3,1},{4,6},{5,7},{6,4},{7,5},{8,10},{9,11},{10,... | collective-permute-start | bytes 5898248 | tf_op jit(solution)/shard_map/ppermute | solution.py:719
  44.6 7.5 %collective-permute-done.6.refs_2_ = bf16[256,512]{1,0:T(8,128)(2,1)S(1)} collective-permute-done((bf16[256,512]{1,0:T(8,128)(2,1)S(1)}, bf16[256,512]{1,0:T(8,128)(2,1)S(1)}, u32[]{:S(2)}, u32[]{:S(2)}) %collective-permute-start.6) | collective-permute-done | bytes 262176 | tf_op jit(solution)/shard_map/ppermute | solution.py:725
  57.0 2.5 %collective-permute-done.10 = f32[24,256]{1,0:T(8,128)S(1)} collective-permute-done((f32[24,256]{1,0:T(8,128)S(1)}, f32[24,256]{1,0:T(8,128)S(1)}, u32[]{:S(2)}, u32[]{:S(2)}) %collective-permute-start.10) | collective-permute-done | bytes 24608 | tf_op jit(solution)/shard_map/ppermute | solution.py:725
  60.9 3.4 %collective-permute-done.11.f_ref = f32[24,256]{1,0:T(8,128)S(1)} collective-permute-done((f32[24,256]{1,0:T(8,128)S(1)}, f32[24,256]{1,0:T(8,128)S(1)}, u32[]{:S(2)}, u32[]{:S(2)}) %collective-permute-start.11) | collective-permute-done | bytes 24608 | tf_op jit(solution)/shard_map/ppermute | solution.py:725
  65.0 1.5 %density.1 = f32[8,4096]{1,0:T(8,128)S(1)} custom-call(bf16[4096,512]{1,0:T(8,128)(2,1)S(1)} %copy-done.1, f32[8,512]{1,0:T(8,128)S(1)} %get-tuple-element.103.tops_ref.refs_6_.refs_4_, f32[8,512]{1,0:T(8,128)S(1)} %fusion.refs_6_.m_ref), custom_call_target="tpu_custom_call" | custom-call | bytes 209715 | tf_op jit(solution)/shard_map/density/pallas_call | solution.py:405
  67.9 1.4 %collective-permute-start.17 = (bf16[256,512]{1,0:T(8,128)(2,1)S(1)}, bf16[256,512]{1,0:T(8,128)(2,1)S(1)}, u32[]{:S(2)}, u32[]{:S(2)}) collective-permute-start(bf16[256,512]{1,0:T(8,128)(2,1)S(1)} %hold.3), channel_id=1, source_target_pairs={{0,8},{1,5},{2,10},{3,7},{4,12},{5,1},{6,14},{7,3},{8,0},{9,13},{1... | collective-permute-start | bytes 786440 | tf_op jit(solution)/shard_map/ppermute | solution.py:716
  69.3 2.7 %collective-permute-start.18 = (bf16[256,512]{1,0:T(8,128)(2,1)S(1)}, bf16[256,512]{1,0:T(8,128)(2,1)S(1)}, u32[]{:S(2)}, u32[]{:S(2)}) collective-permute-start(bf16[256,512]{1,0:T(8,128)(2,1)S(1)} %get-tuple-element.81.refs_1_.refs_7_), channel_id=1, source_target_pairs={{0,16},{1,17},{2,18},{3,19},{4,20},{5,21},{6,22},{7,23},{8,24},{9,... | collective-permute-start | bytes 786440 | tf_op jit(solution)/shard_map/ppermute | solution.py:716
  71.9 1.5 %collective-permute-start.16 = (bf16[256,512]{1,0:T(8,128)(2,1)S(1)}, bf16[256,512]{1,0:T(8,128)(2,1)S(1)}, u32[]{:S(2)}, u32[]{:S(2)}) collective-permute-start(bf16[256,512]{1,0:T(8,128)(2,1)S(1)} %hold.3), channel_id=1, source_target_pairs={{0,4},{1,9},{2,6},{3,11},{4,0},{5,13},{6,2},{7,15},{8,12},{9,1},{1... | collective-permute-start | bytes 786440 | tf_op jit(solution)/shard_map/ppermute | solution.py:716
  74.0 7.2 %collective-permute-done.14 = f32[8,4096]{1,0:T(8,128)S(1)} collective-permute-done((f32[8,4096]{1,0:T(8,128)S(1)}, f32[8,4096]{1,0:T(8,128)S(1)}, u32[]{:S(2)}, u32[]{:S(2)}) %collective-permute-start.14) | collective-permute-done | bytes 131104 | tf_op jit(solution)/shard_map/ppermute | solution.py:725
  81.7 1.6 %collective-permute-start.23 = (bf16[256,512]{1,0:T(8,128)(2,1)S(1)}, bf16[256,512]{1,0:T(8,128)(2,1)S(1)}, u32[]{:S(2)}, u32[]{:S(2)}) collective-permute-start(bf16[256,512]{1,0:T(8,128)(2,1)S(1)} %collective-permute-done.17.refs_2_.refs_5_), channel_id=1, source_target_pairs={{0,4},{1,9},{2,6},{3,11},{4,0},{5,13},{6,2},{7,15},{8,12},{9,1},{1... | collective-permute-start | bytes 786440 | tf_op jit(solution)/shard_map/ppermute | solution.py:716
  84.0 3.5 %collective-permute-done.15.refs_0_.f_ref = f32[8,4096]{1,0:T(8,128)S(1)} collective-permute-done((f32[8,4096]{1,0:T(8,128)S(1)}, f32[8,4096]{1,0:T(8,128)S(1)}, u32[]{:S(2)}, u32[]{:S(2)}) %collective-permute-start.15) | collective-permute-done | bytes 131104 | tf_op jit(solution)/shard_map/ppermute | solution.py:725
  88.8 2.3 %diverge.1 = (bf16[4096,128]{1,0:T(8,128)(2,1)}, bf16[32,512]{1,0:T(8,128)(2,1)S(1)}, f32[8,512]{1,0:T(8,128)S(1)}) custom-call(f32[8,4096]{1,0:T(8,128)S(1)} %add.23.refs_0_.d_ref, f32[8,4096]{1,0:T(8,128)S(1)} %collective-permute-done.15.refs_0_.f_ref, s32[1,4096]{1,0:T(1,128)S(1)} %bitcast.21, s32[1,8]{1,0:T(1,128)S(1)} %bitcast.22, ...), custom_call_target="tpu_custom_call" | custom-call | bytes 209715 | tf_op jit(solution)/shard_map/diverge/pallas_call | solution.py:457
  92.0 3.0 %collective-permute-done.19 = f32[8,512]{1,0:T(8,128)S(1)} collective-permute-done((f32[8,512]{1,0:T(8,128)S(1)}, f32[8,512]{1,0:T(8,128)S(1)}, u32[]{:S(2)}, u32[]{:S(2)}) %collective-permute-start.19) | collective-permute-done | bytes 16416 | tf_op jit(solution)/shard_map/ppermute | solution.py:716
  96.5 2.0 %collective-permute-start.20 = (f32[8,512]{1,0:T(8,128)S(1)}, f32[8,512]{1,0:T(8,128)S(1)}, u32[]{:S(2)}, u32[]{:S(2)}) collective-permute-start(f32[8,512]{1,0:T(8,128)S(1)} %add.25.refs_2_), channel_id=1, source_target_pairs={{0,8},{1,5},{2,10},{3,7},{4,12},{5,1},{6,14},{7,3},{8,0},{9,13},{1... | collective-permute-start | bytes 49160 | tf_op jit(solution)/shard_map/ppermute | solution.py:716
  98.6 1.9 %collective-permute-done.20 = f32[8,512]{1,0:T(8,128)S(1)} collective-permute-done((f32[8,512]{1,0:T(8,128)S(1)}, f32[8,512]{1,0:T(8,128)S(1)}, u32[]{:S(2)}, u32[]{:S(2)}) %collective-permute-start.20) | collective-permute-done | bytes 16416 | tf_op jit(solution)/shard_map/ppermute | solution.py:716
  100.5 2.0 %collective-permute-start.21 = (f32[8,512]{1,0:T(8,128)S(1)}, f32[8,512]{1,0:T(8,128)S(1)}, u32[]{:S(2)}, u32[]{:S(2)}) collective-permute-start(f32[8,512]{1,0:T(8,128)S(1)} %add.26), channel_id=1, source_target_pairs={{0,16},{1,17},{2,18},{3,19},{4,20},{5,21},{6,22},{7,23},{8,24},{9,... | collective-permute-start | bytes 49160 | tf_op jit(solution)/shard_map/ppermute | solution.py:716
  102.5 2.6 %collective-permute-done.21 = f32[8,512]{1,0:T(8,128)S(1)} collective-permute-done((f32[8,512]{1,0:T(8,128)S(1)}, f32[8,512]{1,0:T(8,128)S(1)}, u32[]{:S(2)}, u32[]{:S(2)}) %collective-permute-start.21) | collective-permute-done | bytes 16416 | tf_op jit(solution)/shard_map/ppermute | solution.py:716
  105.1 2.3 %regroup.1 = (bf16[2048,512]{1,0:T(8,128)(2,1)S(1)}, bf16[512,512]{1,0:T(8,128)(2,1)S(1)}, bf16[512,512]{1,0:T(8,128)(2,1)S(1)}, bf16[512,512]{1,0:T(8,128)(2,1)S(1)}, bf16[512,512]{1,0:T(8,128)(2,1)S(1)}) custom-call(s32[8]{0:T(128)S(1)} %stack.58.ids_ref, s32[1]{0:T(128)} %bitcast.17.place_ref, bf16[256,512]{1,0:T(8,128)(2,1)} %collective-permute-done.27.refs_0_, ...), custom_call_target="tpu_custom_call" | custom-call | bytes 209715 | tf_op jit(solution)/shard_map/regroup/pallas_call | solution.py:502
  109.9 14.8 %grad_logits.1 = (f32[4096,512]{1,0:T(8,128)}, f32[1,1]{1,0:T(1,128)}) custom-call(bf16[4096,2048]{1,0:T(8,128)(2,1)} %e_ref.7, bf16[2048,512]{1,0:T(8,128)(2,1)S(1)} %get-tuple-element.91.g_ref, bf16[4096,512]{1,0:T(8,128)(2,1)} %get-tuple-element.102.u_ref.refs_7_, bf16[4096,128]{1,0:T(8,128)(2,1)} %get-tuple-element.84.d_ref, ...), custom_call_target="tpu_custom_call" | custom-call | tf_op jit(solution)/shard_map/grad_logits/pallas_call | solution.py:583
  124.7 9.8 %grad_expression.2.refs_5_ = f32[4096,512]{1,0:T(8,128)S(1)} custom-call(bf16[1024,512]{1,0:T(8,128)(2,1)S(1)} %copy-done.4, bf16[1152,512]{1,0:T(8,128)(2,1)S(1)} %collective-permute-done.12.refs_1_, bf16[1920,512]{1,0:T(8,128)(2,1)S(1)} %collective-permute-done.22.refs_2_, bf16[512,512]{1,0:T(8,128)(2,1)S(1)} %get-tuple-element.93.refs_3_, ...), custom_call_target="tpu_custom_call" | custom-call | tf_op jit(solution)/shard_map/grad_expression/pallas_call | solution.py:680
  134.6 5.2 %grad_expression.3 = f32[4096,512]{1,0:T(8,128)} custom-call(bf16[1024,512]{1,0:T(8,128)(2,1)S(1)} %copy-done.6, bf16[1152,512]{1,0:T(8,128)(2,1)} %collective-permute-done.26.refs_1_, bf16[1920,512]{1,0:T(8,128)(2,1)S(1)} %collective-permute-done.28.refs_2_, bf16[512,512]{1,0:T(8,128)(2,1)S(1)} %collective-permute-done.29.refs_3_, ...), custom_call_target="tpu_custom_call" | custom-call | tf_op jit(solution)/shard_map/grad_expression/pallas_call | solution.py:680
  (96 shorter events, 21.1 us)
Async XLA Ops:
  2.5 26.2 %collective-permute-start = (bf16[1024,512]{1,0:T(8,128)(2,1)S(1)}, bf16[1024,512]{1,0:T(8,128)(2,1)S(1)}, u32[]{:S(2)}, u32[]{:S(2)}) collective-permute-start(bf16[1024,512]{1,0:T(8,128)(2,1)S(1)} %exp_first.1), channel_id=1, source_target_pairs={{0,2},{1,3},{2,0},{3,1},{4,6},{5,7},{6,4},{7,5},{8,10},{9,11},{10,... | collective-permute-start | bytes 3145736 | tf_op jit(solution)/shard_map/ppermute | solution.py:719
  16.7 12.1 %collective-permute-start.3 = (bf16[272,512]{1,0:T(8,128)(2,1)S(1)}, bf16[272,512]{1,0:T(8,128)(2,1)S(1)}, u32[]{:S(2)}, u32[]{:S(2)}) collective-permute-start(bf16[272,512]{1,0:T(8,128)(2,1)S(1)} %get-tuple-element.62), channel_id=1, source_target_pairs={{0,4},{1,9},{2,6},{3,11},{4,0},{5,13},{6,2},{7,15},{8,12},{9,1},{1... | collective-permute-start | bytes 835592 | tf_op jit(solution)/shard_map/ppermute | solution.py:716
  18.0 10.6 %collective-permute-start.1 = (bf16[256,512]{1,0:T(8,128)(2,1)S(1)}, bf16[256,512]{1,0:T(8,128)(2,1)S(1)}, u32[]{:S(2)}, u32[]{:S(2)}) collective-permute-start(bf16[256,512]{1,0:T(8,128)(2,1)S(1)} %get-tuple-element.59), channel_id=1, source_target_pairs={{0,4},{1,9},{2,6},{3,11},{4,0},{5,13},{6,2},{7,15},{8,12},{9,1},{1... | collective-permute-start | bytes 786440 | tf_op jit(solution)/shard_map/ppermute | solution.py:716
  18.8 9.8 %collective-permute-start.2 = (bf16[256,512]{1,0:T(8,128)(2,1)S(1)}, bf16[256,512]{1,0:T(8,128)(2,1)S(1)}, u32[]{:S(2)}, u32[]{:S(2)}) collective-permute-start(bf16[256,512]{1,0:T(8,128)(2,1)S(1)} %get-tuple-element.60), channel_id=1, source_target_pairs={{0,8},{1,9},{2,10},{3,11},{4,12},{5,13},{6,14},{7,15},{8,0},{9,1},... | collective-permute-start | bytes 786440 | tf_op jit(solution)/shard_map/ppermute | solution.py:725
  28.8 3.7 %collective-permute-start.4 = (bf16[1024,512]{1,0:T(8,128)(2,1)S(1)}, bf16[1024,512]{1,0:T(8,128)(2,1)S(1)}, u32[]{:S(2)}, u32[]{:S(2)}) collective-permute-start(bf16[1024,512]{1,0:T(8,128)(2,1)S(1)} %collective-permute-done.refs_0_), channel_id=1, source_target_pairs={{0,1},{1,0},{2,3},{3,2},{4,5},{5,4},{6,7},{7,6},{8,9},{9,8},{10,11... | collective-permute-start | bytes 3145736 | tf_op jit(solution)/shard_map/ppermute | solution.py:719
  30.3 30.6 %collective-permute-start.12 = (bf16[1152,512]{1,0:T(8,128)(2,1)S(1)}, bf16[1152,512]{1,0:T(8,128)(2,1)S(1)}, u32[]{:S(2)}, u32[]{:S(2)}) collective-permute-start(bf16[1152,512]{1,0:T(8,128)(2,1)S(1)} %copy-done.17), channel_id=1, source_target_pairs={{0,2},{1,3},{2,0},{3,1},{4,6},{5,7},{6,4},{7,5},{8,10},{9,11},{10,... | collective-permute-start | bytes 3538952 | tf_op jit(solution)/shard_map/ppermute | solution.py:719
  30.8 6.5 %collective-permute-start.7 = (bf16[272,512]{1,0:T(8,128)(2,1)S(1)}, bf16[272,512]{1,0:T(8,128)(2,1)S(1)}, u32[]{:S(2)}, u32[]{:S(2)}) collective-permute-start(bf16[272,512]{1,0:T(8,128)(2,1)S(1)} %get-tuple-element.63), channel_id=1, source_target_pairs={{0,8},{1,5},{2,10},{3,7},{4,12},{5,1},{6,14},{7,3},{8,0},{9,13},{1... | collective-permute-start | bytes 835592 | tf_op jit(solution)/shard_map/ppermute | solution.py:716
  37.4 15.8 %collective-permute-start.8 = (bf16[272,512]{1,0:T(8,128)(2,1)S(1)}, bf16[272,512]{1,0:T(8,128)(2,1)S(1)}, u32[]{:S(2)}, u32[]{:S(2)}) collective-permute-start(bf16[272,512]{1,0:T(8,128)(2,1)S(1)} %get-tuple-element.72), channel_id=1, source_target_pairs={{0,16},{1,17},{2,18},{3,19},{4,20},{5,21},{6,22},{7,23},{8,24},{9,... | collective-permute-start | bytes 835592 | tf_op jit(solution)/shard_map/ppermute | solution.py:725
  40.1 12.0 %collective-permute-start.6 = (bf16[256,512]{1,0:T(8,128)(2,1)S(1)}, bf16[256,512]{1,0:T(8,128)(2,1)S(1)}, u32[]{:S(2)}, u32[]{:S(2)}) collective-permute-start(bf16[256,512]{1,0:T(8,128)(2,1)S(1)} %get-tuple-element.68), channel_id=1, source_target_pairs={{0,8},{1,9},{2,10},{3,11},{4,12},{5,13},{6,14},{7,15},{8,0},{9,1},... | collective-permute-start | bytes 786440 | tf_op jit(solution)/shard_map/ppermute | solution.py:725
  41.7 10.5 %collective-permute-start.5 = (bf16[256,512]{1,0:T(8,128)(2,1)S(1)}, bf16[256,512]{1,0:T(8,128)(2,1)S(1)}, u32[]{:S(2)}, u32[]{:S(2)}) collective-permute-start(bf16[256,512]{1,0:T(8,128)(2,1)S(1)} %get-tuple-element.67), channel_id=1, source_target_pairs={{0,4},{1,5},{2,6},{3,7},{4,0},{5,1},{6,2},{7,3},{8,12},{9,13},{10,... | collective-permute-start | bytes 786440 | tf_op jit(solution)/shard_map/ppermute | solution.py:725
  43.1 62.0 %collective-permute-start.22 = (bf16[1920,512]{1,0:T(8,128)(2,1)}, bf16[1920,512]{1,0:T(8,128)(2,1)S(1)}, u32[]{:S(2)}, u32[]{:S(2)}) collective-permute-start(bf16[1920,512]{1,0:T(8,128)(2,1)} %get-tuple-element.88), channel_id=1, source_target_pairs={{0,2},{1,3},{2,0},{3,1},{4,6},{5,7},{6,4},{7,5},{8,10},{9,11},{10,... | collective-permute-start | bytes 5898248 | tf_op jit(solution)/shard_map/ppermute | solution.py:719
  55.6 3.8 %collective-permute-start.10 = (f32[24,256]{1,0:T(8,128)S(1)}, f32[24,256]{1,0:T(8,128)S(1)}, u32[]{:S(2)}, u32[]{:S(2)}) collective-permute-start(f32[24,256]{1,0:T(8,128)S(1)} %add.22.s_ref), channel_id=1, source_target_pairs={{0,4},{1,5},{2,6},{3,7},{4,0},{5,1},{6,2},{7,3},{8,12},{9,13},{10,... | collective-permute-start | bytes 73736 | tf_op jit(solution)/shard_map/ppermute | solution.py:725
  59.4 4.8 %collective-permute-start.11 = (f32[24,256]{1,0:T(8,128)S(1)}, f32[24,256]{1,0:T(8,128)S(1)}, u32[]{:S(2)}, u32[]{:S(2)}) collective-permute-start(f32[24,256]{1,0:T(8,128)S(1)} %collective-permute-done.10), channel_id=1, source_target_pairs={{0,6},{1,7},{2,4},{3,5},{4,2},{5,3},{6,0},{7,1},{8,14},{9,15},{10,... | collective-permute-start | bytes 73736 | tf_op jit(solution)/shard_map/ppermute | solution.py:725
  66.4 1.4 collective-permute-start.13
  67.9 13.8 %collective-permute-start.17 = (bf16[256,512]{1,0:T(8,128)(2,1)S(1)}, bf16[256,512]{1,0:T(8,128)(2,1)S(1)}, u32[]{:S(2)}, u32[]{:S(2)}) collective-permute-start(bf16[256,512]{1,0:T(8,128)(2,1)S(1)} %hold.3), channel_id=1, source_target_pairs={{0,8},{1,5},{2,10},{3,7},{4,12},{5,1},{6,14},{7,3},{8,0},{9,13},{1... | collective-permute-start | bytes 786440 | tf_op jit(solution)/shard_map/ppermute | solution.py:716
  69.3 14.7 %collective-permute-start.18 = (bf16[256,512]{1,0:T(8,128)(2,1)S(1)}, bf16[256,512]{1,0:T(8,128)(2,1)S(1)}, u32[]{:S(2)}, u32[]{:S(2)}) collective-permute-start(bf16[256,512]{1,0:T(8,128)(2,1)S(1)} %get-tuple-element.81.refs_1_.refs_7_), channel_id=1, source_target_pairs={{0,16},{1,17},{2,18},{3,19},{4,20},{5,21},{6,22},{7,23},{8,24},{9,... | collective-permute-start | bytes 786440 | tf_op jit(solution)/shard_map/ppermute | solution.py:716
  71.9 12.1 %collective-permute-start.16 = (bf16[256,512]{1,0:T(8,128)(2,1)S(1)}, bf16[256,512]{1,0:T(8,128)(2,1)S(1)}, u32[]{:S(2)}, u32[]{:S(2)}) collective-permute-start(bf16[256,512]{1,0:T(8,128)(2,1)S(1)} %hold.3), channel_id=1, source_target_pairs={{0,4},{1,9},{2,6},{3,11},{4,0},{5,13},{6,2},{7,15},{8,12},{9,1},{1... | collective-permute-start | bytes 786440 | tf_op jit(solution)/shard_map/ppermute | solution.py:716
  73.4 7.7 %collective-permute-start.14 = (f32[8,4096]{1,0:T(8,128)S(1)}, f32[8,4096]{1,0:T(8,128)S(1)}, u32[]{:S(2)}, u32[]{:S(2)}) collective-permute-start(f32[8,4096]{1,0:T(8,128)S(1)} %add.23.refs_0_.d_ref), channel_id=1, source_target_pairs={{0,4},{1,5},{2,6},{3,7},{4,0},{5,1},{6,2},{7,3},{8,12},{9,13},{10,... | collective-permute-start | bytes 393224 | tf_op jit(solution)/shard_map/ppermute | solution.py:725
  81.1 6.3 %collective-permute-start.15 = (f32[8,4096]{1,0:T(8,128)S(1)}, f32[8,4096]{1,0:T(8,128)S(1)}, u32[]{:S(2)}, u32[]{:S(2)}) collective-permute-start(f32[8,4096]{1,0:T(8,128)S(1)} %collective-permute-done.14), channel_id=1, source_target_pairs={{0,6},{1,7},{2,4},{3,5},{4,2},{5,3},{6,0},{7,1},{8,14},{9,15},{10,... | collective-permute-start | bytes 393224 | tf_op jit(solution)/shard_map/ppermute | solution.py:725
  81.7 13.3 %collective-permute-start.23 = (bf16[256,512]{1,0:T(8,128)(2,1)S(1)}, bf16[256,512]{1,0:T(8,128)(2,1)S(1)}, u32[]{:S(2)}, u32[]{:S(2)}) collective-permute-start(bf16[256,512]{1,0:T(8,128)(2,1)S(1)} %collective-permute-done.17.refs_2_.refs_5_), channel_id=1, source_target_pairs={{0,4},{1,9},{2,6},{3,11},{4,0},{5,13},{6,2},{7,15},{8,12},{9,1},{1... | collective-permute-start | bytes 786440 | tf_op jit(solution)/shard_map/ppermute | solution.py:716
  87.5 7.5 %collective-permute-start.24 = (bf16[256,512]{1,0:T(8,128)(2,1)S(1)}, bf16[256,512]{1,0:T(8,128)(2,1)S(1)}, u32[]{:S(2)}, u32[]{:S(2)}) collective-permute-start(bf16[256,512]{1,0:T(8,128)(2,1)S(1)} %hold.4.refs_6_), channel_id=1, source_target_pairs={{0,4},{1,9},{2,6},{3,11},{4,0},{5,13},{6,2},{7,15},{8,12},{9,1},{1... | collective-permute-start | bytes 786440 | tf_op jit(solution)/shard_map/ppermute | solution.py:716
  88.8 6.4 %collective-permute-start.25 = (bf16[256,512]{1,0:T(8,128)(2,1)S(1)}, bf16[256,512]{1,0:T(8,128)(2,1)S(1)}, u32[]{:S(2)}, u32[]{:S(2)}) collective-permute-start(bf16[256,512]{1,0:T(8,128)(2,1)S(1)} %hold.4.refs_6_), channel_id=1, source_target_pairs={{0,8},{1,5},{2,10},{3,7},{4,12},{5,1},{6,14},{7,3},{8,0},{9,13},{1... | collective-permute-start | bytes 786440 | tf_op jit(solution)/shard_map/ppermute | solution.py:716
  91.2 3.8 %collective-permute-start.19 = (f32[8,512]{1,0:T(8,128)S(1)}, f32[8,512]{1,0:T(8,128)S(1)}, u32[]{:S(2)}, u32[]{:S(2)}) collective-permute-start(f32[8,512]{1,0:T(8,128)S(1)} %add.24), channel_id=1, source_target_pairs={{0,4},{1,9},{2,6},{3,11},{4,0},{5,13},{6,2},{7,15},{8,12},{9,1},{1... | collective-permute-start | bytes 49160 | tf_op jit(solution)/shard_map/ppermute | solution.py:716
  95.7 9.4 %collective-permute-start.26 = (bf16[1152,512]{1,0:T(8,128)(2,1)S(1)}, bf16[1152,512]{1,0:T(8,128)(2,1)}, u32[]{:S(2)}, u32[]{:S(2)}) collective-permute-start(bf16[1152,512]{1,0:T(8,128)(2,1)S(1)} %collective-permute-done.12.refs_1_), channel_id=1, source_target_pairs={{0,1},{1,0},{2,3},{3,2},{4,5},{5,4},{6,7},{7,6},{8,9},{9,8},{10,11... | collective-permute-start | bytes 3538952 | tf_op jit(solution)/shard_map/ppermute | solution.py:719
  95.7 9.4 %collective-permute-start.27 = (bf16[256,512]{1,0:T(8,128)(2,1)S(1)}, bf16[256,512]{1,0:T(8,128)(2,1)}, u32[]{:S(2)}, u32[]{:S(2)}) collective-permute-start(bf16[256,512]{1,0:T(8,128)(2,1)S(1)} %hold.5.refs_4_), channel_id=1, source_target_pairs={{0,4},{1,9},{2,6},{3,11},{4,0},{5,13},{6,2},{7,15},{8,12},{9,1},{1... | collective-permute-start | bytes 786440 | tf_op jit(solution)/shard_map/ppermute | solution.py:716
  96.5 3.9 %collective-permute-start.20 = (f32[8,512]{1,0:T(8,128)S(1)}, f32[8,512]{1,0:T(8,128)S(1)}, u32[]{:S(2)}, u32[]{:S(2)}) collective-permute-start(f32[8,512]{1,0:T(8,128)S(1)} %add.25.refs_2_), channel_id=1, source_target_pairs={{0,8},{1,5},{2,10},{3,7},{4,12},{5,1},{6,14},{7,3},{8,0},{9,13},{1... | collective-permute-start | bytes 49160 | tf_op jit(solution)/shard_map/ppermute | solution.py:716
  100.5 4.6 %collective-permute-start.21 = (f32[8,512]{1,0:T(8,128)S(1)}, f32[8,512]{1,0:T(8,128)S(1)}, u32[]{:S(2)}, u32[]{:S(2)}) collective-permute-start(f32[8,512]{1,0:T(8,128)S(1)} %add.26), channel_id=1, source_target_pairs={{0,16},{1,17},{2,18},{3,19},{4,20},{5,21},{6,22},{7,23},{8,24},{9,... | collective-permute-start | bytes 49160 | tf_op jit(solution)/shard_map/ppermute | solution.py:716
  107.5 17.3 %collective-permute-start.32 = (bf16[4096,512]{1,0:T(8,128)(2,1)}, bf16[4096,512]{1,0:T(8,128)(2,1)S(1)}, u32[]{:S(2)}, u32[]{:S(2)}) collective-permute-start(bf16[4096,512]{1,0:T(8,128)(2,1)} %get-tuple-element.102.u_ref.refs_7_), channel_id=1, source_target_pairs={{0,1},{1,0},{2,3},{3,2},{4,5},{5,4},{6,7},{7,6},{8,9},{9,8},{10,11... | collective-permute-start | bytes 12582920 | tf_op jit(solution)/shard_map/ppermute | solution.py:719
  107.5 27.0 %collective-permute-start.28 = (bf16[1920,512]{1,0:T(8,128)(2,1)S(1)}, bf16[1920,512]{1,0:T(8,128)(2,1)S(1)}, u32[]{:S(2)}, u32[]{:S(2)}) collective-permute-start(bf16[1920,512]{1,0:T(8,128)(2,1)S(1)} %collective-permute-done.22.refs_2_), channel_id=1, source_target_pairs={{0,1},{1,0},{2,3},{3,2},{4,5},{5,4},{6,7},{7,6},{8,9},{9,8},{10,11... | collective-permute-start | bytes 5898248 | tf_op jit(solution)/shard_map/ppermute | solution.py:719
  108.0 16.7 %collective-permute-start.30 = (bf16[512,512]{1,0:T(8,128)(2,1)S(1)}, bf16[512,512]{1,0:T(8,128)(2,1)S(1)}, u32[]{:S(2)}, u32[]{:S(2)}) collective-permute-start(bf16[512,512]{1,0:T(8,128)(2,1)S(1)} %get-tuple-element.97), channel_id=1, source_target_pairs={{0,1},{1,0},{2,3},{3,2},{4,5},{5,4},{6,7},{7,6},{8,9},{9,8},{10,11... | collective-permute-start | bytes 1572872 | tf_op jit(solution)/shard_map/ppermute | solution.py:719
  108.1 16.6 %collective-permute-start.31 = (bf16[512,512]{1,0:T(8,128)(2,1)S(1)}, bf16[512,512]{1,0:T(8,128)(2,1)S(1)}, u32[]{:S(2)}, u32[]{:S(2)}) collective-permute-start(bf16[512,512]{1,0:T(8,128)(2,1)S(1)} %get-tuple-element.98), channel_id=1, source_target_pairs={{0,2},{1,3},{2,0},{3,1},{4,6},{5,7},{6,4},{7,5},{8,10},{9,11},{10,... | collective-permute-start | bytes 1572872 | tf_op jit(solution)/shard_map/ppermute | solution.py:719
  109.4 25.1 %collective-permute-start.29 = (bf16[512,512]{1,0:T(8,128)(2,1)S(1)}, bf16[512,512]{1,0:T(8,128)(2,1)S(1)}, u32[]{:S(2)}, u32[]{:S(2)}) collective-permute-start(bf16[512,512]{1,0:T(8,128)(2,1)S(1)} %get-tuple-element.99), channel_id=1, source_target_pairs={{0,3},{1,2},{2,1},{3,0},{4,7},{5,6},{6,5},{7,4},{8,11},{9,10},{10,... | collective-permute-start | bytes 1572872 | tf_op jit(solution)/shard_map/ppermute | solution.py:719
  (19 other events, 236.3 us)
